TPU v7x, 128 devices: a whole 4x4x4 slice. The times are simulated.
128 devices in a mesh: grp: 4 (over z), gz: 32 (over x, y, core).
Axes of the slice: x: 4, y: 4, z: 4, core: 2. Of those that a mesh axis runs over, the one named last changes fastest.
Arguments:
- load: float32 [3, 1024, 64, 128], P(None, ('grp', 'gz')), may hold values from -128 to 128
- phases: int32 [1024, 64, 128], P(('grp', 'gz')), may hold values from 0 to 3
- clamp: int32 [64, 128], replicated, may hold values 0 or 1
- phase_moduli: float32 [4], replicated, may hold values from 0.05 to 1
Outputs:
- displacement: float32 [3, 1024, 64, 128], P(None, ('grp', 'gz'))
- residual: float32 [3, 1024, 64, 128], P(None, ('grp', 'gz'))
All inputs are finite; a program needn't handle non-finite values.
Results may differ from a plain program's by a relative error of at most 0.0003.
Values sent between devices are 32-bit elements; how exact they have to be, the bound alone decides.
No kernel may reach another device: no remote copies, remote signals or barrier semaphores. Data moves between devices by JAX's collectives and lax.ppermute only.
A program may use at most 128 MiB of HBM per device.

v0:
```python
import math

import jax
import jax.numpy as jnp
import numpy as np
from jax import lax
from jax.sharding import PartitionSpec as P

PHASES = 4
COARSEN = 8
CHEB = 4
ITERS = 2


CORNER_OFFSETS = [
    (along_z, along_y, along_x) for along_z in (0, 1) for along_y in (0, 1) for along_x in (0, 1)
]


def passed_along(value, axis, by):
    size = lax.axis_size(axis)
    pairs = [(i, i + by) for i in range(size) if 0 <= i + by < size]
    return lax.ppermute(value, axis, pairs)


def spread(block, axis, holder):
    block = jnp.where(lax.axis_index(axis) == holder, block, jnp.zeros_like(block))
    return lax.psum(block, axis)


def element_matrix():
    poisson = 0.3
    lame_first = poisson / ((1.0 + poisson) * (1.0 - 2.0 * poisson))
    shear = 1.0 / (2.0 * (1.0 + poisson))
    elastic = np.zeros((6, 6))
    elastic[:3, :3] = lame_first
    for axis_one in range(3):
        elastic[axis_one, axis_one] = lame_first + 2.0 * shear
        elastic[axis_one + 3, axis_one + 3] = shear
    points = [0.5 - 0.5 / math.sqrt(3.0), 0.5 + 0.5 / math.sqrt(3.0)]
    pairs = [(0, 1), (1, 2), (0, 2)]
    matrix = np.zeros((24, 24))
    for first_point in points:
        for second_point in points:
            for third_point in points:
                spot = (first_point, second_point, third_point)
                strain = np.zeros((6, 24))
                for corner, offset in enumerate(CORNER_OFFSETS):
                    values = [
                        spot[axis_one] if offset[axis_one] else 1.0 - spot[axis_one]
                        for axis_one in range(3)
                    ]
                    slopes = [1.0 if offset[axis_one] else -1.0 for axis_one in range(3)]
                    slants = []
                    for axis_one in range(3):
                        others = [values[axis_two] for axis_two in range(3) if axis_two != axis_one]
                        slants.append(slopes[axis_one] * others[0] * others[1])
                        strain[axis_one, 3 * corner + axis_one] = slants[axis_one]
                    for position, pair in enumerate(pairs):
                        strain[3 + position, 3 * corner + pair[0]] = slants[pair[1]]
                        strain[3 + position, 3 * corner + pair[1]] = slants[pair[0]]
                matrix = matrix + 0.125 * (strain.T @ elastic @ strain)
    return matrix


def spectral_bound(numbers):
    diagonal_part = np.array([numbers[index, index] for index in range(numbers.shape[0])])
    return float(np.max(np.sum(np.abs(numbers), axis=1) / diagonal_part))


def element_forces(extended, moduli, matrix):
    layers = moduli.shape[0]
    width = min(4, layers)
    blocks = (layers + width - 1) // width
    plane = tuple(extended.shape[2:])

    def add_block(total, index):
        start = index * width
        nodes = lax.dynamic_slice_in_dim(extended, start, width + 1, 1)
        weights = lax.dynamic_slice_in_dim(moduli, start, width, 0)
        gathered = jnp.stack(
            [
                jnp.roll(nodes[:, along_z : along_z + width], (-along_y, -along_x), (2, 3))
                for along_z, along_y, along_x in CORNER_OFFSETS
            ],
            0,
        )
        gathered = gathered.reshape((24, width) + plane)
        forces = (
            jnp.einsum("ij,jzyx->izyx", matrix, gathered, precision=lax.Precision.HIGHEST) * weights
        )
        forces = forces.reshape((8, 3, width) + plane)
        update = jnp.zeros((3, width + 1) + plane, jnp.float32)
        for corner, offset in enumerate(CORNER_OFFSETS):
            update = update.at[:, offset[0] : offset[0] + width].add(
                jnp.roll(forces[corner], (offset[1], offset[2]), (2, 3))
            )
        current = lax.dynamic_slice_in_dim(total, start, width + 1, 1)
        return (lax.dynamic_update_slice_in_dim(total, current + update, start, 1), None)

    initial = jnp.zeros(extended.shape, jnp.float32)
    total, unused = lax.scan(add_block, initial, jnp.arange(blocks, dtype=jnp.int32))
    return total[:, : layers + 1]


def node_diagonal(lower, moduli, matrix):
    layers = moduli.shape[0]
    extended = jnp.concatenate([lower, moduli], 0)
    entries = jnp.diagonal(matrix).reshape(8, 3)
    total = jnp.zeros((3,) + tuple(moduli.shape), jnp.float32)
    for corner, offset in enumerate(CORNER_OFFSETS):
        shifted = jnp.roll(
            extended[1 - offset[0] : 1 - offset[0] + layers], (offset[1], offset[2]), (1, 2)
        )
        total = total + entries[corner][:, None, None, None] * shifted[None]
    return total


def chebyshev(rhs, coarse_apply, coarse_inverse, bound, sweeps):
    bottom = bound / 20.0
    center = 0.5 * (bound + bottom)
    radius = 0.5 * (bound - bottom)
    sigma = center / radius
    rho = 1.0 / sigma
    update = coarse_inverse * rhs / center
    correction = update
    remainder = rhs
    for sweep in range(sweeps - 1):
        remainder = remainder - coarse_apply(update)
        rho_next = 1.0 / (2.0 * sigma - rho)
        update = rho_next * rho * update + 2.0 * rho_next / radius * coarse_inverse * remainder
        correction = correction + update
        rho = rho_next
    return correction


def restrict(field, factor):
    comps, layers, height, breadth = field.shape
    return field.reshape(
        comps, layers // factor, factor, height // factor, factor, breadth // factor, factor
    ).sum((2, 4, 6))


def prolong(coarse, factor):
    comps, layers, height, breadth = coarse.shape
    expanded = jnp.broadcast_to(
        coarse[:, :, None, :, None, :, None],
        (comps, layers, factor, height, factor, breadth, factor),
    )
    return expanded.reshape(comps, layers * factor, height * factor, breadth * factor)


def residual_sum(residual, preconditioned):
    return lax.psum(jnp.sum(residual * preconditioned), ("grp", "gz"))


def body(load, phases, clamp, phase_moduli):
    numbers = element_matrix()
    matrix = jnp.asarray(numbers, jnp.float32)
    bound = spectral_bound(numbers)
    omega = 1.2 / bound
    layers, height, breadth = phases.shape
    factor = COARSEN
    tile = lax.axis_index(("grp", "gz"))
    tiles = lax.axis_size(("grp", "gz"))
    member = lax.axis_index("gz")
    members = lax.axis_size("gz")
    depth = tile * layers + jnp.arange(layers, dtype=jnp.int32)[:, None, None]
    rows_at = jnp.arange(height, dtype=jnp.int32)[None, :, None]
    columns_at = jnp.arange(breadth, dtype=jnp.int32)[None, None, :]
    picked = jnp.zeros((layers, height, breadth), jnp.float32)
    for phase in range(PHASES):
        picked = picked + jnp.where(phases == phase, phase_moduli[phase], jnp.float32(0.0))
    outside = (depth == tiles * layers - 1) | (rows_at == height - 1) | (columns_at == breadth - 1)
    moduli = jnp.where(outside, jnp.float32(0.0), picked)
    free = jnp.where((depth == 0) & (clamp[None] == 1), 0.0, 1.0).astype(jnp.float32)
    lower = passed_along(moduli[-1:], ("grp", "gz"), 1)
    inverse = 1.0 / (free * node_diagonal(lower, moduli, matrix) + 1.0 - free)

    def stiffness(field):
        above = passed_along(field[:, :1], ("grp", "gz"), -1)
        total = element_forces(jnp.concatenate([field, above], 1), moduli, matrix)
        below = passed_along(total[:, -1:], ("grp", "gz"), 1)
        return total[:, :-1].at[:, :1].add(below)

    def operator(field):
        return free * stiffness(free * field) + (1.0 - free) * field

    coarse_layers = layers // factor
    coarse_height = height // factor
    coarse_breadth = breadth // factor
    group_layers = members * coarse_layers
    block_mean = moduli.reshape(
        coarse_layers, factor, coarse_height, factor, coarse_breadth, factor
    ).mean((1, 3, 5))
    coarse_depth = (
        member * coarse_layers + jnp.arange(coarse_layers, dtype=jnp.int32)[:, None, None]
    )
    coarse_rows = jnp.arange(coarse_height, dtype=jnp.int32)[None, :, None]
    coarse_columns = jnp.arange(coarse_breadth, dtype=jnp.int32)[None, None, :]
    coarse_edge = (
        (coarse_depth == group_layers - 1)
        | (coarse_rows == coarse_height - 1)
        | (coarse_columns == coarse_breadth - 1)
    )
    coarse_local = jnp.where(coarse_edge, jnp.float32(0.0), block_mean)
    group_moduli = lax.all_gather(coarse_local, "gz", axis=0, tiled=True)
    coarse_matrix = factor * matrix
    coarse_bottom = jnp.zeros((1, coarse_height, coarse_breadth), jnp.float32)
    coarse_top = jnp.zeros((3, 1, coarse_height, coarse_breadth), jnp.float32)
    coarse_inverse = 1.0 / node_diagonal(coarse_bottom, group_moduli, coarse_matrix)

    def coarse_apply(field):
        return element_forces(jnp.concatenate([field, coarse_top], 1), group_moduli, coarse_matrix)[
            :, :-1
        ]

    def solve_group(summed):
        return chebyshev(summed, coarse_apply, coarse_inverse, bound, CHEB)

    def blank_group(summed):
        return jnp.zeros_like(summed)

    def precondition(current):
        first = omega * current * inverse
        defect = current - operator(first)
        restricted = restrict(defect, factor)
        summed = lax.all_gather(restricted, "gz", axis=1, tiled=True)
        solved = lax.cond(member == 0, solve_group, blank_group, summed)
        solved = spread(solved, "gz", 0)
        own = lax.dynamic_slice_in_dim(solved, member * coarse_layers, coarse_layers, 1)
        second = first + free * prolong(own, factor)
        return second + omega * (current - operator(second)) * inverse

    rhs = free * load
    displacement = jnp.zeros_like(rhs)
    residual = rhs
    preconditioned = precondition(residual)
    direction = preconditioned
    gamma = residual_sum(residual, preconditioned)
    for step in range(ITERS):
        image = operator(direction)
        alpha = gamma / lax.psum(jnp.sum(direction * image), ("grp", "gz"))
        displacement = displacement + alpha * direction
        residual = residual - alpha * image
        if step + 1 < ITERS:
            preconditioned = precondition(residual)
            following = residual_sum(residual, preconditioned)
            direction = preconditioned + following / gamma * direction
            gamma = following
    return (displacement, residual)


def solution(mesh):
    placed = (P(None, ("grp", "gz"), None, None), P(("grp", "gz"), None, None), P(), P())
    return jax.shard_map(
        body,
        mesh=mesh,
        in_specs=placed,
        out_specs=(P(None, ("grp", "gz"), None, None), P(None, ("grp", "gz"), None, None)),
        check_vma=False,
    )
```

profile of v0, /device:TPU:1, one launch (start us, length us, event | category | flops | bytes accessed | tf_op | source)
XLA Modules:
  0.0 2149.7 jit_solution(12329310043015683332)
XLA Ops:
  11.0 26.4 %all_gather.9 = f32[32,8,16]{2,1,0:T(8,128)} all-gather(f32[1,8,16]{2,1,0:T(8,128)S(1)} %bitcast_select_fusion), channel_id=1, replica_groups=mesh['grp'=4,'gz'=32] {'gz'}, dimensions={0}, use_global_device_ids=true | all-gather | bytes 16896 | tf_op jit(solution)/shard_map/all_gather | solution.py:207
  61.6 45.4 %while.252 = (s32[]{:T(128)}, f32[3,9,64,128]{3,2,1,0:T(8,128)}, s32[2]{0:T(128)S(1)}, f32[3,9,64,128]{3,2,1,0:T(8,128)S(1)}, f32[8,64,128]{2,1,0:T(8,128)S(1)},...) while((s32[]{:T(128)}, f32[3,9,64,128]{3,2,1,0:T(8,128)}, ...), condition=%wide.region_3.4_spmd.clone, body=%wide.region_2.3_spmd.sunk.clone.sunk | while | flops 230057488 | bytes 44966448 | solution.py:102
  70.6 6.3 multiply_bitcast_fusion.12
  93.2 6.3 multiply_bitcast_fusion.12
  117.5 26.3 %all-gather = f32[3,256,16]{2,1,0:T(8,128)S(1)} all-gather(f32[3,8,16]{2,1,0:T(8,128)S(1)} %reduce_sum.93), channel_id=2, replica_groups=mesh['grp'=4,'gz'=32] {'gz'}, dimensions={1}, use_global_device_ids=true | all-gather | bytes 50688 | tf_op jit(solution)/shard_map/all_gather | solution.py:228
  143.8 10.6 conditional.2
  154.5 708.8 %psum.42 = f32[3,32,8,16]{3,2,0,1:T(8,128)S(1)} all-reduce(f32[3,32,8,16]{3,2,0,1:T(8,128)S(1)} %broadcast_select_fusion.1), channel_id=1, replica_groups=mesh['grp'=4,'gz'=32] {'gz'}, use_global_device_ids=true, to_apply=%region_14.15 | all-reduce | flops 12288 | bytes 98304 | tf_op jit(solution)/shard_map/psum | solution.py:28
  867.0 7.6 collective-permute-start.3
  876.7 43.9 %while.253 = (s32[]{:T(128)}, f32[3,9,64,128]{3,2,1,0:T(8,128)}, s32[2]{0:T(128)S(1)}, f32[3,9,64,128]{3,2,1,0:T(8,128)S(1)}, f32[8,64,128]{2,1,0:T(8,128)S(1)},...) while((s32[]{:T(128)}, f32[3,9,64,128]{3,2,1,0:T(8,128)}, ...), condition=%wide.region_16.17_spmd.clone, body=%wide.region_15.16_spmd.sunk.clone.sunk | while | flops 230057488 | bytes 52208232 | solution.py:102
  885.7 6.3 multiply_bitcast_fusion.13
  936.0 44.1 %while.254 = (s32[]{:T(128)}, f32[3,9,64,128]{3,2,1,0:T(8,128)}, s32[2]{0:T(128)S(1)}, f32[3,9,64,128]{3,2,1,0:T(8,128)S(1)}, f32[8,64,128]{2,1,0:T(8,128)S(1)},...) while((s32[]{:T(128)}, f32[3,9,64,128]{3,2,1,0:T(8,128)}, ...), condition=%wide.region_20.21_spmd.clone, body=%wide.region_19.20_spmd.sunk.clone.sunk | while | flops 230057488 | bytes 52208232 | solution.py:102
  945.1 6.3 multiply_bitcast_fusion.14
  988.6 75.1 %all-reduce.19 = (f32[]{:T(128)}, f32[]{:T(128)}) all-reduce(f32[]{:T(128)} %get-tuple-element.2519, f32[]{:T(128)} %get-tuple-element.2518), channel_id=1, replica_groups=mesh['grp'=4,'gz'=32] {'grp','gz'}, use_global_device_ids=true, to_apply=%region_18.19 | all-reduce | flops 2 | bytes 16 | tf_op jit(solution)/shard_map/psum | solution.py:154
  1076.8 43.7 %while.255 = (s32[]{:T(128)}, f32[3,9,64,128]{3,2,1,0:T(8,128)}, s32[2]{0:T(128)S(1)}, f32[3,9,64,128]{3,2,1,0:T(8,128)S(1)}, f32[8,64,128]{2,1,0:T(8,128)S(1)},...) while((s32[]{:T(128)}, f32[3,9,64,128]{3,2,1,0:T(8,128)}, ...), condition=%wide.region_24.25_spmd.clone, body=%wide.region_23.24_spmd.sunk.clone.sunk | while | flops 230057488 | bytes 52208232 | solution.py:102
  1085.7 6.4 multiply_bitcast_fusion.15
  1107.6 6.3 multiply_bitcast_fusion.15
  1128.3 28.2 %all-gather.1 = f32[3,256,16]{2,1,0:T(8,128)S(1)} all-gather(f32[3,8,16]{2,1,0:T(8,128)S(1)} %reduce_sum.99), channel_id=3, replica_groups=mesh['grp'=4,'gz'=32] {'gz'}, dimensions={1}, use_global_device_ids=true | all-gather | bytes 50688 | tf_op jit(solution)/shard_map/all_gather | solution.py:228
  1157.6 718.2 %psum.45 = f32[3,32,8,16]{3,2,0,1:T(8,128)S(1)} all-reduce(f32[3,32,8,16]{3,2,0,1:T(8,128)S(1)} %broadcast_select_fusion), channel_id=1, replica_groups=mesh['grp'=4,'gz'=32] {'gz'}, use_global_device_ids=true, to_apply=%region_35.36 | all-reduce | flops 12288 | bytes 98304 | tf_op jit(solution)/shard_map/psum | solution.py:28
  1879.5 7.6 collective-permute-start.9
  1889.1 44.1 %while.256 = (s32[]{:T(128)}, f32[3,9,64,128]{3,2,1,0:T(8,128)}, s32[2]{0:T(128)S(1)}, f32[3,9,64,128]{3,2,1,0:T(8,128)S(1)}, f32[8,64,128]{2,1,0:T(8,128)S(1)},...) while((s32[]{:T(128)}, f32[3,9,64,128]{3,2,1,0:T(8,128)}, ...), condition=%wide.region_37.38_spmd.clone, body=%wide.region_36.37_spmd.sunk.clone.sunk | while | flops 230057488 | bytes 52208232 | solution.py:102
  1898.3 6.3 multiply_bitcast_fusion.16
  1941.7 70.3 %psum.46 = f32[]{:T(128)} all-reduce(f32[]{:T(128)} %multiply_reduce_fusion.1), channel_id=1, replica_groups=mesh['grp'=4,'gz'=32] {'grp','gz'}, use_global_device_ids=true, to_apply=%region_39.40 | all-reduce | flops 1 | bytes 8 | tf_op jit(solution)/shard_map/psum | solution.py:154
  2024.9 43.8 %while.257 = (s32[]{:T(128)}, f32[3,9,64,128]{3,2,1,0:T(8,128)}, s32[2]{0:T(128)S(1)}, f32[3,9,64,128]{3,2,1,0:T(8,128)S(1)}, f32[8,64,128]{2,1,0:T(8,128)S(1)},...) while((s32[]{:T(128)}, f32[3,9,64,128]{3,2,1,0:T(8,128)}, ...), condition=%wide.region_41.42_spmd.clone, body=%wide.region_40.41_spmd.sunk.clone.sunk | while | flops 230057488 | bytes 52208232 | solution.py:102
  2076.3 69.2 %psum.47 = f32[]{:T(128)} all-reduce(f32[]{:T(128)} %multiply_reduce_fusion), channel_id=1, replica_groups=mesh['grp'=4,'gz'=32] {'grp','gz'}, use_global_device_ids=true, to_apply=%region_43.44 | all-reduce | flops 1 | bytes 8 | tf_op jit(solution)/shard_map/psum | solution.py:243
  (687 shorter events, 342.8 us)
Async XLA Ops:
  5.9 46.5 %collective-permute-start = (f32[1,64,128]{2,1,0:T(8,128)S(1)}, f32[1,64,128]{2,1,0:T(8,128)S(1)}, u32[]{:S(2)}, u32[]{:S(2)}) collective-permute-start(f32[1,64,128]{2,1,0:T(8,128)S(1)} %slice.6742), channel_id=1, source_target_pairs={{0,1},{1,2},{2,3},{3,4},{4,5},{5,6},{6,7},{7,8},{8,9},{9,10},{10,1... | collective-permute-start | bytes 98312 | tf_op jit(solution)/shard_map/ppermute | solution.py:23
  46.0 67.6 %copy-start.8 = (f32[8,64,128]{2,1,0:T(8,128)}, f32[8,64,128]{2,1,0:T(8,128)S(1)}, u32[]{:S(2)}) copy-start(f32[8,64,128]{2,1,0:T(8,128)S(1)} %get-tuple-element.3018) | copy-start | bytes 786436
  54.5 5.9 collective-permute-start.1
  108.0 4.7 collective-permute-start.2
  154.5 712.3 %copy-start.4 = (f32[3,8,64,128]{3,2,1,0:T(8,128)S(1)}, f32[3,8,64,128]{3,2,1,0:T(8,128)}, u32[]{:S(2)}) copy-start(f32[3,8,64,128]{3,2,1,0:T(8,128)} %param.237) | copy-start | bytes 2359300
  867.0 8.5 collective-permute-start.3
  876.7 49.2 %copy-start.9 = (f32[8,64,128]{2,1,0:T(8,128)S(1)}, f32[8,64,128]{2,1,0:T(8,128)}, u32[]{:S(2)}) copy-start(f32[8,64,128]{2,1,0:T(8,128)} %copy-done.8) | copy-start | bytes 786436
  921.4 3.5 collective-permute-start.4
  928.3 6.6 collective-permute-start.5
  980.0 85.1 %copy-start.5 = (f32[3,8,64,128]{3,2,1,0:T(8,128)S(1)}, f32[3,8,64,128]{3,2,1,0:T(8,128)}, u32[]{:S(2)}) copy-start(f32[3,8,64,128]{3,2,1,0:T(8,128)} %param.237) | copy-start | bytes 2359300
  980.0 85.1 %copy-start.29 = (f32[3,8,64,128]{3,2,1,0:T(8,128)S(1)}, f32[3,8,64,128]{3,2,1,0:T(8,128)}, u32[]{:S(2)}) copy-start(f32[3,8,64,128]{3,2,1,0:T(8,128)} %get-tuple-element.2707) | copy-start | bytes 2359300
  981.1 3.5 collective-permute-start.6
  1068.5 6.1 collective-permute-start.7
  1121.4 3.5 collective-permute-start.8
  1157.5 721.7 %copy-start.6 = (f32[3,8,64,128]{3,2,1,0:T(8,128)S(1)}, f32[3,8,64,128]{3,2,1,0:T(8,128)}, u32[]{:S(2)}) copy-start(f32[3,8,64,128]{3,2,1,0:T(8,128)} %get-tuple-element.2705) | copy-start | bytes 2359300
  1879.5 8.5 collective-permute-start.9
  1889.1 50.5 %copy-start.10 = (f32[8,64,128]{2,1,0:T(8,128)S(1)}, f32[8,64,128]{2,1,0:T(8,128)}, u32[]{:S(2)}) copy-start(f32[8,64,128]{2,1,0:T(8,128)} %copy-done.8) | copy-start | bytes 786436
  1933.2 80.1 %copy-start.7 = (f32[3,8,64,128]{3,2,1,0:T(8,128)S(1)}, f32[3,8,64,128]{3,2,1,0:T(8,128)}, u32[]{:S(2)}) copy-start(f32[3,8,64,128]{3,2,1,0:T(8,128)} %get-tuple-element.2705) | copy-start | bytes 2359300
  1933.2 80.1 %copy-start.30 = (f32[3,8,64,128]{3,2,1,0:T(8,128)S(1)}, f32[3,8,64,128]{3,2,1,0:T(8,128)}, u32[]{:S(2)}) copy-start(f32[3,8,64,128]{3,2,1,0:T(8,128)} %get-tuple-element.2707) | copy-start | bytes 2359300
  1934.3 3.5 collective-permute-start.10
  2016.7 5.9 collective-permute-start.11
  2068.7 78.1 %copy-start.11 = (f32[8,64,128]{2,1,0:T(8,128)S(1)}, f32[8,64,128]{2,1,0:T(8,128)}, u32[]{:S(2)}) copy-start(f32[8,64,128]{2,1,0:T(8,128)} %copy-done.8) | copy-start | bytes 786436
  2068.7 78.1 %copy-start.31 = (f32[3,8,64,128]{3,2,1,0:T(8,128)S(1)}, f32[3,8,64,128]{3,2,1,0:T(8,128)}, u32[]{:S(2)}) copy-start(f32[3,8,64,128]{3,2,1,0:T(8,128)} %get-tuple-element.2707) | copy-start | bytes 2359300
  2069.7 3.5 collective-permute-start.12
  (46 other events, 513.9 us)
where the time goes:
time: 2190 us; the launch traced here: 2150 us
  blocking collectives  1720 us (79%)
  other arithmetic  150 us (7%)
  local copies, waits for them, and re-layouts  116 us (5%)
  matrix products  76.1 us (3%)
  starting transfers between devices  41.9 us (2%)
    psum x2, blocking collectives, spread(): return lax.psum(block, axis)  1430 us
    psum x2, blocking collectives, residual_sum(): return lax.psum(jnp.sum(residual * preconditioned), ('grp', 'gz'))  145 us
    dot_general x12, matrix products, add_block(): jnp.einsum('ij,jzyx->izyx', matrix, gathered, precision=lax.Precision.HIG...  76.1 us
    psum x1, blocking collectives, body(): alpha = gamma / lax.psum(jnp.sum(direction * image), ('grp', 'gz'))  69.2 us
    all_gather x2, blocking collectives, precondition(): summed = lax.all_gather(restricted, 'gz', axis=1, tiled=True)  54.5 us
    while x60, other arithmetic  52.5 us
  transfers between devices with their start and end apart: 13, of which 10 were waited for; matrix products, arithmetic and copies ran while one was open for 1% of the time, Pallas kernels for 0%

commit v1 on v0

v1 whole, which is shorter than its diff:
```python
import functools
import math

import jax
import jax.numpy as jnp
import numpy as np
from jax import lax
from jax.experimental import pallas as pl
from jax.experimental.pallas import tpu as pltpu
from jax.sharding import PartitionSpec as P

COARSEN = 8
CHEB = 4
BOTH = ("grp", "gz")
GROUP = 32
H = 5
EXT = 17
WINDOW = 16
CORNER_OFFSETS = [(a, b, c) for a in (0, 1) for b in (0, 1) for c in (0, 1)]


def element_matrix():
    poisson = 0.3
    lame_first = poisson / ((1.0 + poisson) * (1.0 - 2.0 * poisson))
    shear = 1.0 / (2.0 * (1.0 + poisson))
    elastic = np.zeros((6, 6))
    elastic[:3, :3] = lame_first
    for axis_one in range(3):
        elastic[axis_one, axis_one] = lame_first + 2.0 * shear
        elastic[axis_one + 3, axis_one + 3] = shear
    points = [0.5 - 0.5 / math.sqrt(3.0), 0.5 + 0.5 / math.sqrt(3.0)]
    pairs = [(0, 1), (1, 2), (0, 2)]
    matrix = np.zeros((24, 24))
    for first_point in points:
        for second_point in points:
            for third_point in points:
                spot = (first_point, second_point, third_point)
                strain = np.zeros((6, 24))
                for corner, offset in enumerate(CORNER_OFFSETS):
                    values = [spot[i] if offset[i] else 1.0 - spot[i] for i in range(3)]
                    slopes = [1.0 if offset[i] else -1.0 for i in range(3)]
                    slants = []
                    for axis_one in range(3):
                        others = [values[i] for i in range(3) if i != axis_one]
                        slants.append(slopes[axis_one] * others[0] * others[1])
                        strain[axis_one, 3 * corner + axis_one] = slants[axis_one]
                    for position, pair in enumerate(pairs):
                        strain[3 + position, 3 * corner + pair[0]] = slants[pair[1]]
                        strain[3 + position, 3 * corner + pair[1]] = slants[pair[0]]
                matrix = matrix + 0.125 * (strain.T @ elastic @ strain)
    return matrix


NUMBERS = element_matrix()
BOUND = float(np.max(np.sum(np.abs(NUMBERS), axis=1) / np.diag(NUMBERS)))
OMEGA = 1.2 / BOUND
DIAGONAL = float(np.mean(np.diag(NUMBERS)))


def mode_matrix():
    haar = np.array([[1.0, 1.0], [-1.0, 1.0]])
    change = np.kron(np.kron(np.kron(haar, haar), haar), np.eye(3))
    return change @ NUMBERS @ change.T / 64.0


def mode_groups():
    modes = mode_matrix()
    near = np.abs(modes) > 1e-9
    left = [i for i in range(24) if near[i].any()]
    groups = []
    while left:
        group = [left[0]]
        for i in group:
            group += [j for j in left if near[i, j] and j not in group]
        groups.append(sorted(group))
        left = [i for i in left if i not in group]
    return modes, groups


MODES, MODE_GROUPS = mode_groups()


def mode_forces(value, scale):
    force = [None] * 24
    for group in MODE_GROUPS:
        diagonal = [float(MODES[i, i]) * scale for i in group]
        if len(group) == 1:
            force[group[0]] = diagonal[0] * value[group[0]]
            continue
        across = float(MODES[group[0], group[1]]) * scale
        apart = diagonal[0] - across
        total = value[group[0]]
        for i in group[1:]:
            total = total + value[i]
        total = across * total
        for i in group:
            if abs(apart) < 1e-9:
                force[i] = total
            else:
                force[i] = apart * value[i] + total
    return force


def lanes(value, by):
    return pltpu.roll(value, by % value.shape[1], 1)


def rows(value, by):
    return pltpu.roll(value, by % value.shape[0], 0)


def at(j):
    return slice(8 * j, 8 * j + 8)


def stiff(low, high, field, finish, moduli_ref, along_ref, up_ref, free):
    row = lax.broadcasted_iota(jnp.int32, (8, 128), 0)
    first_row = row == 0
    last_row = row == 7

    def x_modes(n, j):
        held = free(n, j)
        result = []
        for value in field(n, j):
            value = value * held
            beside = lanes(value, -1)
            result += [value + beside, beside - value]
        return result

    def xy_modes(n, j, here):
        if j < 7:
            values = x_modes(n, j + 1)
            after = (values, [rows(v, -1) for v in values])
        else:
            zero = jnp.zeros((8, 128), jnp.float32)
            after = ([zero] * 6, [zero] * 6)
        result = []
        for value, rolled, rolled_after in zip(here[0], here[1], after[1]):
            beside = jnp.where(last_row, rolled_after, rolled)
            result += [value + beside, beside - value]
        return result, after

    def start(n):
        values = x_modes(n, 0)
        return values, [rows(v, -1) for v in values]

    def layer(n, begin):
        here = start(n)
        carried = [jnp.zeros((8, 128), jnp.float32)] * 6
        for j in range(8):
            now, here = xy_modes(n, j, here)
            before = [along_ref[q, at(j), :] for q in range(12)]
            for q in range(12):
                along_ref[q, at(j), :] = now[q]
            weight = moduli_ref[n - 1, at(j), :]
            value = [None] * 24
            for k in range(3):
                for c in range(2):
                    for b in range(2):
                        q = 4 * k + 2 * c + b
                        value[3 * (2 * b + c) + k] = before[q] + now[q]
                        value[3 * (4 + 2 * b + c) + k] = now[q] - before[q]
            force = mode_forces(value, 1.0)
            done = {}
            weighted = []
            for i in range(24):
                f = force[i]
                if f is None:
                    weighted.append(None)
                    continue
                if id(f) not in done:
                    done[id(f)] = weight * f
                weighted.append(done[id(f)])
            totals = []
            for k in range(3):
                for c in range(2):
                    for b in range(2):
                        q = 4 * k + 2 * c + b
                        same = weighted[3 * (2 * b + c) + k]
                        change = weighted[3 * (4 + 2 * b + c) + k]
                        if not begin:
                            total = up_ref[q, at(j), :] - change
                            totals.append(total if same is None else total + same)
                        up_ref[q, at(j), :] = change if same is None else same + change
            if begin:
                continue
            out = []
            for k in range(3):
                parts = []
                for c in range(2):
                    same, change = totals[4 * k + 2 * c], totals[4 * k + 2 * c + 1]
                    over = rows(same + change, 1)
                    parts.append(same - change + jnp.where(first_row, carried[2 * k + c], over))
                    carried[2 * k + c] = over
                out.append(parts[0] - parts[1] + lanes(parts[0] + parts[1], 1))
            finish(n - 1, j, out)

    here = start(low - 1)
    for j in range(8):
        now, here = xy_modes(low - 1, j, here)
        for q in range(12):
            along_ref[q, at(j), :] = now[q]
    layer(low, True)

    def step(n, unused):
        layer(n, False)
        return unused

    lax.fori_loop(low + 1, high + 1, step, 0)


def free_of(keep_ref, tile):
    def free(n, j):
        inside = jnp.where(tile * 8 + n == H, jnp.float32(0.0), jnp.float32(1.0))
        return jnp.maximum(keep_ref[at(j), :], inside)

    return free


def tile_index():
    return lax.axis_index("grp") * lax.axis_size("gz") + lax.axis_index("gz")


def coarse_pattern():
    fine = lax.broadcasted_iota(jnp.int32, (128, 128), 0)
    lane = lax.broadcasted_iota(jnp.int32, (128, 128), 1)
    return jnp.where((fine >> 3) == (lane & 15), 1.0, 0.0).astype(jnp.float32)


def exact_dot(a, b, contract):
    return lax.dot_general(
        a, b, (contract, ((), ())), precision=lax.Precision.HIGHEST,
        preferred_element_type=jnp.float32,
    )


def block_sums(planes):
    count = planes.shape[0] // 64
    summed = exact_dot(planes, coarse_pattern(), ((1,), (0,)))
    row = lax.broadcasted_iota(jnp.int32, (64, 128), 0)
    lane = lax.broadcasted_iota(jnp.int32, (64, 128), 1)
    own = (row >> 3) == (lane >> 4)
    return [
        jnp.sum(jnp.where(own, summed[64 * k : 64 * k + 64], 0.0), axis=0, keepdims=True)
        for k in range(count)
    ]


def send_rows(out_ref, four):
    block = jnp.concatenate(four + four, 0)
    for i in range(out_ref.shape[0] // 8):
        out_ref[at(i), :] = block


def coarse_solve(gathered_ref, coarse_ref, tile, window_ref, solved_ref, spread_ref):
    begin = window_begin(tile)
    window_ref[...] = gathered_ref[pl.ds(pl.multiple_of(4 * begin, 8), 4 * WINDOW), :]
    rhs = [window_ref[pl.ds(k, WINDOW, stride=4), :] for k in range(3)]
    if coarse_ref is None:
        moduli = window_ref[pl.ds(3, WINDOW, stride=4), :]
        row = lax.broadcasted_iota(jnp.int32, (WINDOW, 128), 0)
        moduli = jnp.where(row == WINDOW - 1, 0.0, moduli)
    else:
        moduli = coarse_ref[...]
    summed = moduli + lanes(moduli, 1)
    summed = summed + lanes(summed, 16)
    summed = DIAGONAL * COARSEN * (summed + rows(summed, 1))
    inverse = jnp.where(summed > 0.0, 1.0 / jnp.where(summed > 0.0, summed, 1.0), 0.0)

    def apply(field):
        value = [None] * 24
        for k in range(3):
            near = lanes(field[k], -1)
            for c, along_x in enumerate((field[k] + near, near - field[k])):
                near_y = lanes(along_x, -16)
                for b, along_y in enumerate((along_x + near_y, near_y - along_x)):
                    near_z = rows(along_y, -1)
                    value[3 * (2 * b + c) + k] = along_y + near_z
                    value[3 * (4 + 2 * b + c) + k] = near_z - along_y
        force = [None if f is None else moduli * f for f in mode_forces(value, COARSEN)]
        result = []
        for k in range(3):
            parts_x = []
            for c in range(2):
                parts_y = []
                for b in range(2):
                    same, change = force[3 * (2 * b + c) + k], force[3 * (4 + 2 * b + c) + k]
                    if same is None:
                        parts_y.append(rows(change, 1) - change)
                    else:
                        parts_y.append(same - change + rows(same + change, 1))
                parts_x.append(parts_y[0] - parts_y[1] + lanes(parts_y[0] + parts_y[1], 16))
            result.append(parts_x[0] - parts_x[1] + lanes(parts_x[0] + parts_x[1], 1))
        return result

    bottom = BOUND / 20.0
    center = 0.5 * (BOUND + bottom)
    radius = 0.5 * (BOUND - bottom)
    sigma = center / radius
    rho = 1.0 / sigma
    update = [inverse * (s * (1.0 / center)) for s in rhs]
    correction = update
    remainder = rhs
    for sweep in range(CHEB - 1):
        image = apply(update)
        remainder = [r - a for r, a in zip(remainder, image)]
        rho_next = 1.0 / (2.0 * sigma - rho)
        update = [
            (rho_next * rho) * u + (2.0 * rho_next / radius) * (inverse * r)
            for u, r in zip(update, remainder)
        ]
        correction = [c + u for c, u in zip(correction, update)]
        rho = rho_next
    row = lax.broadcasted_iota(jnp.int32, (8, 128), 0)
    lane = lax.broadcasted_iota(jnp.int32, (8, 128), 1)
    own = row == (lane >> 4)
    for k in range(3):
        solved_ref[WINDOW * k : WINDOW * (k + 1), :] = correction[k]
    blocks = []
    for which in range(3):
        place = jnp.clip(tile - begin + which - 1, 0, WINDOW - 1)
        for k in range(3):
            line = solved_ref[pl.ds(WINDOW * k + place, 1), :]
            blocks.append(jnp.where(own, jnp.broadcast_to(line, (8, 128)), 0.0))
    spread_ref[...] = exact_dot(
        jnp.concatenate(blocks, 0), coarse_pattern(), ((1,), (1,))
    )
    return moduli


def window_begin(tile):
    return 2 * jnp.minimum(jnp.maximum(tile - 7, 0) >> 1, (128 - WINDOW) // 2)


def correction_of(spread_ref):
    def correction(n, j):
        which = jnp.where(n < H, 0, jnp.where(n < H + 8, 1, 2))
        return [
            jnp.broadcast_to(spread_ref[pl.ds((3 * which + k) * 8 + j, 1), :], (8, 128))
            for k in range(3)
        ]

    return correction


def set_up_kernel(load_ref, phases_ref, below_ref, above_ref, clamp_ref, table_ref,
                  rhs_ref, moduli_ref, inverse_ref, keep_ref, send_ref,
                  along_ref, up_ref, sum_ref):
    tile = tile_index()
    keep_ref[...] = 1.0 - clamp_ref[...].astype(jnp.float32)
    row = lax.broadcasted_iota(jnp.int32, (64, 128), 0)
    lane = lax.broadcasted_iota(jnp.int32, (64, 128), 1)
    interior = (row < 63) & (lane < 127)
    table = [table_ref[i] for i in range(4)]

    def pick(labels, n):
        depth = tile * 8 + n
        inside = interior & ((depth >= 0) & (depth < 1023))
        value = jnp.zeros((64, 128), jnp.float32)
        for i in range(4):
            value = jnp.where(labels == i, table[i], value)
        return jnp.where(inside, value, 0.0)

    for n in range(-5, 0):
        moduli_ref[n + H] = pick(below_ref[12 + n + 5].astype(jnp.int32), n)
    total = jnp.zeros((64, 128), jnp.float32)
    for n in range(8):
        value = pick(phases_ref[n], n)
        moduli_ref[n + H] = value
        total = total + value
    for n in range(8, 12):
        moduli_ref[n + H] = pick(above_ref[12 + n - 8].astype(jnp.int32), n)
    sum_ref[3] = total
    free = free_of(keep_ref, tile)

    for n in range(-4, 12):
        depth = tile * 8 + n
        both = moduli_ref[n - 1 + H] + moduli_ref[n + H]
        both = both + rows(both, 1)
        both = DIAGONAL * (both + lanes(both, 1))
        inside = jnp.where(depth == 0, jnp.float32(0.0), jnp.float32(1.0))
        held = jnp.maximum(keep_ref[...], inside)
        both = held * both + 1.0 - held
        exists = (depth >= 0) & (depth < 1024)
        both = jnp.where(exists, both, 1.0)
        inverse_ref[n + H] = jnp.where(exists, 1.0 / both, 0.0)
        for k in range(3):
            if n < 0:
                value = below_ref[4 * k + n + 4]
            elif n < 8:
                value = load_ref[k, n]
            else:
                value = above_ref[4 * k + n - 8]
            rhs_ref[k, n + H] = held * value

    for k in range(3):
        sum_ref[k] = jnp.zeros((64, 128), jnp.float32)

    def first(n, j):
        scaled = OMEGA * inverse_ref[n, at(j), :]
        return [rhs_ref[k, n, at(j), :] * scaled for k in range(3)]

    def finish(n, j, out):
        held = free(n, j) > 0.0
        value = first(n, j)
        for k in range(3):
            image = jnp.where(held, out[k], value[k])
            sum_ref[k, at(j), :] += rhs_ref[k, n, at(j), :] - image

    stiff(5, 13, first, finish, moduli_ref, along_ref, up_ref, free)
    four = block_sums(sum_ref[...].reshape(256, 128))
    lane = lax.broadcasted_iota(jnp.int32, (1, 128), 1)
    edge = (lane >= 112) | ((lane & 15) == 15) | (lax.rem(tile, GROUP) == GROUP - 1)
    four[3] = jnp.where(edge, 0.0, four[3] * (1.0 / 512.0))
    send_rows(send_ref, four)


def middle_kernel(gathered_ref, rhs_ref, moduli_ref, inverse_ref, keep_ref,
                  ahead_ref, image_ref, coarse_ref, send_ref,
                  along_ref, up_ref, sum_ref, dots_ref, window_ref, solved_ref, spread_ref):
    tile = tile_index()
    free = free_of(keep_ref, tile)
    coarse_ref[...] = coarse_solve(gathered_ref, None, tile, window_ref, solved_ref, spread_ref)
    correction = correction_of(spread_ref)

    def second(n, j):
        scaled = OMEGA * inverse_ref[n, at(j), :]
        held = free(n, j)
        result = []
        for k, coarse_value in enumerate(correction(n, j)):
            value = rhs_ref[k, n, at(j), :] * scaled + held * coarse_value
            result.append(value)
        return result

    def smooth(n, j, out):
        held = free(n, j) > 0.0
        scaled = OMEGA * inverse_ref[n, at(j), :]
        for k, value in enumerate(second(n, j)):
            image = jnp.where(held, out[k], value)
            ahead_ref[k, n, at(j), :] = value + (rhs_ref[k, n, at(j), :] - image) * scaled

    stiff(2, 16, second, smooth, moduli_ref, along_ref, up_ref, free)

    def ahead(n, j):
        return [ahead_ref[k, n, at(j), :] for k in range(3)]

    def keep_image(n, j, out):
        held = free(n, j) > 0.0
        for k in range(3):
            image_ref[k, n, at(j), :] = jnp.where(
                held, out[k], ahead_ref[k, n, at(j), :]
            )

    stiff(3, 15, ahead, keep_image, moduli_ref, along_ref, up_ref, free)

    for k in range(3):
        sum_ref[k] = jnp.zeros((64, 128), jnp.float32)
    dots_ref[...] = jnp.zeros_like(dots_ref)

    def first(n, j):
        scaled = OMEGA * inverse_ref[n, at(j), :]
        return [image_ref[k, n, at(j), :] * scaled for k in range(3)]

    def finish(n, j, out):
        held = free(n, j) > 0.0
        value = first(n, j)
        for k in range(3):
            image = image_ref[k, n, at(j), :]
            sum_ref[k, at(j), :] += image - jnp.where(held, out[k], value[k])
            now = ahead_ref[k, n, at(j), :]
            dots_ref[0, k] += now * rhs_ref[k, n, at(j), :]
            dots_ref[1, k] += now * image

    stiff(5, 13, first, finish, moduli_ref, along_ref, up_ref, free)
    three = block_sums(sum_ref[...].reshape(192, 128))
    lane = lax.broadcasted_iota(jnp.int32, (1, 128), 1)
    gamma = jnp.sum(dots_ref[0])
    energy = jnp.sum(dots_ref[1])
    dots = jnp.where(lane == 0, gamma, jnp.where(lane == 1, energy, 0.0))
    send_rows(send_ref, three + [dots])


def lane_value(line, i):
    lane = lax.broadcasted_iota(jnp.int32, line.shape, 1)
    return jnp.sum(jnp.where(lane == i, line, 0.0))


def last_kernel(gathered_ref, rhs_ref, moduli_ref, inverse_ref, keep_ref, ahead_ref, image_ref,
                coarse_ref,
                next_ref, next_image_ref, scalars_ref, send_ref,
                whole_ref, along_ref, up_ref, dots_ref, window_ref, solved_ref, spread_ref):
    tile = tile_index()
    free = free_of(keep_ref, tile)
    dots = jnp.sum(gathered_ref[pl.ds(3, 128, stride=4), :], axis=0, keepdims=True)
    scalars_ref[...] = jnp.broadcast_to(dots, (8, 128))
    alpha = lane_value(dots, 0) / lane_value(dots, 1)
    coarse_solve(gathered_ref, coarse_ref, tile, window_ref, solved_ref, spread_ref)
    correction = correction_of(spread_ref)

    def second(n, j):
        scaled = OMEGA * inverse_ref[n, at(j), :]
        held = free(n, j)
        result = []
        for k, coarse_value in enumerate(correction(n, j)):
            value = image_ref[k, n, at(j), :] * scaled + held * coarse_value
            result.append(value)
        return result

    def smooth(n, j, out):
        held = free(n, j) > 0.0
        scaled = OMEGA * inverse_ref[n, at(j), :]
        for k, value in enumerate(second(n, j)):
            image = jnp.where(held, out[k], value)
            value = value + (image_ref[k, n, at(j), :] - image) * scaled
            whole_ref[k, n, at(j), :] = ahead_ref[k, n, at(j), :] - alpha * value

    stiff(4, 14, second, smooth, moduli_ref, along_ref, up_ref, free)
    dots_ref[...] = jnp.zeros_like(dots_ref)

    def ahead(n, j):
        return [whole_ref[k, n, at(j), :] for k in range(3)]

    def finish(n, j, out):
        held = free(n, j) > 0.0
        for k in range(3):
            value = whole_ref[k, n, at(j), :]
            image = jnp.where(held, out[k], value)
            next_ref[k, n - H, at(j), :] = value
            next_image_ref[k, n - H, at(j), :] = image
            before = image_ref[k, n, at(j), :]
            dots_ref[0, k] += value * (rhs_ref[k, n, at(j), :] - alpha * before)
            dots_ref[1, k] += value * image
            dots_ref[2, k] += value * before

    stiff(5, 13, ahead, finish, moduli_ref, along_ref, up_ref, free)
    lane = lax.broadcasted_iota(jnp.int32, (8, 128), 1)
    line = jnp.zeros((8, 128), jnp.float32)
    for i in range(3):
        line = jnp.where(lane == i, jnp.sum(dots_ref[i]), line)
    for i in range(16):
        send_ref[at(i), :] = line


def close_kernel(gathered_ref, scalars_ref, rhs_ref, ahead_ref, image_ref, next_ref,
                 next_image_ref, displacement_ref, residual_ref):
    before = scalars_ref[0:1, :]
    gamma, energy = lane_value(before, 0), lane_value(before, 1)
    dots = jnp.sum(gathered_ref[...], axis=0, keepdims=True)
    following, own, cross = (lane_value(dots, i) for i in range(3))
    alpha = gamma / energy
    beta = following / gamma
    alpha_next = following / (own + 2.0 * beta * cross + beta * beta * energy)

    def step(n, unused):
        for k in range(3):
            ahead = ahead_ref[k, n + H]
            image = image_ref[k, n + H]
            direction = next_ref[k, n] + beta * ahead
            displacement_ref[k, n] = alpha * ahead + alpha_next * direction
            residual = rhs_ref[k, n + H] - alpha * image
            residual_ref[k, n] = residual - alpha_next * (next_image_ref[k, n] + beta * image)
        return unused

    lax.fori_loop(0, 8, step, 0)


def call(kernel, outs, scratch, *args, smem=()):
    spaces = [
        pl.BlockSpec(memory_space=pltpu.SMEM if i in smem else pltpu.VMEM)
        for i in range(len(args))
    ]
    return pl.pallas_call(
        kernel,
        out_shape=[jax.ShapeDtypeStruct(s, jnp.float32) for s in outs],
        in_specs=spaces,
        out_specs=[pl.BlockSpec(memory_space=pltpu.VMEM)] * len(outs),
        scratch_shapes=[pltpu.VMEM(s, jnp.float32) for s in scratch],
        compiler_params=pltpu.CompilerParams(vmem_limit_bytes=40 * 2**20),
    )(*args)


def to_all(block):
    count = block.shape[0] // 128
    parts = lax.all_to_all(block.reshape(128, count, 128), BOTH, 0, 0)
    return parts.reshape(block.shape)


def body(load, phases, clamp, phase_moduli):
    size = lax.axis_size(BOTH)
    labels = phases.astype(jnp.float32)
    top = jnp.concatenate([load[:, 4:].reshape(12, 64, 128), labels[3:]], 0)
    low = jnp.concatenate([load[:, :4].reshape(12, 64, 128), labels[:4]], 0)
    below = lax.ppermute(top, BOTH, [(i, i + 1) for i in range(size - 1)])
    above = lax.ppermute(low, BOTH, [(i + 1, i) for i in range(size - 1)])

    plane = (64, 128)
    field = (3, EXT) + plane
    work = [(12,) + plane, (12,) + plane]
    rhs, moduli, inverse, keep, send = call(
        set_up_kernel,
        [field, (EXT,) + plane, (EXT,) + plane, plane, (512, 128)],
        work + [(4,) + plane],
        load, phases, below, above, clamp, phase_moduli, smem=(5,),
    )
    gathered = to_all(send)
    ahead, image, coarse, send = call(
        middle_kernel,
        [field, field, (WINDOW, 128), (512, 128)],
        work + [(3,) + plane, (2, 3, 8, 128), (4 * WINDOW, 128), (3 * WINDOW, 128), (72, 128)],
        gathered, rhs, moduli, inverse, keep,
    )
    gathered = to_all(send)
    own = (3, 8) + plane
    following, following_image, scalars, send = call(
        last_kernel,
        [own, own, (8, 128), (128, 128)],
        [field] + work + [(3, 3, 8, 128), (4 * WINDOW, 128), (3 * WINDOW, 128), (72, 128)],
        gathered, rhs, moduli, inverse, keep, ahead, image, coarse,
    )
    gathered = to_all(send)
    displacement, residual = call(
        close_kernel, [own, own], [],
        gathered, scalars, rhs, ahead, image, following, following_image,
    )
    return displacement, residual


def solution(mesh):
    placed = (P(None, BOTH, None, None), P(BOTH, None, None), P(), P())
    return jax.shard_map(
        body,
        mesh=mesh,
        in_specs=placed,
        out_specs=(P(None, BOTH, None, None), P(None, BOTH, None, None)),
        check_vma=False,
    )
```

time: 2190 us -> 102 us (0.05); the launches traced: 2150 us -> 101 us
  blocking collectives: 1720 us -> 53.2 us
  other arithmetic: 150 us -> 1.05 us
  local copies, waits for them, and re-layouts: 116 us -> 1.31 us
  matrix products: 76.1 us -> 0 us
  starting transfers between devices: 41.9 us -> 6.52 us
  Pallas kernels: 0 us -> 30.1 us
    psum x5 -> x0, blocking collectives: 1640 us -> none  [the longest x2 1430 us: spread(): return lax.psum(block, axis)]
    all_gather x3 -> x0, blocking collectives: 80.9 us -> none  [the longest x2 54.5 us: precondition(): summed = lax.all_gather(restricted, 'gz', axis=1, tiled=True)]
    dot_general x12 -> x0, matrix products: 76.1 us -> none  [add_block(): jnp.einsum('ij,jzyx->izyx', matrix, gathered, precision=lax.Precision.HIG...]
    all_to_all x0 -> x3, blocking collectives: none -> 53.2 us  [to_all(): parts = lax.all_to_all(block.reshape(128, count, 128), BOTH, 0, 0)]
    while x60 -> x0, other arithmetic: 52.5 us -> none
    slice x137 -> x3, local copies, waits for them, and re-layouts: 43.1 us -> 1.29 us  [the longest x2 1.28 us: body(): low = jnp.concatenate([load[:, :4].reshape(12, 64, 128), labels[:4]], 0)]
    scatter-add x78 -> x0, other arithmetic: 36 us -> none  [the longest x72 30.6 us: add_block(): update.at[:, offset[0]:offset[0] + width]]
    ppermute x13 -> x2, starting transfers between devices: 41.9 us -> 6.52 us  [the longest x1 4.59 us: body(): below = lax.ppermute(top, BOTH, [(i, i + 1) for i in range(size - 1)])]
  transfers between devices with their start and end apart: 13 -> 2, of which waited for: 10 -> 1; matrix products, arithmetic and copies ran while one was open for 1% -> 0% of each run, Pallas kernels for 0% -> 0%
where the time goes in v1:
time: 102 us; the launch traced here: 101 us
  blocking collectives  53.2 us (52%)
  Pallas kernels  30.1 us (30%)
  waiting for transfers between devices  8.57 us (8%)
  starting transfers between devices  6.52 us (6%)
  local copies, waits for them, and re-layouts  1.31 us (1%)
  other arithmetic  1.05 us (1%)
    all_to_all x3, blocking collectives, to_all(): parts = lax.all_to_all(block.reshape(128, count, 128), BOTH, 0, 0)  53.2 us
    pallas_call x4, Pallas kernels, call(): pl.pallas_call(kernel, out_shape=[jax.ShapeDtypeStruct(s, jnp.float32) fo...  30.1 us
    ppermute x1, waiting for transfers between devices, body(): above = lax.ppermute(low, BOTH, [(i + 1, i) for i in range(size - 1)])  8.57 us
    ppermute x1, starting transfers between devices, body(): below = lax.ppermute(top, BOTH, [(i, i + 1) for i in range(size - 1)])  4.59 us
  transfers between devices with their start and end apart: 2, of which 1 were waited for; matrix products, arithmetic and copies ran while one was open for 0% of the time, Pallas kernels for 0%

profile of v1, /device:TPU:1, one launch (start us, length us, event | category | flops | bytes accessed | tf_op | source)
XLA Modules:
  0.0 101.5 jit_solution(3630568112251108089)
XLA Ops:
  0.6 1.0 convert_element_type.3
  1.6 0.0 copy-start
  1.6 0.0 copy-start.1
  1.6 0.0 copy-start.2
  1.7 0.0 copy-start.3
  1.7 1.3 %fusion = (f32[3,4,64,128]{3,2,1,0:T(8,128)S(1)}, f32[3,4,64,128]{3,2,1,0:T(8,128)S(1)}) fusion(f32[3,8,64,128]{3,2,1,0:T(8,128)} %load_ref.1), kind=kLoop, calls=%fused_computation.2 | loop fusion | bytes 1572864 | tf_op jit(solution)/shard_map/slice | solution.py:592
  3.0 4.6 %collective-permute-start = (f32[17,64,128]{2,1,0:T(8,128)S(1)}, f32[17,64,128]{2,1,0:T(8,128)S(1)}, u32[]{:S(2)}, u32[]{:S(2)}) collective-permute-start(f32[17,64,128]{2,1,0:T(8,128)S(1)} %pad_maximum_fusion), channel_id=1, source_target_pairs={{0,1},{1,2},{2,3},{3,4},{4,5},{5,6},{6,7},{7,8},{8,9},{9,10},{10,1... | collective-permute-start | bytes 1671176 | tf_op jit(solution)/shard_map/ppermute | solution.py:593
  7.7 1.9 %collective-permute-start.1 = (f32[16,64,128]{2,1,0:T(8,128)S(1)}, f32[16,64,128]{2,1,0:T(8,128)S(1)}, u32[]{:S(2)}, u32[]{:S(2)}) collective-permute-start(f32[16,64,128]{2,1,0:T(8,128)S(1)} %pad_maximum_fusion.1), channel_id=1, source_target_pairs={{1,0},{2,1},{3,2},{4,3},{5,4},{6,5},{7,6},{8,7},{9,8},{10,9},{11,1... | collective-permute-start | bytes 1572872 | tf_op jit(solution)/shard_map/ppermute | solution.py:594
  9.6 8.6 %collective-permute-done.1.above_ref = f32[16,64,128]{2,1,0:T(8,128)S(1)} collective-permute-done((f32[16,64,128]{2,1,0:T(8,128)S(1)}, f32[16,64,128]{2,1,0:T(8,128)S(1)}, u32[]{:S(2)}, u32[]{:S(2)}) %collective-permute-start.1) | collective-permute-done | bytes 524320 | tf_op jit(solution)/shard_map/ppermute | solution.py:594
  18.2 0.0 collective-permute-done.below_ref
  18.2 0.0 copy-done
  18.2 0.0 copy-done.1
  18.2 0.0 copy-done.2
  18.2 0.0 copy-done.3
  18.2 4.5 %shard_map.59 = (f32[3,17,64,128]{3,2,1,0:T(8,128)S(1)}, f32[17,64,128]{2,1,0:T(8,128)S(1)}, f32[17,64,128]{2,1,0:T(8,128)S(1)}, f32[64,128]{1,0:T(8,128)S(1)}, f32[512,128]{1,0:T(8,128)S(1)}) custom-call(f32[3,8,64,128]{3,2,1,0:T(8,128)S(1)} %copy-done, s32[8,64,128]{2,1,0:T(8,128)S(1)} %copy-done.1, f32[17,64,128]{2,1,0:T(8,128)S(1)} %collective-permute-done.below_ref, ...), custom_call_target="tpu_custom_call" | custom-call | tf_op jit(solution)/shard_map/pallas_call | solution.py:572
  22.7 24.2 %all_to_all.15 = f32[128,4,128]{2,1,0:T(4,128)S(1)} all-to-all(f32[128,4,128]{2,1,0:T(4,128)S(1)} %bitcast.13), channel_id=1, replica_groups=mesh['grp'=4,'gz'=32] {'grp','gz'}, dimensions={0} | all-to-all | bytes 524288 | tf_op jit(solution)/shard_map/all_to_all | solution.py:584
  46.9 15.1 %shard_map.60 = (f32[3,17,64,128]{3,2,1,0:T(8,128)S(1)}, f32[3,17,64,128]{3,2,1,0:T(8,128)S(1)}, f32[16,128]{1,0:T(8,128)S(1)}, f32[512,128]{1,0:T(8,128)S(1)}) custom-call(f32[512,128]{1,0:T(8,128)S(1)} %bitcast.11, f32[3,17,64,128]{3,2,1,0:T(8,128)S(1)} %get-tuple-element.16.rhs_ref, f32[17,64,128]{2,1,0:T(8,128)S(1)} %get-tuple-element.17.moduli_ref, ...), custom_call_target="tpu_custom_call" | custom-call | tf_op jit(solution)/shard_map/pallas_call | solution.py:572
  62.1 15.2 %all_to_all.16 = f32[128,4,128]{2,1,0:T(4,128)S(1)} all-to-all(f32[128,4,128]{2,1,0:T(4,128)S(1)} %bitcast.14), channel_id=1, replica_groups=mesh['grp'=4,'gz'=32] {'grp','gz'}, dimensions={0} | all-to-all | bytes 524288 | tf_op jit(solution)/shard_map/all_to_all | solution.py:584
  77.3 8.8 %shard_map.61 = (f32[3,8,64,128]{3,2,1,0:T(8,128)S(1)}, f32[3,8,64,128]{3,2,1,0:T(8,128)S(1)}, f32[8,128]{1,0:T(8,128)S(1)}, f32[128,128]{1,0:T(8,128)S(1)}) custom-call(f32[512,128]{1,0:T(8,128)S(1)} %bitcast.10, f32[3,17,64,128]{3,2,1,0:T(8,128)S(1)} %get-tuple-element.16.rhs_ref, f32[17,64,128]{2,1,0:T(8,128)S(1)} %get-tuple-element.17.moduli_ref, ...), custom_call_target="tpu_custom_call" | custom-call | tf_op jit(solution)/shard_map/pallas_call | solution.py:572
  86.0 13.7 %all_to_all.17 = f32[128,1,128]{2,1,0:T(1,128)S(1)} all-to-all(f32[128,1,128]{2,1,0:T(1,128)S(1)} %bitcast.15), channel_id=1, replica_groups=mesh['grp'=4,'gz'=32] {'grp','gz'}, dimensions={0} | all-to-all | bytes 131072 | tf_op jit(solution)/shard_map/all_to_all | solution.py:584
  99.7 1.7 %shard_map.62 = (f32[3,8,64,128]{3,2,1,0:T(8,128)}, f32[3,8,64,128]{3,2,1,0:T(8,128)}) custom-call(f32[128,128]{1,0:T(8,128)S(1)} %bitcast.12, f32[8,128]{1,0:T(8,128)S(1)} %get-tuple-element.25.scalars_ref, f32[3,17,64,128]{3,2,1,0:T(8,128)S(1)} %get-tuple-element.16.rhs_ref, f32[3,17,64,128]{3,2,1,0:T(8,128)S(1)} %get-tuple-element.21.ahead_ref, ...), custom_call_target="tpu_custom_call" | custom-call | tf_op jit(solution)/shard_map/pallas_call | solution.py:572
  (4 shorter events, 0.1 us)
Async XLA Ops:
  1.6 16.5 %copy-start = (f32[3,8,64,128]{3,2,1,0:T(8,128)S(1)}, f32[3,8,64,128]{3,2,1,0:T(8,128)}, u32[]{:S(2)}) copy-start(f32[3,8,64,128]{3,2,1,0:T(8,128)} %load_ref.1) | copy-start | bytes 2359300
  1.6 16.5 %copy-start.1 = (s32[8,64,128]{2,1,0:T(8,128)S(1)}, s32[8,64,128]{2,1,0:T(8,128)}, u32[]{:S(2)}) copy-start(s32[8,64,128]{2,1,0:T(8,128)} %phases_ref.1) | copy-start | bytes 786436
  1.6 16.5 %copy-start.2 = (s32[64,128]{1,0:T(8,128)S(1)}, s32[64,128]{1,0:T(8,128)}, u32[]{:S(2)}) copy-start(s32[64,128]{1,0:T(8,128)} %clamp_ref.1) | copy-start | bytes 98308
  1.7 16.5 %copy-start.3 = (f32[4]{0:T(128)S(1)}, f32[4]{0:T(128)}, u32[]{:S(2)}) copy-start(f32[4]{0:T(128)} %table_ref.1) | copy-start | bytes 52
  3.0 15.2 %collective-permute-start = (f32[17,64,128]{2,1,0:T(8,128)S(1)}, f32[17,64,128]{2,1,0:T(8,128)S(1)}, u32[]{:S(2)}, u32[]{:S(2)}) collective-permute-start(f32[17,64,128]{2,1,0:T(8,128)S(1)} %pad_maximum_fusion), channel_id=1, source_target_pairs={{0,1},{1,2},{2,3},{3,4},{4,5},{5,6},{6,7},{7,8},{8,9},{9,10},{10,1... | collective-permute-start | bytes 1671176 | tf_op jit(solution)/shard_map/ppermute | solution.py:593
  7.7 10.5 %collective-permute-start.1 = (f32[16,64,128]{2,1,0:T(8,128)S(1)}, f32[16,64,128]{2,1,0:T(8,128)S(1)}, u32[]{:S(2)}, u32[]{:S(2)}) collective-permute-start(f32[16,64,128]{2,1,0:T(8,128)S(1)} %pad_maximum_fusion.1), channel_id=1, source_target_pairs={{1,0},{2,1},{3,2},{4,3},{5,4},{6,5},{7,6},{8,7},{9,8},{10,9},{11,1... | collective-permute-start | bytes 1572872 | tf_op jit(solution)/shard_map/ppermute | solution.py:594

commit v2 on v1

--- a/solution.py
+++ b/solution.py
@@ -113,45 +113,50 @@
     return slice(8 * j, 8 * j + 8)
 
 
-def stiff(low, high, field, finish, moduli_ref, along_ref, up_ref, free):
+def stiff(low, high, field, finish, moduli_ref, along_ref, up_ref, free, x_ref, late_ref):
     row = lax.broadcasted_iota(jnp.int32, (8, 128), 0)
     first_row = row == 0
     last_row = row == 7
 
     def x_modes(n, j):
         held = free(n, j)
-        result = []
-        for value in field(n, j):
+        for k, value in enumerate(field(n, j)):
             value = value * held
             beside = lanes(value, -1)
-            result += [value + beside, beside - value]
-        return result
-
-    def xy_modes(n, j, here):
-        if j < 7:
-            values = x_modes(n, j + 1)
-            after = (values, [rows(v, -1) for v in values])
-        else:
-            zero = jnp.zeros((8, 128), jnp.float32)
-            after = ([zero] * 6, [zero] * 6)
+            x_ref[2 * k, at(j), :] = value + beside
+            x_ref[2 * k + 1, at(j), :] = beside - value
+
+    def take(j):
+        values = [x_ref[q, at(j), :] for q in range(6)]
+        return values, [rows(v, -1) for v in values]
+
+    def xy_modes(here, after):
         result = []
         for value, rolled, rolled_after in zip(here[0], here[1], after[1]):
             beside = jnp.where(last_row, rolled_after, rolled)
             result += [value + beside, beside - value]
-        return result, after
-
-    def start(n):
-        values = x_modes(n, 0)
-        return values, [rows(v, -1) for v in values]
-
-    def layer(n, begin):
-        here = start(n)
+        return result
+
+    def flush(n, j):
+        late = [late_ref[q, at(j), :] for q in range(6)]
+        finish(n, j, [late[2 * k] + lanes(late[2 * k + 1], 1) for k in range(3)])
+
+    def layer(n, stage):
+        here = take(0)
         carried = [jnp.zeros((8, 128), jnp.float32)] * 6
+        zero = jnp.zeros((8, 128), jnp.float32)
         for j in range(8):
-            now, here = xy_modes(n, j, here)
+            after = take(j + 1) if j < 7 else ([zero] * 6, [zero] * 6)
+            now = xy_modes(here, after)
+            here = after
+            x_modes(jnp.minimum(n + 1, high), j)
+            if stage > 2:
+                flush(n - 2, j)
             before = [along_ref[q, at(j), :] for q in range(12)]
             for q in range(12):
                 along_ref[q, at(j), :] = now[q]
+            if stage == 0:
+                continue
             weight = moduli_ref[n - 1, at(j), :]
             value = [None] * 24
             for k in range(3):
@@ -178,13 +183,12 @@
                         q = 4 * k + 2 * c + b
                         same = weighted[3 * (2 * b + c) + k]
                         change = weighted[3 * (4 + 2 * b + c) + k]
-                        if not begin:
+                        if stage > 1:
                             total = up_ref[q, at(j), :] - change
                             totals.append(total if same is None else total + same)
                         up_ref[q, at(j), :] = change if same is None else same + change
-            if begin:
+            if stage == 1:
                 continue
-            out = []
             for k in range(3):
                 parts = []
                 for c in range(2):
@@ -192,21 +196,25 @@
                     over = rows(same + change, 1)
                     parts.append(same - change + jnp.where(first_row, carried[2 * k + c], over))
                     carried[2 * k + c] = over
-                out.append(parts[0] - parts[1] + lanes(parts[0] + parts[1], 1))
-            finish(n - 1, j, out)
-
-    here = start(low - 1)
+                late_ref[2 * k, at(j), :] = parts[0] - parts[1]
+                late_ref[2 * k + 1, at(j), :] = parts[0] + parts[1]
+
     for j in range(8):
-        now, here = xy_modes(low - 1, j, here)
-        for q in range(12):
-            along_ref[q, at(j), :] = now[q]
-    layer(low, True)
-
-    def step(n, unused):
-        layer(n, False)
+        x_modes(low - 1, j)
+    for stage in range(3):
+        layer(low - 1 + stage, stage)
+
+    def step(i, unused):
+        layer(low + 2 + 2 * i, 3)
+        layer(low + 3 + 2 * i, 3)
         return unused
 
-    lax.fori_loop(low + 1, high + 1, step, 0)
+    pairs = (high - low - 1) // 2
+    lax.fori_loop(0, pairs, step, 0)
+    if low + 2 + 2 * pairs == high:
+        layer(high, 3)
+    for j in range(8):
+        flush(high - 1, j)
 
 
 def free_of(keep_ref, tile):
@@ -343,56 +351,73 @@
     return correction
 
 
-def set_up_kernel(load_ref, phases_ref, below_ref, above_ref, clamp_ref, table_ref,
-                  rhs_ref, moduli_ref, inverse_ref, keep_ref, send_ref,
-                  along_ref, up_ref, sum_ref):
-    tile = tile_index()
-    keep_ref[...] = 1.0 - clamp_ref[...].astype(jnp.float32)
+def set_up(low, high, load_ref, phases_ref, below_refs, above_refs, table_ref, keep_ref,
+           rhs_ref, moduli_ref, inverse_ref, tile):
     row = lax.broadcasted_iota(jnp.int32, (64, 128), 0)
     lane = lax.broadcasted_iota(jnp.int32, (64, 128), 1)
     interior = (row < 63) & (lane < 127)
     table = [table_ref[i] for i in range(4)]
 
-    def pick(labels, n):
+    def label(n):
+        if n < -2:
+            return below_refs[1][9 + n + 5].astype(jnp.int32)
+        if n < 0:
+            return below_refs[0][3 + n + 2].astype(jnp.int32)
+        if n < 8:
+            return phases_ref[n]
+        if n < 9:
+            return above_refs[0][3].astype(jnp.int32)
+        return above_refs[1][9 + n - 9].astype(jnp.int32)
+
+    def load(k, n):
+        if n < -1:
+            return below_refs[1][3 * k + n + 4]
+        if n < 0:
+            return below_refs[0][k]
+        if n < 8:
+            return load_ref[k, n]
+        if n < 9:
+            return above_refs[0][k]
+        return above_refs[1][3 * k + n - 9]
+
+    before = None
+    for n in range(low - 1, high):
         depth = tile * 8 + n
         inside = interior & ((depth >= 0) & (depth < 1023))
+        labels = label(n)
         value = jnp.zeros((64, 128), jnp.float32)
         for i in range(4):
             value = jnp.where(labels == i, table[i], value)
-        return jnp.where(inside, value, 0.0)
-
-    for n in range(-5, 0):
-        moduli_ref[n + H] = pick(below_ref[12 + n + 5].astype(jnp.int32), n)
-    total = jnp.zeros((64, 128), jnp.float32)
-    for n in range(8):
-        value = pick(phases_ref[n], n)
+        value = jnp.where(inside, value, 0.0)
         moduli_ref[n + H] = value
-        total = total + value
-    for n in range(8, 12):
-        moduli_ref[n + H] = pick(above_ref[12 + n - 8].astype(jnp.int32), n)
+        if n >= low:
+            both = before + value
+            both = both + rows(both, 1)
+            both = DIAGONAL * (both + lanes(both, 1))
+            inside = jnp.where(depth == 0, jnp.float32(0.0), jnp.float32(1.0))
+            held = jnp.maximum(keep_ref[...], inside)
+            both = held * both + 1.0 - held
+            exists = (depth >= 0) & (depth < 1024)
+            both = jnp.where(exists, both, 1.0)
+            inverse_ref[n + H] = jnp.where(exists, 1.0 / both, 0.0)
+            for k in range(3):
+                rhs_ref[k, n + H] = held * load(k, n)
+        before = value
+
+
+def first_kernel(load_ref, phases_ref, below_ref, above_ref, clamp_ref, table_ref,
+                 send_ref,
+                 rhs_ref, moduli_ref, inverse_ref, keep_ref,
+                 along_ref, up_ref, x_ref, late_ref, sum_ref):
+    tile = tile_index()
+    keep_ref[...] = 1.0 - clamp_ref[...].astype(jnp.float32)
+    set_up(-1, 9, load_ref, phases_ref, (below_ref,), (above_ref,), table_ref, keep_ref,
+           rhs_ref, moduli_ref, inverse_ref, tile)
+    free = free_of(keep_ref, tile)
+    total = moduli_ref[H]
+    for n in range(1, 8):
+        total = total + moduli_ref[n + H]
     sum_ref[3] = total
-    free = free_of(keep_ref, tile)
-
-    for n in range(-4, 12):
-        depth = tile * 8 + n
-        both = moduli_ref[n - 1 + H] + moduli_ref[n + H]
-        both = both + rows(both, 1)
-        both = DIAGONAL * (both + lanes(both, 1))
-        inside = jnp.where(depth == 0, jnp.float32(0.0), jnp.float32(1.0))
-        held = jnp.maximum(keep_ref[...], inside)
-        both = held * both + 1.0 - held
-        exists = (depth >= 0) & (depth < 1024)
-        both = jnp.where(exists, both, 1.0)
-        inverse_ref[n + H] = jnp.where(exists, 1.0 / both, 0.0)
-        for k in range(3):
-            if n < 0:
-                value = below_ref[4 * k + n + 4]
-            elif n < 8:
-                value = load_ref[k, n]
-            else:
-                value = above_ref[4 * k + n - 8]
-            rhs_ref[k, n + H] = held * value
-
     for k in range(3):
         sum_ref[k] = jnp.zeros((64, 128), jnp.float32)
 
@@ -407,7 +432,7 @@
             image = jnp.where(held, out[k], value[k])
             sum_ref[k, at(j), :] += rhs_ref[k, n, at(j), :] - image
 
-    stiff(5, 13, first, finish, moduli_ref, along_ref, up_ref, free)
+    stiff(5, 13, first, finish, moduli_ref, along_ref, up_ref, free, x_ref, late_ref)
     four = block_sums(sum_ref[...].reshape(256, 128))
     lane = lax.broadcasted_iota(jnp.int32, (1, 128), 1)
     edge = (lane >= 112) | ((lane & 15) == 15) | (lax.rem(tile, GROUP) == GROUP - 1)
@@ -415,9 +440,18 @@
     send_rows(send_ref, four)
 
 
+def ready_kernel(load_ref, phases_ref, below_ref, above_ref, far_below_ref, far_above_ref,
+                 clamp_ref, table_ref,
+                 rhs_ref, moduli_ref, inverse_ref, keep_ref):
+    keep_ref[...] = 1.0 - clamp_ref[...].astype(jnp.float32)
+    set_up(-4, 12, load_ref, phases_ref, (below_ref, far_below_ref),
+           (above_ref, far_above_ref), table_ref, keep_ref,
+           rhs_ref, moduli_ref, inverse_ref, tile_index())
+
+
 def middle_kernel(gathered_ref, rhs_ref, moduli_ref, inverse_ref, keep_ref,
                   ahead_ref, image_ref, coarse_ref, send_ref,
-                  along_ref, up_ref, sum_ref, dots_ref, window_ref, solved_ref, spread_ref):
+                  along_ref, up_ref, x_ref, late_ref, sum_ref, dots_ref, window_ref, solved_ref, spread_ref):
     tile = tile_index()
     free = free_of(keep_ref, tile)
     coarse_ref[...] = coarse_solve(gathered_ref, None, tile, window_ref, solved_ref, spread_ref)
@@ -439,7 +473,7 @@
             image = jnp.where(held, out[k], value)
             ahead_ref[k, n, at(j), :] = value + (rhs_ref[k, n, at(j), :] - image) * scaled
 
-    stiff(2, 16, second, smooth, moduli_ref, along_ref, up_ref, free)
+    stiff(2, 16, second, smooth, moduli_ref, along_ref, up_ref, free, x_ref, late_ref)
 
     def ahead(n, j):
         return [ahead_ref[k, n, at(j), :] for k in range(3)]
@@ -451,7 +485,7 @@
                 held, out[k], ahead_ref[k, n, at(j), :]
             )
 
-    stiff(3, 15, ahead, keep_image, moduli_ref, along_ref, up_ref, free)
+    stiff(3, 15, ahead, keep_image, moduli_ref, along_ref, up_ref, free, x_ref, late_ref)
 
     for k in range(3):
         sum_ref[k] = jnp.zeros((64, 128), jnp.float32)
@@ -471,7 +505,7 @@
             dots_ref[0, k] += now * rhs_ref[k, n, at(j), :]
             dots_ref[1, k] += now * image
 
-    stiff(5, 13, first, finish, moduli_ref, along_ref, up_ref, free)
+    stiff(5, 13, first, finish, moduli_ref, along_ref, up_ref, free, x_ref, late_ref)
     three = block_sums(sum_ref[...].reshape(192, 128))
     lane = lax.broadcasted_iota(jnp.int32, (1, 128), 1)
     gamma = jnp.sum(dots_ref[0])
@@ -488,7 +522,7 @@
 def last_kernel(gathered_ref, rhs_ref, moduli_ref, inverse_ref, keep_ref, ahead_ref, image_ref,
                 coarse_ref,
                 next_ref, next_image_ref, scalars_ref, send_ref,
-                whole_ref, along_ref, up_ref, dots_ref, window_ref, solved_ref, spread_ref):
+                whole_ref, along_ref, up_ref, x_ref, late_ref, dots_ref, window_ref, solved_ref, spread_ref):
     tile = tile_index()
     free = free_of(keep_ref, tile)
     dots = jnp.sum(gathered_ref[pl.ds(3, 128, stride=4), :], axis=0, keepdims=True)
@@ -514,7 +548,7 @@
             value = value + (image_ref[k, n, at(j), :] - image) * scaled
             whole_ref[k, n, at(j), :] = ahead_ref[k, n, at(j), :] - alpha * value
 
-    stiff(4, 14, second, smooth, moduli_ref, along_ref, up_ref, free)
+    stiff(4, 14, second, smooth, moduli_ref, along_ref, up_ref, free, x_ref, late_ref)
     dots_ref[...] = jnp.zeros_like(dots_ref)
 
     def ahead(n, j):
@@ -532,7 +566,7 @@
             dots_ref[1, k] += value * image
             dots_ref[2, k] += value * before
 
-    stiff(5, 13, ahead, finish, moduli_ref, along_ref, up_ref, free)
+    stiff(5, 13, ahead, finish, moduli_ref, along_ref, up_ref, free, x_ref, late_ref)
     lane = lax.broadcasted_iota(jnp.int32, (8, 128), 1)
     line = jnp.zeros((8, 128), jnp.float32)
     for i in range(3):
@@ -575,7 +609,7 @@
         in_specs=spaces,
         out_specs=[pl.BlockSpec(memory_space=pltpu.VMEM)] * len(outs),
         scratch_shapes=[pltpu.VMEM(s, jnp.float32) for s in scratch],
-        compiler_params=pltpu.CompilerParams(vmem_limit_bytes=40 * 2**20),
+        compiler_params=pltpu.CompilerParams(vmem_limit_bytes=14 * 2**20),
     )(*args)
 
 
@@ -587,22 +621,36 @@
 
 def body(load, phases, clamp, phase_moduli):
     size = lax.axis_size(BOTH)
-    labels = phases.astype(jnp.float32)
-    top = jnp.concatenate([load[:, 4:].reshape(12, 64, 128), labels[3:]], 0)
-    low = jnp.concatenate([load[:, :4].reshape(12, 64, 128), labels[:4]], 0)
-    below = lax.ppermute(top, BOTH, [(i, i + 1) for i in range(size - 1)])
-    above = lax.ppermute(low, BOTH, [(i + 1, i) for i in range(size - 1)])
+    up = [(i, i + 1) for i in range(size - 1)]
+    down = [(i + 1, i) for i in range(size - 1)]
+
+    def pack(load, phases, first, last, first_phase, last_phase=None):
+        nodes = load[:, first:last].reshape(3 * (last - first), 64, 128)
+        labels = phases[first_phase : last_phase or last].astype(jnp.float32)
+        return jnp.concatenate([nodes, labels], 0)
+
+    near_top, near_low = pack(load, phases, 7, 8, 6), pack(load, phases, 0, 1, 0)
+    below = lax.ppermute(near_top, BOTH, up)
+    above = lax.ppermute(near_low, BOTH, down)
+    far_load, far_phases, unused = lax.optimization_barrier((load, phases, (near_top, near_low)))
+    far_below = lax.ppermute(pack(far_load, far_phases, 4, 7, 3, 6), BOTH, up)
+    far_above = lax.ppermute(pack(far_load, far_phases, 1, 4, 1), BOTH, down)
 
     plane = (64, 128)
     field = (3, EXT) + plane
-    work = [(12,) + plane, (12,) + plane]
-    rhs, moduli, inverse, keep, send = call(
-        set_up_kernel,
-        [field, (EXT,) + plane, (EXT,) + plane, plane, (512, 128)],
-        work + [(4,) + plane],
+    ready = [field, (EXT,) + plane, (EXT,) + plane, plane]
+    work = [(12,) + plane, (12,) + plane, (6,) + plane, (6,) + plane]
+    (send,) = call(
+        first_kernel,
+        [(512, 128)],
+        ready + work + [(4,) + plane],
         load, phases, below, above, clamp, phase_moduli, smem=(5,),
     )
     gathered = to_all(send)
+    rhs, moduli, inverse, keep = call(
+        ready_kernel, ready, [],
+        load, phases, below, above, far_below, far_above, clamp, phase_moduli, smem=(7,),
+    )
     ahead, image, coarse, send = call(
         middle_kernel,
         [field, field, (WINDOW, 128), (512, 128)],

time: 102 us -> 106 us (1.039)
  blocking collectives: 53.2 us -> 31.8 us
  starting transfers between devices: 6.52 us -> 24.2 us
  local copies, waits for them, and re-layouts: 1.31 us -> 11 us
  Pallas kernels: 30.1 us -> 25.8 us
  other arithmetic: 1.05 us -> 2.79 us
    all_to_all x3 -> x2, blocking collectives: 53.2 us -> 31.8 us  [to_all(): parts = lax.all_to_all(block.reshape(128, count, 128), BOTH, 0, 0)]
    all_to_all x0 -> x1, starting transfers between devices: none -> 13.3 us  [to_all(): parts = lax.all_to_all(block.reshape(128, count, 128), BOTH, 0, 0)]
    unnamed x8 -> x34, local copies, waits for them, and re-layouts: 0.03 us -> 9.97 us
    ppermute x2 -> x4, starting transfers between devices: 6.52 us -> 10.9 us  [the longest x1 4.59 us: body(): below = lax.ppermute(near_top, BOTH, up)]
    pallas_call x4 -> x5, Pallas kernels: 30.1 us -> 25.8 us  [call(): pl.pallas_call(kernel, out_shape=[jax.ShapeDtypeStruct(s, jnp.float32) fo...]
    all_to_all x0 -> x1, waiting for transfers between devices: none -> 2.54 us  [to_all(): parts = lax.all_to_all(block.reshape(128, count, 128), BOTH, 0, 0)]
    ppermute x2 -> x4, waiting for transfers between devices: 8.57 us -> 6.15 us  [the longest x1 6.14 us: body(): above = lax.ppermute(near_low, BOTH, down)]
    convert_element_type x1 -> x3, other arithmetic: 0.97 us -> 2.71 us  [pack(): labels = phases[first_phase:last_phase or last].astype(jnp.float32)]
  transfers between devices with their start and end apart: 2 -> 5, of which waited for: 1 -> 2; matrix products, arithmetic and copies ran while one was open for 0% -> 2% of each run, Pallas kernels for 0% -> 5%
where the time goes in v2:
time: 106 us; the launch traced here: 105 us
  blocking collectives  31.8 us (30%)
  Pallas kernels  25.8 us (24%)
  starting transfers between devices  24.2 us (23%)
  local copies, waits for them, and re-layouts  11 us (10%)
  waiting for transfers between devices  8.68 us (8%)
  other arithmetic  2.79 us (3%)
    all_to_all x2, blocking collectives, to_all(): parts = lax.all_to_all(block.reshape(128, count, 128), BOTH, 0, 0)  31.8 us
    pallas_call x5, Pallas kernels, call(): pl.pallas_call(kernel, out_shape=[jax.ShapeDtypeStruct(s, jnp.float32) fo...  25.8 us
    all_to_all x1, starting transfers between devices, to_all(): parts = lax.all_to_all(block.reshape(128, count, 128), BOTH, 0, 0)  13.3 us
    unnamed x34, local copies, waits for them, and re-layouts  9.97 us
    ppermute x1, waiting for transfers between devices, body(): above = lax.ppermute(near_low, BOTH, down)  6.14 us
    ppermute x1, starting transfers between devices, body(): below = lax.ppermute(near_top, BOTH, up)  4.59 us
    convert_element_type x3, other arithmetic, pack(): labels = phases[first_phase:last_phase or last].astype(jnp.float32)  2.71 us
    all_to_all x1, waiting for transfers between devices, to_all(): parts = lax.all_to_all(block.reshape(128, count, 128), BOTH, 0, 0)  2.54 us
  transfers between devices with their start and end apart: 5, of which 2 were waited for; matrix products, arithmetic and copies ran while one was open for 2% of the time, Pallas kernels for 5%

profile of v2, /device:TPU:1, one launch (start us, length us, event | category | flops | bytes accessed | tf_op | source)
XLA Modules:
  0.0 105.1 jit_solution(1796732177017828402)
XLA Ops:
  0.6 0.9 slice_convert_fusion.2
  1.6 1.0 slice_bitcast_fusion
  2.5 4.6 %collective-permute-start = (f32[5,64,128]{2,1,0:T(8,128)S(1)}, f32[5,64,128]{2,1,0:T(8,128)S(1)}, u32[]{:S(2)}, u32[]{:S(2)}) collective-permute-start(f32[5,64,128]{2,1,0:T(8,128)S(1)} %pad_maximum_fusion.2), channel_id=1, source_target_pairs={{0,1},{1,2},{2,3},{3,4},{4,5},{5,6},{6,7},{7,8},{8,9},{9,10},{10,1... | collective-permute-start | bytes 491528 | tf_op jit(solution)/shard_map/ppermute | solution.py:633
  7.1 0.8 slice_convert_fusion.3
  7.9 1.0 slice_convert_fusion
  9.1 1.9 %collective-permute-start.2 = (f32[12,64,128]{2,1,0:T(8,128)S(1)}, f32[12,64,128]{2,1,0:T(8,128)S(1)}, u32[]{:S(2)}, u32[]{:S(2)}) collective-permute-start(f32[12,64,128]{2,1,0:T(8,128)S(1)} %pad_maximum_fusion), channel_id=1, source_target_pairs={{0,1},{1,2},{2,3},{3,4},{4,5},{5,6},{6,7},{7,8},{8,9},{9,10},{10,1... | collective-permute-start | bytes 1179656 | tf_op jit(solution)/shard_map/ppermute | solution.py:636
  11.0 2.4 %collective-permute-start.3 = (f32[12,64,128]{2,1,0:T(8,128)S(1)}, f32[12,64,128]{2,1,0:T(8,128)S(1)}, u32[]{:S(2)}, u32[]{:S(2)}) collective-permute-start(f32[12,64,128]{2,1,0:T(8,128)S(1)} %pad_maximum_fusion.1), channel_id=1, source_target_pairs={{1,0},{2,1},{3,2},{4,3},{5,4},{6,5},{7,6},{8,7},{9,8},{10,9},{11,1... | collective-permute-start | bytes 1179656 | tf_op jit(solution)/shard_map/ppermute | solution.py:637
  13.5 1.9 %collective-permute-start.1 = (f32[4,64,128]{2,1,0:T(8,128)S(1)}, f32[4,64,128]{2,1,0:T(8,128)S(1)}, u32[]{:S(2)}, u32[]{:S(2)}) collective-permute-start(f32[4,64,128]{2,1,0:T(8,128)S(1)} %pad_maximum_fusion.3), channel_id=1, source_target_pairs={{1,0},{2,1},{3,2},{4,3},{5,4},{6,5},{7,6},{8,7},{9,8},{10,9},{11,1... | collective-permute-start | bytes 393224 | tf_op jit(solution)/shard_map/ppermute | solution.py:634
  15.4 6.1 %collective-permute-done.1.above_ref = f32[4,64,128]{2,1,0:T(8,128)S(1)} collective-permute-done((f32[4,64,128]{2,1,0:T(8,128)S(1)}, f32[4,64,128]{2,1,0:T(8,128)S(1)}, u32[]{:S(2)}, u32[]{:S(2)}) %collective-permute-start.1) | collective-permute-done | bytes 131104 | tf_op jit(solution)/shard_map/ppermute | solution.py:634
  21.6 4.2 %shard_map.59 = f32[512,128]{1,0:T(8,128)} custom-call(f32[3,8,64,128]{3,2,1,0:T(8,128)S(1)} %copy-done, s32[8,64,128]{2,1,0:T(8,128)S(1)} %copy-done.1, f32[5,64,128]{2,1,0:T(8,128)S(1)} %collective-permute-done.below_ref, f32[4,64,128]{2,1,0:T(8,128)S(1)} %collective-permute-done.1.above_ref, s32[64,128]{1,0:T(8,128)S(1)} %copy-done.14, f32[4]{0:T(128)S(1)} %copy-done.16), custom_call_target="tpu_custom_call" | custom-call | tf_op jit(solution)/shard_map/pallas_call | solution.py:606
  26.5 13.3 %all-to-all-start = ((f32[128,4,128]{2,1,0:T(4,128)}), f32[128,4,128]{2,1,0:T(4,128)S(1)}, u32[]{:S(2)}, u32[]{:S(2)}) async-start(f32[128,4,128]{2,1,0:T(4,128)} %bitcast.2), calls=%async_computation | async-start | bytes 524288 | tf_op jit(solution)/shard_map/all_to_all | solution.py:618
  41.3 0.9 copy-done.5
  42.2 0.9 copy-done.7
  43.1 1.0 copy-done.9
  44.1 1.0 copy-done.11
  45.9 1.0 shard_map.60
  46.9 0.8 copy-done.2
  48.4 2.5 %all-to-all-done = f32[128,4,128]{2,1,0:T(4,128)S(1)} async-done(((f32[128,4,128]{2,1,0:T(4,128)}), f32[128,4,128]{2,1,0:T(4,128)S(1)}, u32[]{:S(2)}, u32[]{:S(2)}) %all-to-all-start) | async-done | bytes 262176 | tf_op jit(solution)/shard_map/all_to_all | solution.py:618
  50.9 1.1 %copy-done.3 = f32[17,64,128]{2,1,0:T(8,128)S(1)} copy-done((f32[17,64,128]{2,1,0:T(8,128)S(1)}, f32[17,64,128]{2,1,0:T(8,128)}, u32[]{:S(2)}) %copy-start.3) | copy-done | bytes 557080
  52.7 11.7 %shard_map.61 = (f32[3,17,64,128]{3,2,1,0:T(8,128)S(1)}, f32[3,17,64,128]{3,2,1,0:T(8,128)S(1)}, f32[16,128]{1,0:T(8,128)S(1)}, f32[512,128]{1,0:T(8,128)S(1)}) custom-call(f32[512,128]{1,0:T(8,128)S(1)} %bitcast.18, f32[3,17,64,128]{3,2,1,0:T(8,128)S(1)} %get-tuple-element.18.rhs_ref, f32[17,64,128]{2,1,0:T(8,128)S(1)} %get-tuple-element.19.moduli_ref, ...), custom_call_target="tpu_custom_call" | custom-call | tf_op jit(solution)/shard_map/pallas_call | solution.py:606
  64.4 18.1 %all_to_all.15 = f32[128,4,128]{2,1,0:T(4,128)S(1)} all-to-all(f32[128,4,128]{2,1,0:T(4,128)S(1)} %bitcast.21), channel_id=1, replica_groups=mesh['grp'=4,'gz'=32] {'grp','gz'}, dimensions={0} | all-to-all | bytes 524288 | tf_op jit(solution)/shard_map/all_to_all | solution.py:618
  82.5 7.1 %shard_map.62 = (f32[3,8,64,128]{3,2,1,0:T(8,128)S(1)}, f32[3,8,64,128]{3,2,1,0:T(8,128)S(1)}, f32[8,128]{1,0:T(8,128)S(1)}, f32[128,128]{1,0:T(8,128)S(1)}) custom-call(f32[512,128]{1,0:T(8,128)S(1)} %bitcast.19, f32[3,17,64,128]{3,2,1,0:T(8,128)S(1)} %get-tuple-element.18.rhs_ref, f32[17,64,128]{2,1,0:T(8,128)S(1)} %get-tuple-element.19.moduli_ref, ...), custom_call_target="tpu_custom_call" | custom-call | tf_op jit(solution)/shard_map/pallas_call | solution.py:606
  89.6 13.7 %all_to_all.16 = f32[128,1,128]{2,1,0:T(1,128)S(1)} all-to-all(f32[128,1,128]{2,1,0:T(1,128)S(1)} %bitcast.22), channel_id=1, replica_groups=mesh['grp'=4,'gz'=32] {'grp','gz'}, dimensions={0} | all-to-all | bytes 131072 | tf_op jit(solution)/shard_map/all_to_all | solution.py:618
  103.4 1.7 %shard_map.63 = (f32[3,8,64,128]{3,2,1,0:T(8,128)}, f32[3,8,64,128]{3,2,1,0:T(8,128)}) custom-call(f32[128,128]{1,0:T(8,128)S(1)} %bitcast.20, f32[8,128]{1,0:T(8,128)S(1)} %get-tuple-element.27.scalars_ref, f32[3,17,64,128]{3,2,1,0:T(8,128)S(1)} %get-tuple-element.18.rhs_ref, f32[3,17,64,128]{3,2,1,0:T(8,128)S(1)} %get-tuple-element.23.ahead_ref, ...), custom_call_target="tpu_custom_call" | custom-call | tf_op jit(solution)/shard_map/pallas_call | solution.py:606
  (36 shorter events, 4.5 us)
Async XLA Ops:
  0.6 8.3 %copy-start = (f32[3,8,64,128]{3,2,1,0:T(8,128)S(1)}, f32[3,8,64,128]{3,2,1,0:T(8,128)}, u32[]{:S(2)}) copy-start(f32[3,8,64,128]{3,2,1,0:T(8,128)} %load_ref.3) | copy-start | bytes 2359300
  2.5 19.0 %collective-permute-start = (f32[5,64,128]{2,1,0:T(8,128)S(1)}, f32[5,64,128]{2,1,0:T(8,128)S(1)}, u32[]{:S(2)}, u32[]{:S(2)}) collective-permute-start(f32[5,64,128]{2,1,0:T(8,128)S(1)} %pad_maximum_fusion.2), channel_id=1, source_target_pairs={{0,1},{1,2},{2,3},{3,4},{4,5},{5,6},{6,7},{7,8},{8,9},{9,10},{10,1... | collective-permute-start | bytes 491528 | tf_op jit(solution)/shard_map/ppermute | solution.py:633
  7.9 13.6 %copy-start.1 = (s32[8,64,128]{2,1,0:T(8,128)S(1)}, s32[8,64,128]{2,1,0:T(8,128)}, u32[]{:S(2)}) copy-start(s32[8,64,128]{2,1,0:T(8,128)} %phases_ref.3) | copy-start | bytes 786436
  7.9 13.6 %copy-start.14 = (s32[64,128]{1,0:T(8,128)S(1)}, s32[64,128]{1,0:T(8,128)}, u32[]{:S(2)}) copy-start(s32[64,128]{1,0:T(8,128)} %clamp_ref.3) | copy-start | bytes 98308
  7.9 13.6 %copy-start.16 = (f32[4]{0:T(128)S(1)}, f32[4]{0:T(128)}, u32[]{:S(2)}) copy-start(f32[4]{0:T(128)} %table_ref.3) | copy-start | bytes 52
  9.1 30.7 %collective-permute-start.2 = (f32[12,64,128]{2,1,0:T(8,128)S(1)}, f32[12,64,128]{2,1,0:T(8,128)S(1)}, u32[]{:S(2)}, u32[]{:S(2)}) collective-permute-start(f32[12,64,128]{2,1,0:T(8,128)S(1)} %pad_maximum_fusion), channel_id=1, source_target_pairs={{0,1},{1,2},{2,3},{3,4},{4,5},{5,6},{6,7},{7,8},{8,9},{9,10},{10,1... | collective-permute-start | bytes 1179656 | tf_op jit(solution)/shard_map/ppermute | solution.py:636
  11.0 29.5 %collective-permute-start.3 = (f32[12,64,128]{2,1,0:T(8,128)S(1)}, f32[12,64,128]{2,1,0:T(8,128)S(1)}, u32[]{:S(2)}, u32[]{:S(2)}) collective-permute-start(f32[12,64,128]{2,1,0:T(8,128)S(1)} %pad_maximum_fusion.1), channel_id=1, source_target_pairs={{1,0},{2,1},{3,2},{4,3},{5,4},{6,5},{7,6},{8,7},{9,8},{10,9},{11,1... | collective-permute-start | bytes 1179656 | tf_op jit(solution)/shard_map/ppermute | solution.py:637
  13.5 8.1 %collective-permute-start.1 = (f32[4,64,128]{2,1,0:T(8,128)S(1)}, f32[4,64,128]{2,1,0:T(8,128)S(1)}, u32[]{:S(2)}, u32[]{:S(2)}) collective-permute-start(f32[4,64,128]{2,1,0:T(8,128)S(1)} %pad_maximum_fusion.3), channel_id=1, source_target_pairs={{1,0},{2,1},{3,2},{4,3},{5,4},{6,5},{7,6},{8,7},{9,8},{10,9},{11,1... | collective-permute-start | bytes 393224 | tf_op jit(solution)/shard_map/ppermute | solution.py:634
  21.5 4.3 %copy-start.6 = (f32[4,64,128]{2,1,0:T(8,128)}, f32[4,64,128]{2,1,0:T(8,128)S(1)}, u32[]{:S(2)}) copy-start(f32[4,64,128]{2,1,0:T(8,128)S(1)} %collective-permute-done.1.above_ref) | copy-start | bytes 393220
  25.8 0.7 copy-start.4
  26.5 24.4 %all-to-all-start = ((f32[128,4,128]{2,1,0:T(4,128)}), f32[128,4,128]{2,1,0:T(4,128)S(1)}, u32[]{:S(2)}, u32[]{:S(2)}) async-start(f32[128,4,128]{2,1,0:T(4,128)} %bitcast.2), calls=%async_computation | async-start | bytes 524288 | tf_op jit(solution)/shard_map/all_to_all | solution.py:618
  39.8 0.7 copy-start.8
  40.6 0.7 copy-start.10
  41.3 0.9 copy-start.5
  42.2 0.9 copy-start.7
  43.1 1.0 copy-start.9
  44.1 1.0 copy-start.11
  45.1 0.8 copy-start.15
  46.9 0.8 copy-start.2
  47.7 0.6 copy-start.12
  50.9 1.1 %copy-start.3 = (f32[17,64,128]{2,1,0:T(8,128)S(1)}, f32[17,64,128]{2,1,0:T(8,128)}, u32[]{:S(2)}) copy-start(f32[17,64,128]{2,1,0:T(8,128)} %copy-done.2) | copy-start | bytes 1671172
  51.9 0.8 copy-start.13

commit v3 on v2

--- a/solution.py
+++ b/solution.py
@@ -351,23 +351,50 @@
     return correction
 
 
-def set_up(low, high, load_ref, phases_ref, below_refs, above_refs, table_ref, keep_ref,
-           rhs_ref, moduli_ref, inverse_ref, tile):
+def pack_kernel(load_ref, phases_ref, table_ref,
+                top_ref, low_ref, far_top_ref, far_low_ref, moduli_ref):
+    tile = tile_index()
     row = lax.broadcasted_iota(jnp.int32, (64, 128), 0)
     lane = lax.broadcasted_iota(jnp.int32, (64, 128), 1)
     interior = (row < 63) & (lane < 127)
     table = [table_ref[i] for i in range(4)]
-
-    def label(n):
+    for n in range(8):
+        value = jnp.zeros((64, 128), jnp.float32)
+        for i in range(4):
+            value = jnp.where(phases_ref[n] == i, table[i], value)
+        inside = interior if n < 7 else interior & (tile < 127)
+        value = jnp.where(inside, value, 0.0)
+        moduli_ref[n] = value
+        if n >= 6:
+            top_ref[3 + n - 6] = value
+        elif n >= 3:
+            far_top_ref[9 + n - 3] = value
+        if n == 0:
+            low_ref[3] = value
+        elif n < 4:
+            far_low_ref[9 + n - 1] = value
+        if n == 1:
+            low_ref[4] = value
+    for k in range(3):
+        top_ref[k] = load_ref[k, 7]
+        low_ref[k] = load_ref[k, 0]
+        for n in range(3):
+            far_top_ref[3 * k + n] = load_ref[k, 4 + n]
+            far_low_ref[3 * k + n] = load_ref[k, 1 + n]
+
+
+def set_up(low, high, load_ref, own_ref, below_refs, above_refs, keep_ref,
+           rhs_ref, moduli_ref, inverse_ref, tile):
+    def moduli(n):
         if n < -2:
-            return below_refs[1][9 + n + 5].astype(jnp.int32)
+            return below_refs[1][9 + n + 5]
         if n < 0:
-            return below_refs[0][3 + n + 2].astype(jnp.int32)
+            return below_refs[0][3 + n + 2]
         if n < 8:
-            return phases_ref[n]
+            return own_ref[n]
         if n < 9:
-            return above_refs[0][3].astype(jnp.int32)
-        return above_refs[1][9 + n - 9].astype(jnp.int32)
+            return above_refs[0][3]
+        return above_refs[1][9 + n - 9]
 
     def load(k, n):
         if n < -1:
@@ -383,12 +410,7 @@
     before = None
     for n in range(low - 1, high):
         depth = tile * 8 + n
-        inside = interior & ((depth >= 0) & (depth < 1023))
-        labels = label(n)
-        value = jnp.zeros((64, 128), jnp.float32)
-        for i in range(4):
-            value = jnp.where(labels == i, table[i], value)
-        value = jnp.where(inside, value, 0.0)
+        value = moduli(n)
         moduli_ref[n + H] = value
         if n >= low:
             both = before + value
@@ -405,13 +427,13 @@
         before = value
 
 
-def first_kernel(load_ref, phases_ref, below_ref, above_ref, clamp_ref, table_ref,
+def first_kernel(load_ref, own_ref, below_ref, above_ref, clamp_ref,
                  send_ref,
                  rhs_ref, moduli_ref, inverse_ref, keep_ref,
                  along_ref, up_ref, x_ref, late_ref, sum_ref):
     tile = tile_index()
     keep_ref[...] = 1.0 - clamp_ref[...].astype(jnp.float32)
-    set_up(-1, 9, load_ref, phases_ref, (below_ref,), (above_ref,), table_ref, keep_ref,
+    set_up(-1, 9, load_ref, own_ref, (below_ref,), (above_ref,), keep_ref,
            rhs_ref, moduli_ref, inverse_ref, tile)
     free = free_of(keep_ref, tile)
     total = moduli_ref[H]
@@ -440,19 +462,16 @@
     send_rows(send_ref, four)
 
 
-def ready_kernel(load_ref, phases_ref, below_ref, above_ref, far_below_ref, far_above_ref,
-                 clamp_ref, table_ref,
-                 rhs_ref, moduli_ref, inverse_ref, keep_ref):
+def middle_kernel(gathered_ref, load_ref, own_ref, below_ref, above_ref,
+                  far_below_ref, far_above_ref, clamp_ref,
+                  ahead_ref, image_ref, coarse_ref, send_ref,
+                  rhs_ref, moduli_ref, inverse_ref, keep_ref,
+                  along_ref, up_ref, x_ref, late_ref,
+                  sum_ref, dots_ref, window_ref, solved_ref, spread_ref):
+    tile = tile_index()
     keep_ref[...] = 1.0 - clamp_ref[...].astype(jnp.float32)
-    set_up(-4, 12, load_ref, phases_ref, (below_ref, far_below_ref),
-           (above_ref, far_above_ref), table_ref, keep_ref,
-           rhs_ref, moduli_ref, inverse_ref, tile_index())
-
-
-def middle_kernel(gathered_ref, rhs_ref, moduli_ref, inverse_ref, keep_ref,
-                  ahead_ref, image_ref, coarse_ref, send_ref,
-                  along_ref, up_ref, x_ref, late_ref, sum_ref, dots_ref, window_ref, solved_ref, spread_ref):
-    tile = tile_index()
+    set_up(-4, 12, load_ref, own_ref, (below_ref, far_below_ref),
+           (above_ref, far_above_ref), keep_ref, rhs_ref, moduli_ref, inverse_ref, tile)
     free = free_of(keep_ref, tile)
     coarse_ref[...] = coarse_solve(gathered_ref, None, tile, window_ref, solved_ref, spread_ref)
     correction = correction_of(spread_ref)
@@ -624,38 +643,29 @@
     up = [(i, i + 1) for i in range(size - 1)]
     down = [(i + 1, i) for i in range(size - 1)]
 
-    def pack(load, phases, first, last, first_phase, last_phase=None):
-        nodes = load[:, first:last].reshape(3 * (last - first), 64, 128)
-        labels = phases[first_phase : last_phase or last].astype(jnp.float32)
-        return jnp.concatenate([nodes, labels], 0)
-
-    near_top, near_low = pack(load, phases, 7, 8, 6), pack(load, phases, 0, 1, 0)
-    below = lax.ppermute(near_top, BOTH, up)
-    above = lax.ppermute(near_low, BOTH, down)
-    far_load, far_phases, unused = lax.optimization_barrier((load, phases, (near_top, near_low)))
-    far_below = lax.ppermute(pack(far_load, far_phases, 4, 7, 3, 6), BOTH, up)
-    far_above = lax.ppermute(pack(far_load, far_phases, 1, 4, 1), BOTH, down)
-
     plane = (64, 128)
     field = (3, EXT) + plane
     ready = [field, (EXT,) + plane, (EXT,) + plane, plane]
     work = [(12,) + plane, (12,) + plane, (6,) + plane, (6,) + plane]
+    top, low, far_top, far_low, moduli_own = call(
+        pack_kernel,
+        [(5,) + plane, (5,) + plane, (12,) + plane, (12,) + plane, (8,) + plane], [],
+        load, phases, phase_moduli, smem=(2,),
+    )
+    below = lax.ppermute(top, BOTH, up)
+    above = lax.ppermute(low, BOTH, down)
+    far_below = lax.ppermute(far_top, BOTH, up)
+    far_above = lax.ppermute(far_low, BOTH, down)
     (send,) = call(
-        first_kernel,
-        [(512, 128)],
-        ready + work + [(4,) + plane],
-        load, phases, below, above, clamp, phase_moduli, smem=(5,),
+        first_kernel, [(512, 128)], ready + work + [(4,) + plane],
+        load, moduli_own, below, above, clamp,
     )
     gathered = to_all(send)
-    rhs, moduli, inverse, keep = call(
-        ready_kernel, ready, [],
-        load, phases, below, above, far_below, far_above, clamp, phase_moduli, smem=(7,),
-    )
-    ahead, image, coarse, send = call(
+    ahead, image, coarse, send, rhs, moduli, inverse, keep = call(
         middle_kernel,
-        [field, field, (WINDOW, 128), (512, 128)],
+        [field, field, (WINDOW, 128), (512, 128)] + ready,
         work + [(3,) + plane, (2, 3, 8, 128), (4 * WINDOW, 128), (3 * WINDOW, 128), (72, 128)],
-        gathered, rhs, moduli, inverse, keep,
+        gathered, load, moduli_own, below, above, far_below, far_above, clamp,
     )
     gathered = to_all(send)
     own = (3, 8) + plane

time: 106 us -> 95.7 us (0.903)
  local copies, waits for them, and re-layouts: 11 us -> 3.49 us
  blocking collectives: 31.8 us -> 28.9 us
  other arithmetic: 2.79 us -> 0 us
  waiting for transfers between devices: 8.68 us -> 11.1 us
  starting transfers between devices: 24.2 us -> 26 us
    all_to_all x1, waiting for transfers between devices: 2.54 us -> 11.1 us  [to_all(): parts = lax.all_to_all(block.reshape(128, count, 128), BOTH, 0, 0)]
    unnamed x34 -> x12, local copies, waits for them, and re-layouts: 9.97 us -> 3.49 us
    ppermute x4, waiting for transfers between devices: 6.15 us -> 0.01 us  [the longest x1 0.01 us: body(): below = lax.ppermute(top, BOTH, up)]
    all_to_all x2, blocking collectives: 31.8 us -> 28.9 us  [to_all(): parts = lax.all_to_all(block.reshape(128, count, 128), BOTH, 0, 0)]
    convert_element_type x3 -> x0, other arithmetic: 2.71 us -> none  [pack(): labels = phases[first_phase:last_phase or last].astype(jnp.float32)]
    ppermute x4, starting transfers between devices: 10.9 us -> 12.1 us  [the longest x1 4.59 us: body(): below = lax.ppermute(top, BOTH, up)]
  transfers between devices with their start and end apart: 5 -> 5, of which waited for: 2 -> 1; matrix products, arithmetic and copies ran while one was open for 2% -> 0% of each run, Pallas kernels for 5% -> 4%
where the time goes in v3:
time: 95.7 us; the launch traced here: 95.3 us
  blocking collectives  28.9 us (30%)
  starting transfers between devices  26 us (27%)
  Pallas kernels  25.1 us (26%)
  waiting for transfers between devices  11.1 us (12%)
  local copies, waits for them, and re-layouts  3.49 us (4%)
    all_to_all x2, blocking collectives, to_all(): parts = lax.all_to_all(block.reshape(128, count, 128), BOTH, 0, 0)  28.9 us
    pallas_call x5, Pallas kernels, call(): pl.pallas_call(kernel, out_shape=[jax.ShapeDtypeStruct(s, jnp.float32) fo...  25.1 us
    all_to_all x1, starting transfers between devices, to_all(): parts = lax.all_to_all(block.reshape(128, count, 128), BOTH, 0, 0)  13.9 us
    all_to_all x1, waiting for transfers between devices, to_all(): parts = lax.all_to_all(block.reshape(128, count, 128), BOTH, 0, 0)  11.1 us
    ppermute x1, starting transfers between devices, body(): below = lax.ppermute(top, BOTH, up)  4.59 us
    ppermute x1, starting transfers between devices, body(): far_below = lax.ppermute(far_top, BOTH, up)  3.64 us
    unnamed x12, local copies, waits for them, and re-layouts  3.49 us
    ppermute x1, starting transfers between devices, body(): above = lax.ppermute(low, BOTH, down)  1.92 us
  transfers between devices with their start and end apart: 5, of which 1 were waited for; matrix products, arithmetic and copies ran while one was open for 0% of the time, Pallas kernels for 4%

profile of v3, /device:TPU:1, one launch (start us, length us, event | category | flops | bytes accessed | tf_op | source)
XLA Modules:
  0.0 95.3 jit_solution(1604121107032799060)
XLA Ops:
  0.6 0.0 copy-start
  0.6 1.1 %copy-done = f32[3,8,64,128]{3,2,1,0:T(8,128)S(1)} copy-done((f32[3,8,64,128]{3,2,1,0:T(8,128)S(1)}, f32[3,8,64,128]{3,2,1,0:T(8,128)}, u32[]{:S(2)}) %copy-start) | copy-done | bytes 786456
  1.8 0.9 copy-done.2
  2.7 0.7 copy-done.5
  3.4 0.6 shard_map.59
  4.0 4.6 %collective-permute-start = (f32[5,64,128]{2,1,0:T(8,128)S(1)}, f32[5,64,128]{2,1,0:T(8,128)S(1)}, u32[]{:S(2)}, u32[]{:S(2)}) collective-permute-start(f32[5,64,128]{2,1,0:T(8,128)S(1)} %get-tuple-element.20), channel_id=1, source_target_pairs={{0,1},{1,2},{2,3},{3,4},{4,5},{5,6},{6,7},{7,8},{8,9},{9,10},{10,1... | collective-permute-start | bytes 491528 | tf_op jit(solution)/shard_map/ppermute | solution.py:655
  8.6 1.9 %collective-permute-start.1 = (f32[5,64,128]{2,1,0:T(8,128)S(1)}, f32[5,64,128]{2,1,0:T(8,128)S(1)}, u32[]{:S(2)}, u32[]{:S(2)}) collective-permute-start(f32[5,64,128]{2,1,0:T(8,128)S(1)} %get-tuple-element.21), channel_id=1, source_target_pairs={{1,0},{2,1},{3,2},{4,3},{5,4},{6,5},{7,6},{8,7},{9,8},{10,9},{11,1... | collective-permute-start | bytes 491528 | tf_op jit(solution)/shard_map/ppermute | solution.py:656
  10.6 3.6 %collective-permute-start.2 = (f32[12,64,128]{2,1,0:T(8,128)S(1)}, f32[12,64,128]{2,1,0:T(8,128)S(1)}, u32[]{:S(2)}, u32[]{:S(2)}) collective-permute-start(f32[12,64,128]{2,1,0:T(8,128)S(1)} %get-tuple-element.22), channel_id=1, source_target_pairs={{0,1},{1,2},{2,3},{3,4},{4,5},{5,6},{6,7},{7,8},{8,9},{9,10},{10,1... | collective-permute-start | bytes 1179656 | tf_op jit(solution)/shard_map/ppermute | solution.py:657
  14.2 1.9 %collective-permute-start.3 = (f32[12,64,128]{2,1,0:T(8,128)S(1)}, f32[12,64,128]{2,1,0:T(8,128)S(1)}, u32[]{:S(2)}, u32[]{:S(2)}) collective-permute-start(f32[12,64,128]{2,1,0:T(8,128)S(1)} %get-tuple-element.23), channel_id=1, source_target_pairs={{1,0},{2,1},{3,2},{4,3},{5,4},{6,5},{7,6},{8,7},{9,8},{10,9},{11,1... | collective-permute-start | bytes 1179656 | tf_op jit(solution)/shard_map/ppermute | solution.py:658
  16.1 0.0 collective-permute-done.below_ref
  16.1 0.0 collective-permute-done.1.above_ref
  16.2 0.0 copy-start.3
  16.2 0.7 copy-done.3
  16.9 3.6 %shard_map.60 = f32[512,128]{1,0:T(8,128)} custom-call(f32[3,8,64,128]{3,2,1,0:T(8,128)S(1)} %copy-done, f32[8,64,128]{2,1,0:T(8,128)S(1)} %get-tuple-element.19.own_ref, f32[5,64,128]{2,1,0:T(8,128)S(1)} %collective-permute-done.below_ref, f32[5,64,128]{2,1,0:T(8,128)S(1)} %collective-permute-done.1.above_ref, s32[64,128]{1,0:T(8,128)S(1)} %copy-done.3), custom_call_target="tpu_custom_call" | custom-call | tf_op jit(solution)/shard_map/pallas_call | solution.py:625
  20.5 13.9 %all-to-all-start = ((f32[128,4,128]{2,1,0:T(4,128)}), f32[128,4,128]{2,1,0:T(4,128)S(1)}, u32[]{:S(2)}, u32[]{:S(2)}) async-start(f32[128,4,128]{2,1,0:T(4,128)} %bitcast), calls=%async_computation | async-start | bytes 524288 | tf_op jit(solution)/shard_map/all_to_all | solution.py:637
  34.4 0.0 collective-permute-done.2.far_below_ref
  34.4 0.0 collective-permute-done.3.far_above_ref
  34.4 11.1 %all-to-all-done = f32[128,4,128]{2,1,0:T(4,128)S(1)} async-done(((f32[128,4,128]{2,1,0:T(4,128)}), f32[128,4,128]{2,1,0:T(4,128)S(1)}, u32[]{:S(2)}, u32[]{:S(2)}) %all-to-all-start) | async-done | bytes 262176 | tf_op jit(solution)/shard_map/all_to_all | solution.py:637
  45.5 0.0 copy-done.1
  45.5 12.0 %shard_map.61 = (f32[3,17,64,128]{3,2,1,0:T(8,128)S(1)}, f32[3,17,64,128]{3,2,1,0:T(8,128)S(1)}, f32[16,128]{1,0:T(8,128)S(1)}, f32[512,128]{1,0:T(8,128)S(1)}, ...) custom-call(f32[512,128]{1,0:T(8,128)S(1)} %bitcast.8, ...), custom_call_target="tpu_custom_call" | custom-call | tf_op jit(solution)/shard_map/pallas_call | solution.py:625
  57.5 15.2 %all_to_all.15 = f32[128,4,128]{2,1,0:T(4,128)S(1)} all-to-all(f32[128,4,128]{2,1,0:T(4,128)S(1)} %bitcast.11), channel_id=1, replica_groups=mesh['grp'=4,'gz'=32] {'grp','gz'}, dimensions={0} | all-to-all | bytes 524288 | tf_op jit(solution)/shard_map/all_to_all | solution.py:637
  72.7 7.2 %shard_map.62 = (f32[3,8,64,128]{3,2,1,0:T(8,128)S(1)}, f32[3,8,64,128]{3,2,1,0:T(8,128)S(1)}, f32[8,128]{1,0:T(8,128)S(1)}, f32[128,128]{1,0:T(8,128)S(1)}) custom-call(f32[512,128]{1,0:T(8,128)S(1)} %bitcast.9, f32[3,17,64,128]{3,2,1,0:T(8,128)S(1)} %get-tuple-element.25.rhs_ref, f32[17,64,128]{2,1,0:T(8,128)S(1)} %get-tuple-element.26.moduli_ref, ...), custom_call_target="tpu_custom_call" | custom-call | tf_op jit(solution)/shard_map/pallas_call | solution.py:625
  79.9 13.7 %all_to_all.16 = f32[128,1,128]{2,1,0:T(1,128)S(1)} all-to-all(f32[128,1,128]{2,1,0:T(1,128)S(1)} %bitcast.12), channel_id=1, replica_groups=mesh['grp'=4,'gz'=32] {'grp','gz'}, dimensions={0} | all-to-all | bytes 131072 | tf_op jit(solution)/shard_map/all_to_all | solution.py:637
  93.6 1.7 %shard_map.63 = (f32[3,8,64,128]{3,2,1,0:T(8,128)}, f32[3,8,64,128]{3,2,1,0:T(8,128)}) custom-call(f32[128,128]{1,0:T(8,128)S(1)} %bitcast.10, f32[8,128]{1,0:T(8,128)S(1)} %get-tuple-element.33.scalars_ref, f32[3,17,64,128]{3,2,1,0:T(8,128)S(1)} %get-tuple-element.25.rhs_ref, f32[3,17,64,128]{3,2,1,0:T(8,128)S(1)} %get-tuple-element.29.ahead_ref, ...), custom_call_target="tpu_custom_call" | custom-call | tf_op jit(solution)/shard_map/pallas_call | solution.py:625
  (5 shorter events, 0.0 us)
Async XLA Ops:
  0.6 1.1 %copy-start = (f32[3,8,64,128]{3,2,1,0:T(8,128)S(1)}, f32[3,8,64,128]{3,2,1,0:T(8,128)}, u32[]{:S(2)}) copy-start(f32[3,8,64,128]{3,2,1,0:T(8,128)} %load_ref.5) | copy-start | bytes 2359300
  1.8 0.9 copy-start.2
  2.7 0.7 copy-start.5
  3.4 42.1 %copy-start.1 = (f32[3,8,64,128]{3,2,1,0:T(8,128)S(1)}, f32[3,8,64,128]{3,2,1,0:T(8,128)}, u32[]{:S(2)}) copy-start(f32[3,8,64,128]{3,2,1,0:T(8,128)} %load_ref.5) | copy-start | bytes 2359300
  3.4 42.1 %copy-start.4 = (s32[64,128]{1,0:T(8,128)S(1)}, s32[64,128]{1,0:T(8,128)}, u32[]{:S(2)}) copy-start(s32[64,128]{1,0:T(8,128)} %clamp_ref.3) | copy-start | bytes 98308
  4.0 12.1 %collective-permute-start = (f32[5,64,128]{2,1,0:T(8,128)S(1)}, f32[5,64,128]{2,1,0:T(8,128)S(1)}, u32[]{:S(2)}, u32[]{:S(2)}) collective-permute-start(f32[5,64,128]{2,1,0:T(8,128)S(1)} %get-tuple-element.20), channel_id=1, source_target_pairs={{0,1},{1,2},{2,3},{3,4},{4,5},{5,6},{6,7},{7,8},{8,9},{9,10},{10,1... | collective-permute-start | bytes 491528 | tf_op jit(solution)/shard_map/ppermute | solution.py:655
  8.6 7.5 %collective-permute-start.1 = (f32[5,64,128]{2,1,0:T(8,128)S(1)}, f32[5,64,128]{2,1,0:T(8,128)S(1)}, u32[]{:S(2)}, u32[]{:S(2)}) collective-permute-start(f32[5,64,128]{2,1,0:T(8,128)S(1)} %get-tuple-element.21), channel_id=1, source_target_pairs={{1,0},{2,1},{3,2},{4,3},{5,4},{6,5},{7,6},{8,7},{9,8},{10,9},{11,1... | collective-permute-start | bytes 491528 | tf_op jit(solution)/shard_map/ppermute | solution.py:656
  10.6 23.9 %collective-permute-start.2 = (f32[12,64,128]{2,1,0:T(8,128)S(1)}, f32[12,64,128]{2,1,0:T(8,128)S(1)}, u32[]{:S(2)}, u32[]{:S(2)}) collective-permute-start(f32[12,64,128]{2,1,0:T(8,128)S(1)} %get-tuple-element.22), channel_id=1, source_target_pairs={{0,1},{1,2},{2,3},{3,4},{4,5},{5,6},{6,7},{7,8},{8,9},{9,10},{10,1... | collective-permute-start | bytes 1179656 | tf_op jit(solution)/shard_map/ppermute | solution.py:657
  14.2 20.2 %collective-permute-start.3 = (f32[12,64,128]{2,1,0:T(8,128)S(1)}, f32[12,64,128]{2,1,0:T(8,128)S(1)}, u32[]{:S(2)}, u32[]{:S(2)}) collective-permute-start(f32[12,64,128]{2,1,0:T(8,128)S(1)} %get-tuple-element.23), channel_id=1, source_target_pairs={{1,0},{2,1},{3,2},{4,3},{5,4},{6,5},{7,6},{8,7},{9,8},{10,9},{11,1... | collective-permute-start | bytes 1179656 | tf_op jit(solution)/shard_map/ppermute | solution.py:658
  16.2 0.8 copy-start.3
  20.5 25.0 %all-to-all-start = ((f32[128,4,128]{2,1,0:T(4,128)}), f32[128,4,128]{2,1,0:T(4,128)S(1)}, u32[]{:S(2)}, u32[]{:S(2)}) async-start(f32[128,4,128]{2,1,0:T(4,128)} %bitcast), calls=%async_computation | async-start | bytes 524288 | tf_op jit(solution)/shard_map/all_to_all | solution.py:637

commit v4 on v3

--- a/solution.py
+++ b/solution.py
@@ -351,61 +351,90 @@
     return correction
 
 
-def pack_kernel(load_ref, phases_ref, table_ref,
-                top_ref, low_ref, far_top_ref, far_low_ref, moduli_ref):
+def pack_kernel(load_hbm, phases_hbm, table_ref,
+                chip_ref, link_ref, moduli_ref,
+                load_ref, phases_ref, arrived):
+    fetch_phases = pltpu.make_async_copy(phases_hbm, phases_ref, arrived.at[0])
+    fetch_load = pltpu.make_async_copy(load_hbm, load_ref, arrived.at[1])
+    fetch_phases.start()
+    fetch_load.start()
     tile = tile_index()
     row = lax.broadcasted_iota(jnp.int32, (64, 128), 0)
     lane = lax.broadcasted_iota(jnp.int32, (64, 128), 1)
     interior = (row < 63) & (lane < 127)
     table = [table_ref[i] for i in range(4)]
+    fetch_phases.wait()
     for n in range(8):
         value = jnp.zeros((64, 128), jnp.float32)
         for i in range(4):
             value = jnp.where(phases_ref[n] == i, table[i], value)
         inside = interior if n < 7 else interior & (tile < 127)
-        value = jnp.where(inside, value, 0.0)
-        moduli_ref[n] = value
-        if n >= 6:
-            top_ref[3 + n - 6] = value
-        elif n >= 3:
-            far_top_ref[9 + n - 3] = value
-        if n == 0:
-            low_ref[3] = value
-        elif n < 4:
-            far_low_ref[9 + n - 1] = value
-        if n == 1:
-            low_ref[4] = value
+        moduli_ref[n] = jnp.where(inside, value, 0.0)
+    fetch_load.wait()
+
+    def fill(top_ref, low_ref):
+        for k in range(3):
+            top_ref[k] = load_ref[k, 7]
+            low_ref[k] = load_ref[k, 0]
+            for n in range(3):
+                top_ref[5 + 3 * k + n] = load_ref[k, 4 + n]
+                low_ref[5 + 3 * k + n] = load_ref[k, 1 + n]
+        for n in range(2):
+            top_ref[3 + n] = moduli_ref[6 + n]
+            low_ref[3 + n] = moduli_ref[n]
+        for n in range(3):
+            top_ref[14 + n] = moduli_ref[3 + n]
+            low_ref[14 + n] = moduli_ref[1 + n]
+
+    @pl.when((tile & 1) == 0)
+    def even():
+        fill(chip_ref, link_ref)
+
+    @pl.when((tile & 1) == 1)
+    def odd():
+        fill(link_ref, chip_ref)
+
+
+def own_kernel(load_ref, own_ref, clamp_ref, rhs_ref, moduli_ref, keep_ref):
+    keep_ref[...] = 1.0 - clamp_ref[...].astype(jnp.float32)
+    moduli_ref[...] = own_ref[...]
     for k in range(3):
-        top_ref[k] = load_ref[k, 7]
-        low_ref[k] = load_ref[k, 0]
-        for n in range(3):
-            far_top_ref[3 * k + n] = load_ref[k, 4 + n]
-            far_low_ref[3 * k + n] = load_ref[k, 1 + n]
-
-
-def set_up(low, high, load_ref, own_ref, below_refs, above_refs, keep_ref,
+        rhs_ref[k] = load_ref[k]
+        held = jnp.where(tile_index() == 0, keep_ref[...], 1.0)
+        rhs_ref[k, 0] = held * load_ref[k, 0]
+
+
+def set_up(low, high, load_ref, own_ref, chip_ref, link_ref, keep_ref,
            rhs_ref, moduli_ref, inverse_ref, tile):
+    even = (tile & 1) == 0
+
+    def below(i):
+        return jnp.where(even, link_ref[i], chip_ref[i])
+
+    def above(i):
+        return jnp.where(even, chip_ref[i], link_ref[i])
+
     def moduli(n):
         if n < -2:
-            return below_refs[1][9 + n + 5]
+            return below(14 + n + 5)
         if n < 0:
-            return below_refs[0][3 + n + 2]
+            return below(3 + n + 2)
         if n < 8:
             return own_ref[n]
         if n < 9:
-            return above_refs[0][3]
-        return above_refs[1][9 + n - 9]
+            return above(3)
+        return above(14 + n - 9)
 
     def load(k, n):
         if n < -1:
-            return below_refs[1][3 * k + n + 4]
+            return below(5 + 3 * k + n + 4)
         if n < 0:
-            return below_refs[0][k]
+            return below(k)
         if n < 8:
             return load_ref[k, n]
         if n < 9:
-            return above_refs[0][k]
-        return above_refs[1][3 * k + n - 9]
+            return above(k)
+        return above(5 + 3 * k + n - 9)
 
     before = None
     for n in range(low - 1, high):
@@ -427,13 +456,12 @@
         before = value
 
 
-def first_kernel(load_ref, own_ref, below_ref, above_ref, clamp_ref,
+def first_kernel(link_ref, chip_ref, load_ref, own_ref, keep_ref,
                  send_ref,
-                 rhs_ref, moduli_ref, inverse_ref, keep_ref,
+                 rhs_ref, moduli_ref, inverse_ref,
                  along_ref, up_ref, x_ref, late_ref, sum_ref):
     tile = tile_index()
-    keep_ref[...] = 1.0 - clamp_ref[...].astype(jnp.float32)
-    set_up(-1, 9, load_ref, own_ref, (below_ref,), (above_ref,), keep_ref,
+    set_up(-1, 9, load_ref, own_ref, chip_ref, link_ref, keep_ref,
            rhs_ref, moduli_ref, inverse_ref, tile)
     free = free_of(keep_ref, tile)
     total = moduli_ref[H]
@@ -462,16 +490,14 @@
     send_rows(send_ref, four)
 
 
-def middle_kernel(gathered_ref, load_ref, own_ref, below_ref, above_ref,
-                  far_below_ref, far_above_ref, clamp_ref,
+def middle_kernel(gathered_ref, link_ref, chip_ref, load_ref, own_ref, keep_ref,
                   ahead_ref, image_ref, coarse_ref, send_ref,
-                  rhs_ref, moduli_ref, inverse_ref, keep_ref,
+                  rhs_ref, moduli_ref, inverse_ref,
                   along_ref, up_ref, x_ref, late_ref,
                   sum_ref, dots_ref, window_ref, solved_ref, spread_ref):
     tile = tile_index()
-    keep_ref[...] = 1.0 - clamp_ref[...].astype(jnp.float32)
-    set_up(-4, 12, load_ref, own_ref, (below_ref, far_below_ref),
-           (above_ref, far_above_ref), keep_ref, rhs_ref, moduli_ref, inverse_ref, tile)
+    set_up(-4, 12, load_ref, own_ref, chip_ref, link_ref, keep_ref,
+           rhs_ref, moduli_ref, inverse_ref, tile)
     free = free_of(keep_ref, tile)
     coarse_ref[...] = coarse_solve(gathered_ref, None, tile, window_ref, solved_ref, spread_ref)
     correction = correction_of(spread_ref)
@@ -617,7 +643,7 @@
     lax.fori_loop(0, 8, step, 0)
 
 
-def call(kernel, outs, scratch, *args, smem=()):
+def call(kernel, outs, scratch, *args, smem=(), cost=None):
     spaces = [
         pl.BlockSpec(memory_space=pltpu.SMEM if i in smem else pltpu.VMEM)
         for i in range(len(args))
@@ -628,6 +654,7 @@
         in_specs=spaces,
         out_specs=[pl.BlockSpec(memory_space=pltpu.VMEM)] * len(outs),
         scratch_shapes=[pltpu.VMEM(s, jnp.float32) for s in scratch],
+        cost_estimate=cost,
         compiler_params=pltpu.CompilerParams(vmem_limit_bytes=14 * 2**20),
     )(*args)
 
@@ -640,35 +667,46 @@
 
 def body(load, phases, clamp, phase_moduli):
     size = lax.axis_size(BOTH)
-    up = [(i, i + 1) for i in range(size - 1)]
-    down = [(i + 1, i) for i in range(size - 1)]
-
+    pairs = [(i, i ^ 1) for i in range(size)]
+    links = [(i, i + (1 if i % 2 else -1)) for i in range(1, size - 1)]
     plane = (64, 128)
     field = (3, EXT) + plane
-    ready = [field, (EXT,) + plane, (EXT,) + plane, plane]
+    ready = [field, (EXT,) + plane, (EXT,) + plane]
     work = [(12,) + plane, (12,) + plane, (6,) + plane, (6,) + plane]
-    top, low, far_top, far_low, moduli_own = call(
+    halo = (17,) + plane
+    vmem = pl.BlockSpec(memory_space=pltpu.VMEM)
+    to_chip, to_link, moduli_own = pl.pallas_call(
         pack_kernel,
-        [(5,) + plane, (5,) + plane, (12,) + plane, (12,) + plane, (8,) + plane], [],
-        load, phases, phase_moduli, smem=(2,),
+        out_shape=[jax.ShapeDtypeStruct(s, jnp.float32) for s in (halo, halo, (8,) + plane)],
+        in_specs=[pl.BlockSpec(memory_space=pltpu.HBM)] * 2
+        + [pl.BlockSpec(memory_space=pltpu.SMEM)],
+        out_specs=[vmem, vmem, vmem],
+        scratch_shapes=[
+            pltpu.VMEM(load.shape, jnp.float32),
+            pltpu.VMEM(phases.shape, jnp.int32),
+            pltpu.SemaphoreType.DMA((2,)),
+        ],
+        compiler_params=pltpu.CompilerParams(vmem_limit_bytes=60 * 2**20),
+    )(load, phases, phase_moduli)
+    from_link = lax.ppermute(to_link, BOTH, links)
+    from_chip = lax.ppermute(to_chip, BOTH, pairs)
+    own = (3, 8) + plane
+    rhs_own, moduli_own, keep = call(
+        own_kernel, [own, (8,) + plane, plane], [], load, moduli_own, clamp,
+        cost=pl.CostEstimate(flops=20_000_000, bytes_accessed=20_000_000, transcendentals=0),
     )
-    below = lax.ppermute(top, BOTH, up)
-    above = lax.ppermute(low, BOTH, down)
-    far_below = lax.ppermute(far_top, BOTH, up)
-    far_above = lax.ppermute(far_low, BOTH, down)
     (send,) = call(
         first_kernel, [(512, 128)], ready + work + [(4,) + plane],
-        load, moduli_own, below, above, clamp,
+        from_link, from_chip, rhs_own, moduli_own, keep,
     )
     gathered = to_all(send)
-    ahead, image, coarse, send, rhs, moduli, inverse, keep = call(
+    ahead, image, coarse, send, rhs, moduli, inverse = call(
         middle_kernel,
         [field, field, (WINDOW, 128), (512, 128)] + ready,
         work + [(3,) + plane, (2, 3, 8, 128), (4 * WINDOW, 128), (3 * WINDOW, 128), (72, 128)],
-        gathered, load, moduli_own, below, above, far_below, far_above, clamp,
+        gathered, from_link, from_chip, rhs_own, moduli_own, keep,
     )
     gathered = to_all(send)
-    own = (3, 8) + plane
     following, following_image, scalars, send = call(
         last_kernel,
         [own, own, (8, 128), (128, 128)],

time: 95.7 us -> 93.3 us (0.975)
  blocking collectives: 28.9 us -> 53.4 us
  starting transfers between devices: 26 us -> 4.68 us
  waiting for transfers between devices: 11.1 us -> 4.4 us
  Pallas kernels: 25.1 us -> 27 us
    all_to_all x2 -> x3, blocking collectives: 28.9 us -> 53.4 us  [to_all(): parts = lax.all_to_all(block.reshape(128, count, 128), BOTH, 0, 0)]
    all_to_all x1 -> x0, starting transfers between devices: 13.9 us -> none  [to_all(): parts = lax.all_to_all(block.reshape(128, count, 128), BOTH, 0, 0)]
    all_to_all x1 -> x0, waiting for transfers between devices: 11.1 us -> none  [to_all(): parts = lax.all_to_all(block.reshape(128, count, 128), BOTH, 0, 0)]
    ppermute x4 -> x2, starting transfers between devices: 12.1 us -> 4.68 us  [the longest x1 4.6 us: body(): from_link = lax.ppermute(to_link, BOTH, links)]
    ppermute x4 -> x2, waiting for transfers between devices: 0.01 us -> 4.4 us  [the longest x1 4.4 us: body(): from_link = lax.ppermute(to_link, BOTH, links)]
    pallas_call x0 -> x1, Pallas kernels: none -> 3.03 us  [body(): pl.pallas_call(pack_kernel, out_shape=[jax.ShapeDtypeStruct(s, jnp.float3...]
    pallas_call x5, Pallas kernels: 25.1 us -> 23.9 us  [call(): pl.pallas_call(kernel, out_shape=[jax.ShapeDtypeStruct(s, jnp.float32) fo...]
    unnamed x12 -> x6, local copies, waits for them, and re-layouts: 3.49 us -> 2.84 us
  transfers between devices with their start and end apart: 5 -> 2, of which waited for: 1 -> 1; matrix products, arithmetic and copies ran while one was open for 0% -> 0% of each run, Pallas kernels for 4% -> 0%
where the time goes in v4:
time: 93.3 us; the launch traced here: 93 us
  blocking collectives  53.4 us (57%)
  Pallas kernels  27 us (29%)
  starting transfers between devices  4.68 us (5%)
  waiting for transfers between devices  4.4 us (5%)
  local copies, waits for them, and re-layouts  2.84 us (3%)
    all_to_all x3, blocking collectives, to_all(): parts = lax.all_to_all(block.reshape(128, count, 128), BOTH, 0, 0)  53.4 us
    pallas_call x5, Pallas kernels, call(): pl.pallas_call(kernel, out_shape=[jax.ShapeDtypeStruct(s, jnp.float32) fo...  23.9 us
    ppermute x1, starting transfers between devices, body(): from_link = lax.ppermute(to_link, BOTH, links)  4.6 us
    ppermute x1, waiting for transfers between devices, body(): from_link = lax.ppermute(to_link, BOTH, links)  4.4 us
    pallas_call x1, Pallas kernels, body(): pl.pallas_call(pack_kernel, out_shape=[jax.ShapeDtypeStruct(s, jnp.float3...  3.03 us
    unnamed x6, local copies, waits for them, and re-layouts  2.84 us
  transfers between devices with their start and end apart: 2, of which 1 were waited for; matrix products, arithmetic and copies ran while one was open for 0% of the time, Pallas kernels for 0%

profile of v4, /device:TPU:1, one launch (start us, length us, event | category | flops | bytes accessed | tf_op | source)
XLA Modules:
  0.0 93.0 jit_solution(9160906682449268377)
XLA Ops:
  0.6 3.0 %shard_map.59 = (f32[17,64,128]{2,1,0:T(8,128)}, f32[17,64,128]{2,1,0:T(8,128)}, f32[8,64,128]{2,1,0:T(8,128)}) custom-call(f32[3,8,64,128]{3,2,1,0:T(8,128)} %load_ref.1, s32[8,64,128]{2,1,0:T(8,128)} %phases_hbm.1, f32[4]{0:T(128)} %table_ref.1), custom_call_target="tpu_custom_call" | custom-call | tf_op jit(solution)/shard_map/pallas_call | solution.py:678
  3.7 4.6 %collective-permute-start = (f32[17,64,128]{2,1,0:T(8,128)}, f32[17,64,128]{2,1,0:T(8,128)S(1)}, u32[]{:S(2)}, u32[]{:S(2)}) collective-permute-start(f32[17,64,128]{2,1,0:T(8,128)} %get-tuple-element.19), channel_id=1, source_target_pairs={{1,2},{2,1},{3,4},{4,3},{5,6},{6,5},{7,8},{8,7},{9,10},{10,9},{11,... | collective-permute-start | bytes 1671176 | tf_op jit(solution)/shard_map/ppermute | solution.py:691
  8.3 0.1 collective-permute-start.1
  8.4 0.0 copy-start
  8.4 1.1 %copy-done = f32[3,8,64,128]{3,2,1,0:T(8,128)S(1)} copy-done((f32[3,8,64,128]{3,2,1,0:T(8,128)S(1)}, f32[3,8,64,128]{3,2,1,0:T(8,128)}, u32[]{:S(2)}) %copy-start) | copy-done | bytes 786456
  9.5 0.0 copy-start.1
  9.5 0.9 %copy-done.1 = f32[8,64,128]{2,1,0:T(8,128)S(1)} copy-done((f32[8,64,128]{2,1,0:T(8,128)S(1)}, f32[8,64,128]{2,1,0:T(8,128)}, u32[]{:S(2)}) %copy-start.1) | copy-done | bytes 262168
  10.5 0.0 copy-start.2
  10.5 0.8 copy-done.2
  11.2 0.1 shard_map.60
  11.3 4.4 %collective-permute-done.link_ref = f32[17,64,128]{2,1,0:T(8,128)S(1)} collective-permute-done((f32[17,64,128]{2,1,0:T(8,128)}, f32[17,64,128]{2,1,0:T(8,128)S(1)}, u32[]{:S(2)}, u32[]{:S(2)}) %collective-permute-start) | collective-permute-done | bytes 557088 | tf_op jit(solution)/shard_map/ppermute | solution.py:691
  15.7 0.0 collective-permute-done.1.chip_ref
  15.7 2.9 %shard_map.61 = f32[512,128]{1,0:T(8,128)S(1)} custom-call(f32[17,64,128]{2,1,0:T(8,128)S(1)} %collective-permute-done.link_ref, f32[17,64,128]{2,1,0:T(8,128)S(1)} %collective-permute-done.1.chip_ref, f32[3,8,64,128]{3,2,1,0:T(8,128)S(1)} %get-tuple-element.22.load_ref, f32[8,64,128]{2,1,0:T(8,128)S(1)} %get-tuple-element.23.own_ref, ...), custom_call_target="tpu_custom_call" | custom-call | tf_op jit(solution)/shard_map/pallas_call | solution.py:651
  18.6 24.5 %all_to_all.15 = f32[128,4,128]{2,1,0:T(4,128)S(1)} all-to-all(f32[128,4,128]{2,1,0:T(4,128)S(1)} %bitcast.10), channel_id=1, replica_groups=mesh['grp'=4,'gz'=32] {'grp','gz'}, dimensions={0} | all-to-all | bytes 524288 | tf_op jit(solution)/shard_map/all_to_all | solution.py:664
  43.1 12.1 %shard_map.62 = (f32[3,17,64,128]{3,2,1,0:T(8,128)S(1)}, f32[3,17,64,128]{3,2,1,0:T(8,128)S(1)}, f32[16,128]{1,0:T(8,128)S(1)}, f32[512,128]{1,0:T(8,128)S(1)}, ...) custom-call(f32[512,128]{1,0:T(8,128)S(1)} %bitcast.8, ...), custom_call_target="tpu_custom_call" | custom-call | tf_op jit(solution)/shard_map/pallas_call | solution.py:651
  55.2 15.2 %all_to_all.16 = f32[128,4,128]{2,1,0:T(4,128)S(1)} all-to-all(f32[128,4,128]{2,1,0:T(4,128)S(1)} %bitcast.12), channel_id=1, replica_groups=mesh['grp'=4,'gz'=32] {'grp','gz'}, dimensions={0} | all-to-all | bytes 524288 | tf_op jit(solution)/shard_map/all_to_all | solution.py:664
  70.4 7.2 %shard_map.63 = (f32[3,8,64,128]{3,2,1,0:T(8,128)S(1)}, f32[3,8,64,128]{3,2,1,0:T(8,128)S(1)}, f32[8,128]{1,0:T(8,128)S(1)}, f32[128,128]{1,0:T(8,128)S(1)}) custom-call(f32[512,128]{1,0:T(8,128)S(1)} %bitcast.9, f32[3,17,64,128]{3,2,1,0:T(8,128)S(1)} %get-tuple-element.26.rhs_ref, f32[17,64,128]{2,1,0:T(8,128)S(1)} %get-tuple-element.27.moduli_ref, ...), custom_call_target="tpu_custom_call" | custom-call | tf_op jit(solution)/shard_map/pallas_call | solution.py:651
  77.6 13.7 %all_to_all.17 = f32[128,1,128]{2,1,0:T(1,128)S(1)} all-to-all(f32[128,1,128]{2,1,0:T(1,128)S(1)} %bitcast.13), channel_id=1, replica_groups=mesh['grp'=4,'gz'=32] {'grp','gz'}, dimensions={0} | all-to-all | bytes 131072 | tf_op jit(solution)/shard_map/all_to_all | solution.py:664
  91.3 1.7 %shard_map.64 = (f32[3,8,64,128]{3,2,1,0:T(8,128)}, f32[3,8,64,128]{3,2,1,0:T(8,128)}) custom-call(f32[128,128]{1,0:T(8,128)S(1)} %bitcast.11, f32[8,128]{1,0:T(8,128)S(1)} %get-tuple-element.33.scalars_ref, f32[3,17,64,128]{3,2,1,0:T(8,128)S(1)} %get-tuple-element.26.rhs_ref, f32[3,17,64,128]{3,2,1,0:T(8,128)S(1)} %get-tuple-element.29.ahead_ref, ...), custom_call_target="tpu_custom_call" | custom-call | tf_op jit(solution)/shard_map/pallas_call | solution.py:651
Async XLA Ops:
  3.7 12.0 %collective-permute-start = (f32[17,64,128]{2,1,0:T(8,128)}, f32[17,64,128]{2,1,0:T(8,128)S(1)}, u32[]{:S(2)}, u32[]{:S(2)}) collective-permute-start(f32[17,64,128]{2,1,0:T(8,128)} %get-tuple-element.19), channel_id=1, source_target_pairs={{1,2},{2,1},{3,4},{4,3},{5,6},{6,5},{7,8},{8,7},{9,10},{10,9},{11,... | collective-permute-start | bytes 1671176 | tf_op jit(solution)/shard_map/ppermute | solution.py:691
  8.3 7.4 %collective-permute-start.1 = (f32[17,64,128]{2,1,0:T(8,128)}, f32[17,64,128]{2,1,0:T(8,128)S(1)}, u32[]{:S(2)}, u32[]{:S(2)}) collective-permute-start(f32[17,64,128]{2,1,0:T(8,128)} %get-tuple-element.20), channel_id=1, source_target_pairs={{0,1},{1,0},{2,3},{3,2},{4,5},{5,4},{6,7},{7,6},{8,9},{9,8},{10,11... | collective-permute-start | bytes 1671176 | tf_op jit(solution)/shard_map/ppermute | solution.py:692
  8.4 1.1 %copy-start = (f32[3,8,64,128]{3,2,1,0:T(8,128)S(1)}, f32[3,8,64,128]{3,2,1,0:T(8,128)}, u32[]{:S(2)}) copy-start(f32[3,8,64,128]{3,2,1,0:T(8,128)} %load_ref.1) | copy-start | bytes 2359300
  9.5 0.9 %copy-start.1 = (f32[8,64,128]{2,1,0:T(8,128)S(1)}, f32[8,64,128]{2,1,0:T(8,128)}, u32[]{:S(2)}) copy-start(f32[8,64,128]{2,1,0:T(8,128)} %get-tuple-element.21.own_ref) | copy-start | bytes 786436
  10.5 0.8 copy-start.2

commit v5 on v4

--- a/solution.py
+++ b/solution.py
@@ -217,6 +217,106 @@
         flush(high - 1, j)
 
 
+def block_forces(field, moduli_ref, along_ref, free, x_ref, total_ref):
+    row = lax.broadcasted_iota(jnp.int32, (8, 128), 0)
+    last_row = row == 7
+
+    def x_modes(n, j):
+        held = free(n, j)
+        for k, value in enumerate(field(n, j)):
+            value = value * held
+            beside = lanes(value, -1)
+            x_ref[2 * k, at(j), :] = value + beside
+            x_ref[2 * k + 1, at(j), :] = beside - value
+
+    def take(j):
+        values = [x_ref[q, at(j), :] for q in range(6)]
+        return values, [rows(v, -1) for v in values]
+
+    def planes(following):
+        here = take(0)
+        zero = jnp.zeros((8, 128), jnp.float32)
+        for j in range(8):
+            after = take(j + 1) if j < 7 else ([zero] * 6, [zero] * 6)
+            now = []
+            for value, rolled, rolled_after in zip(here[0], here[1], after[1]):
+                beside = jnp.where(last_row, rolled_after, rolled)
+                now += [value + beside, beside - value]
+            here = after
+            x_modes(following, j)
+            yield j, now
+
+    def begin(n, following):
+        for j in range(8):
+            x_modes(n, j)
+        for j, now in planes(following):
+            for q in range(12):
+                along_ref[q, at(j), :] = now[q]
+
+    def add(n, following, kind):
+        for j, now in planes(following):
+            before = [along_ref[q, at(j), :] for q in range(12)]
+            for q in range(12):
+                along_ref[q, at(j), :] = now[q]
+            weight = moduli_ref[n - 1, at(j), :]
+            value = [None] * 24
+            for k in range(3):
+                for c in range(2):
+                    for b in range(2):
+                        q = 4 * k + 2 * c + b
+                        value[3 * (2 * b + c) + k] = before[q] + now[q]
+                        value[3 * (4 + 2 * b + c) + k] = now[q] - before[q]
+            force = mode_forces(value, 1.0)
+            for k in range(3):
+                for c in range(2):
+                    for b in range(2):
+                        q = 4 * k + 2 * c + b
+                        same = force[3 * (2 * b + c) + k]
+                        change = force[3 * (4 + 2 * b + c) + k]
+                        if kind == "inner":
+                            if same is not None:
+                                total_ref[12 + q, at(j), :] += (2.0 * weight) * same
+                            continue
+                        change = weight * change
+                        same = 0.0 if same is None else weight * same
+                        if kind == "below":
+                            total_ref[q, at(j), :] = same + change
+                        elif kind == "lowest":
+                            total_ref[q, at(j), :] += same - change
+                            total_ref[12 + q, at(j), :] += same + change
+                        else:
+                            total_ref[12 + q, at(j), :] += same - change
+
+    return begin, add
+
+
+def block_scatter(total_ref, base, finish):
+    first_row = lax.broadcasted_iota(jnp.int32, (8, 128), 0) == 0
+    carried = [jnp.zeros((8, 128), jnp.float32)] * 6
+    for j in range(8):
+        out = []
+        for k in range(3):
+            parts = []
+            for c in range(2):
+                same = total_ref[base + 4 * k + 2 * c, at(j), :]
+                change = total_ref[base + 4 * k + 2 * c + 1, at(j), :]
+                over = rows(same + change, 1)
+                parts.append(same - change + jnp.where(first_row, carried[2 * k + c], over))
+                carried[2 * k + c] = over
+            out.append(parts[0] - parts[1] + lanes(parts[0] + parts[1], 1))
+        finish(j, out)
+
+
+def inner_layers(add):
+    def step(i, unused):
+        n = H + 2 + 2 * i
+        add(n, n + 1, "inner")
+        add(n + 1, n + 2, "inner")
+        return unused
+
+    lax.fori_loop(0, 3, step, 0)
+
+
 def free_of(keep_ref, tile):
     def free(n, j):
         inside = jnp.where(tile * 8 + n == H, jnp.float32(0.0), jnp.float32(1.0))
@@ -404,7 +504,63 @@
         rhs_ref[k, 0] = held * load_ref[k, 0]
 
 
-def set_up(low, high, load_ref, own_ref, chip_ref, link_ref, keep_ref,
+def inverse_of(before, value, n, keep_ref, tile):
+    depth = tile * 8 + n
+    both = before + value
+    both = both + rows(both, 1)
+    both = DIAGONAL * (both + lanes(both, 1))
+    inside = jnp.where(depth == 0, jnp.float32(0.0), jnp.float32(1.0))
+    held = jnp.maximum(keep_ref[...], inside)
+    both = held * both + 1.0 - held
+    exists = (depth >= 0) & (depth < 1024)
+    both = jnp.where(exists, both, 1.0)
+    return jnp.where(exists, 1.0 / both, 0.0)
+
+
+def first_of(rhs_ref, inverse_ref):
+    def first(n, j):
+        scaled = OMEGA * inverse_ref[n, at(j), :]
+        return [rhs_ref[k, n, at(j), :] * scaled for k in range(3)]
+
+    return first
+
+
+def own_kernel(load_ref, own_ref, clamp_ref,
+               rhs_ref, moduli_ref, inverse_ref, keep_ref, total_ref, sum_ref,
+               along_ref, x_ref):
+    tile = tile_index()
+    keep_ref[...] = 1.0 - clamp_ref[...].astype(jnp.float32)
+    total = jnp.zeros((64, 128), jnp.float32)
+    before = None
+    for n in range(8):
+        value = own_ref[n]
+        moduli_ref[H + n] = value
+        total = total + value
+        if n:
+            inverse_ref[H + n] = inverse_of(before, value, n, keep_ref, tile)
+        before = value
+    sum_ref[3] = total
+    held = jnp.where(tile == 0, keep_ref[...], 1.0)
+    for k in range(3):
+        total = held * load_ref[k, 0]
+        rhs_ref[k, H] = total
+        for n in range(1, 8):
+            rhs_ref[k, H + n] = load_ref[k, n]
+            total = total + load_ref[k, n]
+        sum_ref[k] = total
+    total_ref[...] = jnp.zeros_like(total_ref)
+    inverse_ref[H + 8] = jnp.zeros((64, 128), jnp.float32)
+    for k in range(3):
+        rhs_ref[k, H + 8] = jnp.zeros((64, 128), jnp.float32)
+    begin, add = block_forces(
+        first_of(rhs_ref, inverse_ref), moduli_ref, along_ref, free_of(keep_ref, tile),
+        x_ref, total_ref,
+    )
+    begin(H + 1, H + 2)
+    inner_layers(add)
+
+
+def set_up(link_ref, chip_ref, own_rhs_ref, own_moduli_ref, own_inverse_ref, keep_ref,
            rhs_ref, moduli_ref, inverse_ref, tile):
     even = (tile & 1) == 0
 
@@ -420,7 +576,7 @@
         if n < 0:
             return below(3 + n + 2)
         if n < 8:
-            return own_ref[n]
+            return own_moduli_ref[n + H]
         if n < 9:
             return above(3)
         return above(14 + n - 9)
@@ -430,59 +586,61 @@
             return below(5 + 3 * k + n + 4)
         if n < 0:
             return below(k)
-        if n < 8:
-            return load_ref[k, n]
         if n < 9:
             return above(k)
         return above(5 + 3 * k + n - 9)
 
     before = None
-    for n in range(low - 1, high):
-        depth = tile * 8 + n
+    for n in range(-5, 12):
         value = moduli(n)
         moduli_ref[n + H] = value
-        if n >= low:
-            both = before + value
-            both = both + rows(both, 1)
-            both = DIAGONAL * (both + lanes(both, 1))
-            inside = jnp.where(depth == 0, jnp.float32(0.0), jnp.float32(1.0))
-            held = jnp.maximum(keep_ref[...], inside)
-            both = held * both + 1.0 - held
-            exists = (depth >= 0) & (depth < 1024)
-            both = jnp.where(exists, both, 1.0)
-            inverse_ref[n + H] = jnp.where(exists, 1.0 / both, 0.0)
-            for k in range(3):
-                rhs_ref[k, n + H] = held * load(k, n)
+        if 0 < n < 8:
+            inverse_ref[n + H] = own_inverse_ref[n + H]
+        elif n > -5:
+            inverse_ref[n + H] = inverse_of(before, value, n, keep_ref, tile)
         before = value
-
-
-def first_kernel(link_ref, chip_ref, load_ref, own_ref, keep_ref,
-                 send_ref,
-                 rhs_ref, moduli_ref, inverse_ref,
-                 along_ref, up_ref, x_ref, late_ref, sum_ref):
+        if n < -4:
+            continue
+        for k in range(3):
+            if 0 <= n < 8:
+                rhs_ref[k, n + H] = own_rhs_ref[k, n + H]
+            else:
+                depth = tile * 8 + n
+                inside = jnp.where(depth == 0, jnp.float32(0.0), jnp.float32(1.0))
+                rhs_ref[k, n + H] = jnp.maximum(keep_ref[...], inside) * load(k, n)
+
+
+def first_kernel(link_ref, chip_ref, own_rhs_ref, own_moduli_ref, own_inverse_ref, keep_ref,
+                 inner_ref, own_sum_ref,
+                 send_ref, rhs_ref, moduli_ref, inverse_ref,
+                 along_ref, x_ref, total_ref, sum_ref):
     tile = tile_index()
-    set_up(-1, 9, load_ref, own_ref, chip_ref, link_ref, keep_ref,
+    set_up(link_ref, chip_ref, own_rhs_ref, own_moduli_ref, own_inverse_ref, keep_ref,
            rhs_ref, moduli_ref, inverse_ref, tile)
     free = free_of(keep_ref, tile)
-    total = moduli_ref[H]
-    for n in range(1, 8):
-        total = total + moduli_ref[n + H]
-    sum_ref[3] = total
-    for k in range(3):
-        sum_ref[k] = jnp.zeros((64, 128), jnp.float32)
-
-    def first(n, j):
-        scaled = OMEGA * inverse_ref[n, at(j), :]
-        return [rhs_ref[k, n, at(j), :] * scaled for k in range(3)]
-
-    def finish(n, j, out):
-        held = free(n, j) > 0.0
-        value = first(n, j)
+    total_ref[...] = inner_ref[...]
+    first = first_of(rhs_ref, inverse_ref)
+    begin, add = block_forces(first, moduli_ref, along_ref, free, x_ref, total_ref)
+    begin(H - 1, H)
+    add(H, H + 1, "below")
+    add(H + 1, H + 1, "lowest")
+    begin(H + 7, H + 8)
+    add(H + 8, H + 8, "above")
+
+    def lowest(j, out):
+        held = free(H, j) > 0.0
+        value = first(H, j)
         for k in range(3):
             image = jnp.where(held, out[k], value[k])
-            sum_ref[k, at(j), :] += rhs_ref[k, n, at(j), :] - image
-
-    stiff(5, 13, first, finish, moduli_ref, along_ref, up_ref, free, x_ref, late_ref)
+            sum_ref[k, at(j), :] = own_sum_ref[k, at(j), :] - image
+
+    def others(j, out):
+        for k in range(3):
+            sum_ref[k, at(j), :] -= out[k]
+
+    block_scatter(total_ref, 0, lowest)
+    block_scatter(total_ref, 12, others)
+    sum_ref[3] = own_sum_ref[3]
     four = block_sums(sum_ref[...].reshape(256, 128))
     lane = lax.broadcasted_iota(jnp.int32, (1, 128), 1)
     edge = (lane >= 112) | ((lane & 15) == 15) | (lax.rem(tile, GROUP) == GROUP - 1)
@@ -490,14 +648,11 @@
     send_rows(send_ref, four)
 
 
-def middle_kernel(gathered_ref, link_ref, chip_ref, load_ref, own_ref, keep_ref,
+def middle_kernel(gathered_ref, rhs_ref, moduli_ref, inverse_ref, keep_ref,
                   ahead_ref, image_ref, coarse_ref, send_ref,
-                  rhs_ref, moduli_ref, inverse_ref,
-                  along_ref, up_ref, x_ref, late_ref,
+                  along_ref, up_ref, x_ref, late_ref, total_ref,
                   sum_ref, dots_ref, window_ref, solved_ref, spread_ref):
     tile = tile_index()
-    set_up(-4, 12, load_ref, own_ref, chip_ref, link_ref, keep_ref,
-           rhs_ref, moduli_ref, inverse_ref, tile)
     free = free_of(keep_ref, tile)
     coarse_ref[...] = coarse_solve(gathered_ref, None, tile, window_ref, solved_ref, spread_ref)
     correction = correction_of(spread_ref)
@@ -532,25 +687,43 @@
 
     stiff(3, 15, ahead, keep_image, moduli_ref, along_ref, up_ref, free, x_ref, late_ref)
 
-    for k in range(3):
-        sum_ref[k] = jnp.zeros((64, 128), jnp.float32)
+    total_ref[12:24] = jnp.zeros((12, 64, 128), jnp.float32)
+    first = first_of(image_ref, inverse_ref)
+    begin, add = block_forces(first, moduli_ref, along_ref, free, x_ref, total_ref)
+    begin(H - 1, H)
+    add(H, H + 1, "below")
+    add(H + 1, H + 2, "lowest")
+    inner_layers(add)
+    add(H + 8, H + 8, "above")
+
+    def lowest(j, out):
+        held = free(H, j) > 0.0
+        value = first(H, j)
+        for k in range(3):
+            sum_ref[k, at(j), :] = -jnp.where(held, out[k], value[k])
+
+    def others(j, out):
+        for k in range(3):
+            sum_ref[k, at(j), :] -= out[k]
+
+    block_scatter(total_ref, 0, lowest)
+    block_scatter(total_ref, 12, others)
     dots_ref[...] = jnp.zeros_like(dots_ref)
 
-    def first(n, j):
-        scaled = OMEGA * inverse_ref[n, at(j), :]
-        return [image_ref[k, n, at(j), :] * scaled for k in range(3)]
-
-    def finish(n, j, out):
-        held = free(n, j) > 0.0
-        value = first(n, j)
-        for k in range(3):
-            image = image_ref[k, n, at(j), :]
-            sum_ref[k, at(j), :] += image - jnp.where(held, out[k], value[k])
-            now = ahead_ref[k, n, at(j), :]
-            dots_ref[0, k] += now * rhs_ref[k, n, at(j), :]
-            dots_ref[1, k] += now * image
-
-    stiff(5, 13, first, finish, moduli_ref, along_ref, up_ref, free, x_ref, late_ref)
+    def products(n, unused):
+        for k in range(3):
+            by_rhs, by_image = [], []
+            for j in range(8):
+                image = image_ref[k, n, at(j), :]
+                now = ahead_ref[k, n, at(j), :]
+                sum_ref[k, at(j), :] += image
+                by_rhs.append(now * rhs_ref[k, n, at(j), :])
+                by_image.append(now * image)
+            dots_ref[0, k] += sum(by_rhs[1:], by_rhs[0])
+            dots_ref[1, k] += sum(by_image[1:], by_image[0])
+        return unused
+
+    lax.fori_loop(H, H + 8, products, 0)
     three = block_sums(sum_ref[...].reshape(192, 128))
     lane = lax.broadcasted_iota(jnp.int32, (1, 128), 1)
     gamma = jnp.sum(dots_ref[0])
@@ -691,20 +864,23 @@
     from_link = lax.ppermute(to_link, BOTH, links)
     from_chip = lax.ppermute(to_chip, BOTH, pairs)
     own = (3, 8) + plane
-    rhs_own, moduli_own, keep = call(
-        own_kernel, [own, (8,) + plane, plane], [], load, moduli_own, clamp,
+    own_rhs, own_moduli, own_inverse, keep, inner, own_sum = call(
+        own_kernel, ready + [plane, (24,) + plane, (4,) + plane],
+        [(12,) + plane, (6,) + plane], load, moduli_own, clamp,
         cost=pl.CostEstimate(flops=20_000_000, bytes_accessed=20_000_000, transcendentals=0),
     )
-    (send,) = call(
-        first_kernel, [(512, 128)], ready + work + [(4,) + plane],
-        from_link, from_chip, rhs_own, moduli_own, keep,
+    send, rhs, moduli, inverse = call(
+        first_kernel, [(512, 128)] + ready,
+        [(12,) + plane, (6,) + plane, (24,) + plane, (4,) + plane],
+        from_link, from_chip, own_rhs, own_moduli, own_inverse, keep, inner, own_sum,
     )
     gathered = to_all(send)
-    ahead, image, coarse, send, rhs, moduli, inverse = call(
+    ahead, image, coarse, send = call(
         middle_kernel,
-        [field, field, (WINDOW, 128), (512, 128)] + ready,
-        work + [(3,) + plane, (2, 3, 8, 128), (4 * WINDOW, 128), (3 * WINDOW, 128), (72, 128)],
-        gathered, from_link, from_chip, rhs_own, moduli_own, keep,
+        [field, field, (WINDOW, 128), (512, 128)],
+        work + [(24,) + plane, (3,) + plane, (2, 3, 8, 128), (4 * WINDOW, 128),
+                (3 * WINDOW, 128), (72, 128)],
+        gathered, rhs, moduli, inverse, keep,
     )
     gathered = to_all(send)
     following, following_image, scalars, send = call(

time: 93.3 us -> 90.8 us (0.973)
  Pallas kernels: 27 us -> 25.4 us
  waiting for transfers between devices: 4.4 us -> 3.4 us
    pallas_call x5, Pallas kernels: 23.9 us -> 22.3 us  [call(): pl.pallas_call(kernel, out_shape=[jax.ShapeDtypeStruct(s, jnp.float32) fo...]
    ppermute x1, waiting for transfers between devices: 4.4 us -> 3.4 us  [body(): from_link = lax.ppermute(to_link, BOTH, links)]
  transfers between devices with their start and end apart: 2 -> 2, of which waited for: 1 -> 1; matrix products, arithmetic and copies ran while one was open for 0% -> 0% of each run, Pallas kernels for 0% -> 1%
where the time goes in v5:
time: 90.8 us; the launch traced here: 90.4 us
  blocking collectives  53.4 us (59%)
  Pallas kernels  25.4 us (28%)
  starting transfers between devices  4.68 us (5%)
  waiting for transfers between devices  3.4 us (4%)
  local copies, waits for them, and re-layouts  2.84 us (3%)
    all_to_all x3, blocking collectives, to_all(): parts = lax.all_to_all(block.reshape(128, count, 128), BOTH, 0, 0)  53.4 us
    pallas_call x5, Pallas kernels, call(): pl.pallas_call(kernel, out_shape=[jax.ShapeDtypeStruct(s, jnp.float32) fo...  22.3 us
    ppermute x1, starting transfers between devices, body(): from_link = lax.ppermute(to_link, BOTH, links)  4.6 us
    ppermute x1, waiting for transfers between devices, body(): from_link = lax.ppermute(to_link, BOTH, links)  3.4 us
    pallas_call x1, Pallas kernels, body(): pl.pallas_call(pack_kernel, out_shape=[jax.ShapeDtypeStruct(s, jnp.float3...  3.03 us
    unnamed x6, local copies, waits for them, and re-layouts  2.84 us
  transfers between devices with their start and end apart: 2, of which 1 were waited for; matrix products, arithmetic and copies ran while one was open for 0% of the time, Pallas kernels for 1%

profile of v5, /device:TPU:1, one launch (start us, length us, event | category | flops | bytes accessed | tf_op | source)
XLA Modules:
  0.0 90.4 jit_solution(13219486573073595475)
XLA Ops:
  0.6 3.0 %shard_map.59 = (f32[17,64,128]{2,1,0:T(8,128)}, f32[17,64,128]{2,1,0:T(8,128)}, f32[8,64,128]{2,1,0:T(8,128)}) custom-call(f32[3,8,64,128]{3,2,1,0:T(8,128)} %load_ref.1, s32[8,64,128]{2,1,0:T(8,128)} %phases_hbm.1, f32[4]{0:T(128)} %table_ref.1), custom_call_target="tpu_custom_call" | custom-call | tf_op jit(solution)/shard_map/pallas_call | solution.py:851
  3.7 4.6 %collective-permute-start = (f32[17,64,128]{2,1,0:T(8,128)}, f32[17,64,128]{2,1,0:T(8,128)S(1)}, u32[]{:S(2)}, u32[]{:S(2)}) collective-permute-start(f32[17,64,128]{2,1,0:T(8,128)} %get-tuple-element.23), channel_id=1, source_target_pairs={{1,2},{2,1},{3,4},{4,3},{5,6},{6,5},{7,8},{8,7},{9,10},{10,9},{11,... | collective-permute-start | bytes 1671176 | tf_op jit(solution)/shard_map/ppermute | solution.py:864
  8.3 0.1 collective-permute-start.1
  8.4 0.0 copy-start
  8.4 1.1 %copy-done = f32[3,8,64,128]{3,2,1,0:T(8,128)S(1)} copy-done((f32[3,8,64,128]{3,2,1,0:T(8,128)S(1)}, f32[3,8,64,128]{3,2,1,0:T(8,128)}, u32[]{:S(2)}) %copy-start) | copy-done | bytes 786456
  9.5 0.0 copy-start.1
  9.5 0.9 %copy-done.1 = f32[8,64,128]{2,1,0:T(8,128)S(1)} copy-done((f32[8,64,128]{2,1,0:T(8,128)S(1)}, f32[8,64,128]{2,1,0:T(8,128)}, u32[]{:S(2)}) %copy-start.1) | copy-done | bytes 262168
  10.5 0.0 copy-start.2
  10.5 0.8 copy-done.2
  11.2 1.1 %shard_map.60 = (f32[3,17,64,128]{3,2,1,0:T(8,128)S(1)}, f32[17,64,128]{2,1,0:T(8,128)S(1)}, f32[17,64,128]{2,1,0:T(8,128)S(1)}, f32[64,128]{1,0:T(8,128)S(1)}, ...) custom-call(f32[3,8,64,128]{3,2,1,0:T(8,128)S(1)} %copy-done, f32[8,64,128]{2,1,0:T(8,128)S(1)} %copy-done.1, ...), custom_call_target="tpu_custom_call" | custom-call | flops 20000000 | bytes 20000000 | tf_op jit(solution)/shard_map/pallas_call | solution.py:824
  12.3 3.4 %collective-permute-done.link_ref = f32[17,64,128]{2,1,0:T(8,128)S(1)} collective-permute-done((f32[17,64,128]{2,1,0:T(8,128)}, f32[17,64,128]{2,1,0:T(8,128)S(1)}, u32[]{:S(2)}, u32[]{:S(2)}) %collective-permute-start) | collective-permute-done | bytes 557088 | tf_op jit(solution)/shard_map/ppermute | solution.py:864
  15.7 0.0 collective-permute-done.1.chip_ref
  15.7 1.2 %shard_map.61 = (f32[512,128]{1,0:T(8,128)S(1)}, f32[3,17,64,128]{3,2,1,0:T(8,128)S(1)}, f32[17,64,128]{2,1,0:T(8,128)S(1)}, f32[17,64,128]{2,1,0:T(8,128)S(1)}) custom-call(f32[17,64,128]{2,1,0:T(8,128)S(1)} %collective-permute-done.link_ref, f32[17,64,128]{2,1,0:T(8,128)S(1)} %collective-permute-done.1.chip_ref, ...), custom_call_target="tpu_custom_call" | custom-call | tf_op jit(solution)/shard_map/pallas_call | solution.py:824
  16.9 24.5 %all_to_all.15 = f32[128,4,128]{2,1,0:T(4,128)S(1)} all-to-all(f32[128,4,128]{2,1,0:T(4,128)S(1)} %bitcast.11), channel_id=1, replica_groups=mesh['grp'=4,'gz'=32] {'grp','gz'}, dimensions={0} | all-to-all | bytes 524288 | tf_op jit(solution)/shard_map/all_to_all | solution.py:837
  41.4 11.2 %shard_map.62 = (f32[3,17,64,128]{3,2,1,0:T(8,128)S(1)}, f32[3,17,64,128]{3,2,1,0:T(8,128)S(1)}, f32[16,128]{1,0:T(8,128)S(1)}, f32[512,128]{1,0:T(8,128)S(1)}) custom-call(f32[512,128]{1,0:T(8,128)S(1)} %bitcast.9, f32[3,17,64,128]{3,2,1,0:T(8,128)S(1)} %get-tuple-element.33.rhs_ref, f32[17,64,128]{2,1,0:T(8,128)S(1)} %get-tuple-element.34.moduli_ref, ...), custom_call_target="tpu_custom_call" | custom-call | tf_op jit(solution)/shard_map/pallas_call | solution.py:824
  52.6 15.2 %all_to_all.16 = f32[128,4,128]{2,1,0:T(4,128)S(1)} all-to-all(f32[128,4,128]{2,1,0:T(4,128)S(1)} %bitcast.12), channel_id=1, replica_groups=mesh['grp'=4,'gz'=32] {'grp','gz'}, dimensions={0} | all-to-all | bytes 524288 | tf_op jit(solution)/shard_map/all_to_all | solution.py:837
  67.8 7.2 %shard_map.63 = (f32[3,8,64,128]{3,2,1,0:T(8,128)S(1)}, f32[3,8,64,128]{3,2,1,0:T(8,128)S(1)}, f32[8,128]{1,0:T(8,128)S(1)}, f32[128,128]{1,0:T(8,128)S(1)}) custom-call(f32[512,128]{1,0:T(8,128)S(1)} %bitcast.8, f32[3,17,64,128]{3,2,1,0:T(8,128)S(1)} %get-tuple-element.33.rhs_ref, f32[17,64,128]{2,1,0:T(8,128)S(1)} %get-tuple-element.34.moduli_ref, ...), custom_call_target="tpu_custom_call" | custom-call | tf_op jit(solution)/shard_map/pallas_call | solution.py:824
  74.9 13.7 %all_to_all.17 = f32[128,1,128]{2,1,0:T(1,128)S(1)} all-to-all(f32[128,1,128]{2,1,0:T(1,128)S(1)} %bitcast.13), channel_id=1, replica_groups=mesh['grp'=4,'gz'=32] {'grp','gz'}, dimensions={0} | all-to-all | bytes 131072 | tf_op jit(solution)/shard_map/all_to_all | solution.py:837
  88.7 1.7 %shard_map.64 = (f32[3,8,64,128]{3,2,1,0:T(8,128)}, f32[3,8,64,128]{3,2,1,0:T(8,128)}) custom-call(f32[128,128]{1,0:T(8,128)S(1)} %bitcast.10, f32[8,128]{1,0:T(8,128)S(1)} %get-tuple-element.41.scalars_ref, f32[3,17,64,128]{3,2,1,0:T(8,128)S(1)} %get-tuple-element.33.rhs_ref, f32[3,17,64,128]{3,2,1,0:T(8,128)S(1)} %get-tuple-element.37.ahead_ref, ...), custom_call_target="tpu_custom_call" | custom-call | tf_op jit(solution)/shard_map/pallas_call | solution.py:824
Async XLA Ops:
  3.7 12.0 %collective-permute-start = (f32[17,64,128]{2,1,0:T(8,128)}, f32[17,64,128]{2,1,0:T(8,128)S(1)}, u32[]{:S(2)}, u32[]{:S(2)}) collective-permute-start(f32[17,64,128]{2,1,0:T(8,128)} %get-tuple-element.23), channel_id=1, source_target_pairs={{1,2},{2,1},{3,4},{4,3},{5,6},{6,5},{7,8},{8,7},{9,10},{10,9},{11,... | collective-permute-start | bytes 1671176 | tf_op jit(solution)/shard_map/ppermute | solution.py:864
  8.3 7.4 %collective-permute-start.1 = (f32[17,64,128]{2,1,0:T(8,128)}, f32[17,64,128]{2,1,0:T(8,128)S(1)}, u32[]{:S(2)}, u32[]{:S(2)}) collective-permute-start(f32[17,64,128]{2,1,0:T(8,128)} %get-tuple-element.24), channel_id=1, source_target_pairs={{0,1},{1,0},{2,3},{3,2},{4,5},{5,4},{6,7},{7,6},{8,9},{9,8},{10,11... | collective-permute-start | bytes 1671176 | tf_op jit(solution)/shard_map/ppermute | solution.py:865
  8.4 1.1 %copy-start = (f32[3,8,64,128]{3,2,1,0:T(8,128)S(1)}, f32[3,8,64,128]{3,2,1,0:T(8,128)}, u32[]{:S(2)}) copy-start(f32[3,8,64,128]{3,2,1,0:T(8,128)} %load_ref.1) | copy-start | bytes 2359300
  9.5 0.9 %copy-start.1 = (f32[8,64,128]{2,1,0:T(8,128)S(1)}, f32[8,64,128]{2,1,0:T(8,128)}, u32[]{:S(2)}) copy-start(f32[8,64,128]{2,1,0:T(8,128)} %get-tuple-element.25.own_ref) | copy-start | bytes 786436
  10.5 0.8 copy-start.2

commit v6 on v5

--- a/solution.py
+++ b/solution.py
@@ -452,56 +452,52 @@
 
 
 def pack_kernel(load_hbm, phases_hbm, table_ref,
-                chip_ref, link_ref, moduli_ref,
-                load_ref, phases_ref, arrived):
-    fetch_phases = pltpu.make_async_copy(phases_hbm, phases_ref, arrived.at[0])
-    fetch_load = pltpu.make_async_copy(load_hbm, load_ref, arrived.at[1])
-    fetch_phases.start()
-    fetch_load.start()
+                chip_hbm, link_hbm, moduli_hbm,
+                phases_ref, moduli_ref, arrived, sent):
     tile = tile_index()
-    row = lax.broadcasted_iota(jnp.int32, (64, 128), 0)
-    lane = lax.broadcasted_iota(jnp.int32, (64, 128), 1)
-    interior = (row < 63) & (lane < 127)
-    table = [table_ref[i] for i in range(4)]
-    fetch_phases.wait()
-    for n in range(8):
-        value = jnp.zeros((64, 128), jnp.float32)
-        for i in range(4):
-            value = jnp.where(phases_ref[n] == i, table[i], value)
-        inside = interior if n < 7 else interior & (tile < 127)
-        moduli_ref[n] = jnp.where(inside, value, 0.0)
-    fetch_load.wait()
-
-    def fill(top_ref, low_ref):
-        for k in range(3):
-            top_ref[k] = load_ref[k, 7]
-            low_ref[k] = load_ref[k, 0]
-            for n in range(3):
-                top_ref[5 + 3 * k + n] = load_ref[k, 4 + n]
-                low_ref[5 + 3 * k + n] = load_ref[k, 1 + n]
-        for n in range(2):
-            top_ref[3 + n] = moduli_ref[6 + n]
-            low_ref[3 + n] = moduli_ref[n]
-        for n in range(3):
-            top_ref[14 + n] = moduli_ref[3 + n]
-            low_ref[14 + n] = moduli_ref[1 + n]
+
+    def fill(top_hbm, low_hbm):
+        moves = []
+
+        def move(source, target):
+            copy = pltpu.make_async_copy(source, target, sent.at[len(moves)])
+            copy.start()
+            moves.append(copy)
+
+        fetch = pltpu.make_async_copy(phases_hbm, phases_ref, arrived)
+        fetch.start()
+        for k in range(3):
+            behind = slice(5 + 3 * k, 8 + 3 * k)
+            move(load_hbm.at[k, 4:7], top_hbm.at[behind])
+            move(load_hbm.at[k, 1:4], low_hbm.at[behind])
+            move(load_hbm.at[k, 7], top_hbm.at[k])
+            move(load_hbm.at[k, 0], low_hbm.at[k])
+        row = lax.broadcasted_iota(jnp.int32, (64, 128), 0)
+        lane = lax.broadcasted_iota(jnp.int32, (64, 128), 1)
+        interior = (row < 63) & (lane < 127)
+        table = [table_ref[i] for i in range(4)]
+        fetch.wait()
+        for n in range(8):
+            value = jnp.zeros((64, 128), jnp.float32)
+            for i in range(4):
+                value = jnp.where(phases_ref[n] == i, table[i], value)
+            inside = interior if n < 7 else interior & (tile < 127)
+            moduli_ref[n] = jnp.where(inside, value, 0.0)
+        move(moduli_ref.at[6:8], top_hbm.at[3:5])
+        move(moduli_ref.at[3:6], top_hbm.at[14:17])
+        move(moduli_ref.at[0:2], low_hbm.at[3:5])
+        move(moduli_ref.at[1:4], low_hbm.at[14:17])
+        move(moduli_ref, moduli_hbm)
+        for copy in moves:
+            copy.wait()
 
     @pl.when((tile & 1) == 0)
     def even():
-        fill(chip_ref, link_ref)
+        fill(chip_hbm, link_hbm)
 
     @pl.when((tile & 1) == 1)
     def odd():
-        fill(link_ref, chip_ref)
-
-
-def own_kernel(load_ref, own_ref, clamp_ref, rhs_ref, moduli_ref, keep_ref):
-    keep_ref[...] = 1.0 - clamp_ref[...].astype(jnp.float32)
-    moduli_ref[...] = own_ref[...]
-    for k in range(3):
-        rhs_ref[k] = load_ref[k]
-        held = jnp.where(tile_index() == 0, keep_ref[...], 1.0)
-        rhs_ref[k, 0] = held * load_ref[k, 0]
+        fill(link_hbm, chip_hbm)
 
 
 def inverse_of(before, value, n, keep_ref, tile):
@@ -794,7 +790,8 @@
 
 
 def close_kernel(gathered_ref, scalars_ref, rhs_ref, ahead_ref, image_ref, next_ref,
-                 next_image_ref, displacement_ref, residual_ref):
+                 next_image_ref, displacement_hbm, residual_hbm,
+                 displacement_ref, residual_ref, sent):
     before = scalars_ref[0:1, :]
     gamma, energy = lane_value(before, 0), lane_value(before, 1)
     dots = jnp.sum(gathered_ref[...], axis=0, keepdims=True)
@@ -813,7 +810,18 @@
             residual_ref[k, n] = residual - alpha_next * (next_image_ref[k, n] + beta * image)
         return unused
 
-    lax.fori_loop(0, 8, step, 0)
+    copies = []
+    for part in range(4):
+        lax.fori_loop(2 * part, 2 * part + 2, step, 0)
+        there = slice(2 * part, 2 * part + 2)
+        for source, target in ((displacement_ref, displacement_hbm), (residual_ref, residual_hbm)):
+            copy = pltpu.make_async_copy(
+                source.at[:, there], target.at[:, there], sent.at[len(copies)]
+            )
+            copy.start()
+            copies.append(copy)
+    for copy in copies:
+        copy.wait()
 
 
 def call(kernel, outs, scratch, *args, smem=(), cost=None):
@@ -847,17 +855,17 @@
     ready = [field, (EXT,) + plane, (EXT,) + plane]
     work = [(12,) + plane, (12,) + plane, (6,) + plane, (6,) + plane]
     halo = (17,) + plane
-    vmem = pl.BlockSpec(memory_space=pltpu.VMEM)
+    hbm = pl.BlockSpec(memory_space=pltpu.HBM)
     to_chip, to_link, moduli_own = pl.pallas_call(
         pack_kernel,
         out_shape=[jax.ShapeDtypeStruct(s, jnp.float32) for s in (halo, halo, (8,) + plane)],
-        in_specs=[pl.BlockSpec(memory_space=pltpu.HBM)] * 2
-        + [pl.BlockSpec(memory_space=pltpu.SMEM)],
-        out_specs=[vmem, vmem, vmem],
+        in_specs=[hbm, hbm, pl.BlockSpec(memory_space=pltpu.SMEM)],
+        out_specs=[hbm, hbm, hbm],
         scratch_shapes=[
-            pltpu.VMEM(load.shape, jnp.float32),
             pltpu.VMEM(phases.shape, jnp.int32),
-            pltpu.SemaphoreType.DMA((2,)),
+            pltpu.VMEM((8,) + plane, jnp.float32),
+            pltpu.SemaphoreType.DMA,
+            pltpu.SemaphoreType.DMA((17,)),
         ],
         compiler_params=pltpu.CompilerParams(vmem_limit_bytes=60 * 2**20),
     )(load, phases, phase_moduli)
@@ -890,10 +898,19 @@
         gathered, rhs, moduli, inverse, keep, ahead, image, coarse,
     )
     gathered = to_all(send)
-    displacement, residual = call(
-        close_kernel, [own, own], [],
-        gathered, scalars, rhs, ahead, image, following, following_image,
-    )
+    last = [gathered, scalars, rhs, ahead, image, following, following_image]
+    displacement, residual = pl.pallas_call(
+        close_kernel,
+        out_shape=[jax.ShapeDtypeStruct(own, jnp.float32)] * 2,
+        in_specs=[pl.BlockSpec(memory_space=pltpu.VMEM)] * len(last),
+        out_specs=[hbm, hbm],
+        scratch_shapes=[
+            pltpu.VMEM(own, jnp.float32),
+            pltpu.VMEM(own, jnp.float32),
+            pltpu.SemaphoreType.DMA((8,)),
+        ],
+        compiler_params=pltpu.CompilerParams(vmem_limit_bytes=14 * 2**20),
+    )(*last)
     return displacement, residual
 
 

time: 90.8 us -> 113 us (1.24)
  Pallas kernels: 25.4 us -> 47.9 us
    pallas_call x1, Pallas kernels: 3.03 us -> 25.8 us  [body(): pl.pallas_call(pack_kernel, out_shape=[jax.ShapeDtypeStruct(s, jnp.float3...]
    pallas_call x5 -> x4, Pallas kernels: 22.3 us -> 20.6 us  [call(): pl.pallas_call(kernel, out_shape=[jax.ShapeDtypeStruct(s, jnp.float32) fo...]
    pallas_call x0 -> x1, Pallas kernels: none -> 1.49 us  [body(): pl.pallas_call(close_kernel, out_shape=[jax.ShapeDtypeStruct(own, jnp.flo...]
where the time goes in v6:
time: 113 us
  blocking collectives  53.4 us (47%)
  Pallas kernels  47.9 us (42%)
  starting transfers between devices  4.67 us (4%)
  waiting for transfers between devices  3.4 us (3%)
  local copies, waits for them, and re-layouts  2.84 us (3%)
    all_to_all x3, blocking collectives, to_all(): parts = lax.all_to_all(block.reshape(128, count, 128), BOTH, 0, 0)  53.4 us
    pallas_call x1, Pallas kernels, body(): pl.pallas_call(pack_kernel, out_shape=[jax.ShapeDtypeStruct(s, jnp.float3...  25.8 us
    pallas_call x4, Pallas kernels, call(): pl.pallas_call(kernel, out_shape=[jax.ShapeDtypeStruct(s, jnp.float32) fo...  20.6 us
    ppermute x1, starting transfers between devices, body(): from_link = lax.ppermute(to_link, BOTH, links)  4.59 us
    ppermute x1, waiting for transfers between devices, body(): from_link = lax.ppermute(to_link, BOTH, links)  3.4 us
    unnamed x6, local copies, waits for them, and re-layouts  2.84 us
  transfers between devices with their start and end apart: 2, of which 1 were waited for; matrix products, arithmetic and copies ran while one was open for 0% of the time, Pallas kernels for 1%

profile of v6, /device:TPU:1, one launch (start us, length us, event | category | flops | bytes accessed | tf_op | source)
XLA Modules:
  0.0 112.9 jit_solution(4213270115652406568)
XLA Ops:
  0.6 25.8 %shard_map.59 = (f32[17,64,128]{2,1,0:T(8,128)}, f32[17,64,128]{2,1,0:T(8,128)}, f32[8,64,128]{2,1,0:T(8,128)}) custom-call(f32[3,8,64,128]{3,2,1,0:T(8,128)} %load_ref.1, s32[8,64,128]{2,1,0:T(8,128)} %phases_hbm.1, f32[4]{0:T(128)} %table_ref.1), custom_call_target="tpu_custom_call" | custom-call | tf_op jit(solution)/shard_map/pallas_call | solution.py:859
  26.4 4.6 %collective-permute-start = (f32[17,64,128]{2,1,0:T(8,128)}, f32[17,64,128]{2,1,0:T(8,128)S(1)}, u32[]{:S(2)}, u32[]{:S(2)}) collective-permute-start(f32[17,64,128]{2,1,0:T(8,128)} %get-tuple-element.23), channel_id=1, source_target_pairs={{1,2},{2,1},{3,4},{4,3},{5,6},{6,5},{7,8},{8,7},{9,10},{10,9},{11,... | collective-permute-start | bytes 1671176 | tf_op jit(solution)/shard_map/ppermute | solution.py:872
  31.0 0.1 collective-permute-start.1
  31.1 0.0 copy-start
  31.1 1.1 copy-done
  32.2 0.0 copy-start.1
  32.2 0.9 copy-done.1
  33.2 0.0 copy-start.2
  33.2 0.8 copy-done.2
  33.9 1.1 shard_map.60
  35.0 3.4 %collective-permute-done.link_ref = f32[17,64,128]{2,1,0:T(8,128)S(1)} collective-permute-done((f32[17,64,128]{2,1,0:T(8,128)}, f32[17,64,128]{2,1,0:T(8,128)S(1)}, u32[]{:S(2)}, u32[]{:S(2)}) %collective-permute-start) | collective-permute-done | bytes 557088 | tf_op jit(solution)/shard_map/ppermute | solution.py:872
  38.4 0.0 collective-permute-done.1.chip_ref
  38.4 1.2 %shard_map.61 = (f32[512,128]{1,0:T(8,128)S(1)}, f32[3,17,64,128]{3,2,1,0:T(8,128)S(1)}, f32[17,64,128]{2,1,0:T(8,128)S(1)}, f32[17,64,128]{2,1,0:T(8,128)S(1)}) custom-call(f32[17,64,128]{2,1,0:T(8,128)S(1)} %collective-permute-done.link_ref, f32[17,64,128]{2,1,0:T(8,128)S(1)} %collective-permute-done.1.chip_ref, ...), custom_call_target="tpu_custom_call" | custom-call | tf_op jit(solution)/shard_map/pallas_call | solution.py:832
  39.6 24.5 %all_to_all.15 = f32[128,4,128]{2,1,0:T(4,128)S(1)} all-to-all(f32[128,4,128]{2,1,0:T(4,128)S(1)} %bitcast.11), channel_id=1, replica_groups=mesh['grp'=4,'gz'=32] {'grp','gz'}, dimensions={0} | all-to-all | bytes 524288 | tf_op jit(solution)/shard_map/all_to_all | solution.py:845
  64.1 11.2 %shard_map.62 = (f32[3,17,64,128]{3,2,1,0:T(8,128)S(1)}, f32[3,17,64,128]{3,2,1,0:T(8,128)S(1)}, f32[16,128]{1,0:T(8,128)S(1)}, f32[512,128]{1,0:T(8,128)S(1)}) custom-call(f32[512,128]{1,0:T(8,128)S(1)} %bitcast.9, f32[3,17,64,128]{3,2,1,0:T(8,128)S(1)} %get-tuple-element.33.rhs_ref, f32[17,64,128]{2,1,0:T(8,128)S(1)} %get-tuple-element.34.moduli_ref, ...), custom_call_target="tpu_custom_call" | custom-call | tf_op jit(solution)/shard_map/pallas_call | solution.py:832
  75.3 15.2 %all_to_all.16 = f32[128,4,128]{2,1,0:T(4,128)S(1)} all-to-all(f32[128,4,128]{2,1,0:T(4,128)S(1)} %bitcast.12), channel_id=1, replica_groups=mesh['grp'=4,'gz'=32] {'grp','gz'}, dimensions={0} | all-to-all | bytes 524288 | tf_op jit(solution)/shard_map/all_to_all | solution.py:845
  90.5 7.2 %shard_map.63 = (f32[3,8,64,128]{3,2,1,0:T(8,128)S(1)}, f32[3,8,64,128]{3,2,1,0:T(8,128)S(1)}, f32[8,128]{1,0:T(8,128)S(1)}, f32[128,128]{1,0:T(8,128)S(1)}) custom-call(f32[512,128]{1,0:T(8,128)S(1)} %bitcast.8, f32[3,17,64,128]{3,2,1,0:T(8,128)S(1)} %get-tuple-element.33.rhs_ref, f32[17,64,128]{2,1,0:T(8,128)S(1)} %get-tuple-element.34.moduli_ref, ...), custom_call_target="tpu_custom_call" | custom-call | tf_op jit(solution)/shard_map/pallas_call | solution.py:832
  97.7 13.7 %all_to_all.17 = f32[128,1,128]{2,1,0:T(1,128)S(1)} all-to-all(f32[128,1,128]{2,1,0:T(1,128)S(1)} %bitcast.13), channel_id=1, replica_groups=mesh['grp'=4,'gz'=32] {'grp','gz'}, dimensions={0} | all-to-all | bytes 131072 | tf_op jit(solution)/shard_map/all_to_all | solution.py:845
  111.4 1.5 %shard_map.64 = (f32[3,8,64,128]{3,2,1,0:T(8,128)}, f32[3,8,64,128]{3,2,1,0:T(8,128)}) custom-call(f32[128,128]{1,0:T(8,128)S(1)} %bitcast.10, f32[8,128]{1,0:T(8,128)S(1)} %get-tuple-element.41.scalars_ref, f32[3,17,64,128]{3,2,1,0:T(8,128)S(1)} %get-tuple-element.33.rhs_ref, f32[3,17,64,128]{3,2,1,0:T(8,128)S(1)} %get-tuple-element.37.ahead_ref, ...), custom_call_target="tpu_custom_call" | custom-call | tf_op jit(solution)/shard_map/pallas_call | solution.py:902
Async XLA Ops:
  26.4 12.0 %collective-permute-start = (f32[17,64,128]{2,1,0:T(8,128)}, f32[17,64,128]{2,1,0:T(8,128)S(1)}, u32[]{:S(2)}, u32[]{:S(2)}) collective-permute-start(f32[17,64,128]{2,1,0:T(8,128)} %get-tuple-element.23), channel_id=1, source_target_pairs={{1,2},{2,1},{3,4},{4,3},{5,6},{6,5},{7,8},{8,7},{9,10},{10,9},{11,... | collective-permute-start | bytes 1671176 | tf_op jit(solution)/shard_map/ppermute | solution.py:872
  31.0 7.4 %collective-permute-start.1 = (f32[17,64,128]{2,1,0:T(8,128)}, f32[17,64,128]{2,1,0:T(8,128)S(1)}, u32[]{:S(2)}, u32[]{:S(2)}) collective-permute-start(f32[17,64,128]{2,1,0:T(8,128)} %get-tuple-element.24), channel_id=1, source_target_pairs={{0,1},{1,0},{2,3},{3,2},{4,5},{5,4},{6,7},{7,6},{8,9},{9,8},{10,11... | collective-permute-start | bytes 1671176 | tf_op jit(solution)/shard_map/ppermute | solution.py:873
  31.1 1.1 %copy-start = (f32[3,8,64,128]{3,2,1,0:T(8,128)S(1)}, f32[3,8,64,128]{3,2,1,0:T(8,128)}, u32[]{:S(2)}) copy-start(f32[3,8,64,128]{3,2,1,0:T(8,128)} %load_ref.1) | copy-start | bytes 2359300
  32.2 0.9 copy-start.1
  33.2 0.8 copy-start.2

commit v7 on v6

--- a/solution.py
+++ b/solution.py
@@ -453,7 +453,7 @@
 
 def pack_kernel(load_hbm, phases_hbm, table_ref,
                 chip_hbm, link_hbm, moduli_hbm,
-                phases_ref, moduli_ref, arrived, sent):
+                load_ref, phases_ref, moduli_ref, arrived, sent):
     tile = tile_index()
 
     def fill(top_hbm, low_hbm):
@@ -464,14 +464,13 @@
             copy.start()
             moves.append(copy)
 
-        fetch = pltpu.make_async_copy(phases_hbm, phases_ref, arrived)
+        fetch = pltpu.make_async_copy(phases_hbm, phases_ref, arrived.at[3])
         fetch.start()
-        for k in range(3):
-            behind = slice(5 + 3 * k, 8 + 3 * k)
-            move(load_hbm.at[k, 4:7], top_hbm.at[behind])
-            move(load_hbm.at[k, 1:4], low_hbm.at[behind])
-            move(load_hbm.at[k, 7], top_hbm.at[k])
-            move(load_hbm.at[k, 0], low_hbm.at[k])
+        parts = []
+        for k in range(3):
+            part = pltpu.make_async_copy(load_hbm.at[k], load_ref.at[k], arrived.at[k])
+            part.start()
+            parts.append(part)
         row = lax.broadcasted_iota(jnp.int32, (64, 128), 0)
         lane = lax.broadcasted_iota(jnp.int32, (64, 128), 1)
         interior = (row < 63) & (lane < 127)
@@ -483,6 +482,13 @@
                 value = jnp.where(phases_ref[n] == i, table[i], value)
             inside = interior if n < 7 else interior & (tile < 127)
             moduli_ref[n] = jnp.where(inside, value, 0.0)
+        for k in range(3):
+            behind = slice(5 + 3 * k, 8 + 3 * k)
+            parts[k].wait()
+            move(load_ref.at[k, 4:7], top_hbm.at[behind])
+            move(load_ref.at[k, 1:4], low_hbm.at[behind])
+            move(load_ref.at[k, 7], top_hbm.at[k])
+            move(load_ref.at[k, 0], low_hbm.at[k])
         move(moduli_ref.at[6:8], top_hbm.at[3:5])
         move(moduli_ref.at[3:6], top_hbm.at[14:17])
         move(moduli_ref.at[0:2], low_hbm.at[3:5])
@@ -862,9 +868,10 @@
         in_specs=[hbm, hbm, pl.BlockSpec(memory_space=pltpu.SMEM)],
         out_specs=[hbm, hbm, hbm],
         scratch_shapes=[
+            pltpu.VMEM(load.shape, jnp.float32),
             pltpu.VMEM(phases.shape, jnp.int32),
             pltpu.VMEM((8,) + plane, jnp.float32),
-            pltpu.SemaphoreType.DMA,
+            pltpu.SemaphoreType.DMA((4,)),
             pltpu.SemaphoreType.DMA((17,)),
         ],
         compiler_params=pltpu.CompilerParams(vmem_limit_bytes=60 * 2**20),

time: 113 us -> 90.4 us (0.80)
  Pallas kernels: 47.9 us -> 25.1 us
    pallas_call x1, Pallas kernels: 25.8 us -> 2.96 us  [body(): pl.pallas_call(pack_kernel, out_shape=[jax.ShapeDtypeStruct(s, jnp.float3...]
where the time goes in v7:
time: 90.4 us; the launch traced here: 90.1 us
  blocking collectives  53.4 us (59%)
  Pallas kernels  25.1 us (28%)
  starting transfers between devices  4.67 us (5%)
  waiting for transfers between devices  3.4 us (4%)
  local copies, waits for them, and re-layouts  2.84 us (3%)
    all_to_all x3, blocking collectives, to_all(): parts = lax.all_to_all(block.reshape(128, count, 128), BOTH, 0, 0)  53.4 us
    pallas_call x4, Pallas kernels, call(): pl.pallas_call(kernel, out_shape=[jax.ShapeDtypeStruct(s, jnp.float32) fo...  20.6 us
    ppermute x1, starting transfers between devices, body(): from_link = lax.ppermute(to_link, BOTH, links)  4.59 us
    ppermute x1, waiting for transfers between devices, body(): from_link = lax.ppermute(to_link, BOTH, links)  3.4 us
    pallas_call x1, Pallas kernels, body(): pl.pallas_call(pack_kernel, out_shape=[jax.ShapeDtypeStruct(s, jnp.float3...  2.96 us
    unnamed x6, local copies, waits for them, and re-layouts  2.84 us
  transfers between devices with their start and end apart: 2, of which 1 were waited for; matrix products, arithmetic and copies ran while one was open for 0% of the time, Pallas kernels for 1%

profile of v7, /device:TPU:1, one launch (start us, length us, event | category | flops | bytes accessed | tf_op | source)
XLA Modules:
  0.0 90.1 jit_solution(3270540665374424725)
XLA Ops:
  0.6 3.0 %shard_map.59 = (f32[17,64,128]{2,1,0:T(8,128)}, f32[17,64,128]{2,1,0:T(8,128)}, f32[8,64,128]{2,1,0:T(8,128)}) custom-call(f32[3,8,64,128]{3,2,1,0:T(8,128)} %load_ref.1, s32[8,64,128]{2,1,0:T(8,128)} %phases_hbm.1, f32[4]{0:T(128)} %table_ref.1), custom_call_target="tpu_custom_call" | custom-call | tf_op jit(solution)/shard_map/pallas_call | solution.py:865
  3.6 4.6 %collective-permute-start = (f32[17,64,128]{2,1,0:T(8,128)}, f32[17,64,128]{2,1,0:T(8,128)S(1)}, u32[]{:S(2)}, u32[]{:S(2)}) collective-permute-start(f32[17,64,128]{2,1,0:T(8,128)} %get-tuple-element.23), channel_id=1, source_target_pairs={{1,2},{2,1},{3,4},{4,3},{5,6},{6,5},{7,8},{8,7},{9,10},{10,9},{11,... | collective-permute-start | bytes 1671176 | tf_op jit(solution)/shard_map/ppermute | solution.py:879
  8.2 0.1 collective-permute-start.1
  8.3 0.0 copy-start
  8.3 1.1 %copy-done = f32[3,8,64,128]{3,2,1,0:T(8,128)S(1)} copy-done((f32[3,8,64,128]{3,2,1,0:T(8,128)S(1)}, f32[3,8,64,128]{3,2,1,0:T(8,128)}, u32[]{:S(2)}) %copy-start) | copy-done | bytes 786456
  9.4 0.0 copy-start.1
  9.4 0.9 %copy-done.1 = f32[8,64,128]{2,1,0:T(8,128)S(1)} copy-done((f32[8,64,128]{2,1,0:T(8,128)S(1)}, f32[8,64,128]{2,1,0:T(8,128)}, u32[]{:S(2)}) %copy-start.1) | copy-done | bytes 262168
  10.4 0.0 copy-start.2
  10.4 0.8 copy-done.2
  11.1 1.1 %shard_map.60 = (f32[3,17,64,128]{3,2,1,0:T(8,128)S(1)}, f32[17,64,128]{2,1,0:T(8,128)S(1)}, f32[17,64,128]{2,1,0:T(8,128)S(1)}, f32[64,128]{1,0:T(8,128)S(1)}, ...) custom-call(f32[3,8,64,128]{3,2,1,0:T(8,128)S(1)} %copy-done, f32[8,64,128]{2,1,0:T(8,128)S(1)} %copy-done.1, ...), custom_call_target="tpu_custom_call" | custom-call | flops 20000000 | bytes 20000000 | tf_op jit(solution)/shard_map/pallas_call | solution.py:838
  12.2 3.4 %collective-permute-done.link_ref = f32[17,64,128]{2,1,0:T(8,128)S(1)} collective-permute-done((f32[17,64,128]{2,1,0:T(8,128)}, f32[17,64,128]{2,1,0:T(8,128)S(1)}, u32[]{:S(2)}, u32[]{:S(2)}) %collective-permute-start) | collective-permute-done | bytes 557088 | tf_op jit(solution)/shard_map/ppermute | solution.py:879
  15.6 0.0 collective-permute-done.1.chip_ref
  15.6 1.2 %shard_map.61 = (f32[512,128]{1,0:T(8,128)S(1)}, f32[3,17,64,128]{3,2,1,0:T(8,128)S(1)}, f32[17,64,128]{2,1,0:T(8,128)S(1)}, f32[17,64,128]{2,1,0:T(8,128)S(1)}) custom-call(f32[17,64,128]{2,1,0:T(8,128)S(1)} %collective-permute-done.link_ref, f32[17,64,128]{2,1,0:T(8,128)S(1)} %collective-permute-done.1.chip_ref, ...), custom_call_target="tpu_custom_call" | custom-call | tf_op jit(solution)/shard_map/pallas_call | solution.py:838
  16.8 24.5 %all_to_all.15 = f32[128,4,128]{2,1,0:T(4,128)S(1)} all-to-all(f32[128,4,128]{2,1,0:T(4,128)S(1)} %bitcast.11), channel_id=1, replica_groups=mesh['grp'=4,'gz'=32] {'grp','gz'}, dimensions={0} | all-to-all | bytes 524288 | tf_op jit(solution)/shard_map/all_to_all | solution.py:851
  41.3 11.2 %shard_map.62 = (f32[3,17,64,128]{3,2,1,0:T(8,128)S(1)}, f32[3,17,64,128]{3,2,1,0:T(8,128)S(1)}, f32[16,128]{1,0:T(8,128)S(1)}, f32[512,128]{1,0:T(8,128)S(1)}) custom-call(f32[512,128]{1,0:T(8,128)S(1)} %bitcast.9, f32[3,17,64,128]{3,2,1,0:T(8,128)S(1)} %get-tuple-element.33.rhs_ref, f32[17,64,128]{2,1,0:T(8,128)S(1)} %get-tuple-element.34.moduli_ref, ...), custom_call_target="tpu_custom_call" | custom-call | tf_op jit(solution)/shard_map/pallas_call | solution.py:838
  52.5 15.2 %all_to_all.16 = f32[128,4,128]{2,1,0:T(4,128)S(1)} all-to-all(f32[128,4,128]{2,1,0:T(4,128)S(1)} %bitcast.12), channel_id=1, replica_groups=mesh['grp'=4,'gz'=32] {'grp','gz'}, dimensions={0} | all-to-all | bytes 524288 | tf_op jit(solution)/shard_map/all_to_all | solution.py:851
  67.7 7.2 %shard_map.63 = (f32[3,8,64,128]{3,2,1,0:T(8,128)S(1)}, f32[3,8,64,128]{3,2,1,0:T(8,128)S(1)}, f32[8,128]{1,0:T(8,128)S(1)}, f32[128,128]{1,0:T(8,128)S(1)}) custom-call(f32[512,128]{1,0:T(8,128)S(1)} %bitcast.8, f32[3,17,64,128]{3,2,1,0:T(8,128)S(1)} %get-tuple-element.33.rhs_ref, f32[17,64,128]{2,1,0:T(8,128)S(1)} %get-tuple-element.34.moduli_ref, ...), custom_call_target="tpu_custom_call" | custom-call | tf_op jit(solution)/shard_map/pallas_call | solution.py:838
  74.9 13.7 %all_to_all.17 = f32[128,1,128]{2,1,0:T(1,128)S(1)} all-to-all(f32[128,1,128]{2,1,0:T(1,128)S(1)} %bitcast.13), channel_id=1, replica_groups=mesh['grp'=4,'gz'=32] {'grp','gz'}, dimensions={0} | all-to-all | bytes 131072 | tf_op jit(solution)/shard_map/all_to_all | solution.py:851
  88.6 1.5 %shard_map.64 = (f32[3,8,64,128]{3,2,1,0:T(8,128)}, f32[3,8,64,128]{3,2,1,0:T(8,128)}) custom-call(f32[128,128]{1,0:T(8,128)S(1)} %bitcast.10, f32[8,128]{1,0:T(8,128)S(1)} %get-tuple-element.41.scalars_ref, f32[3,17,64,128]{3,2,1,0:T(8,128)S(1)} %get-tuple-element.33.rhs_ref, f32[3,17,64,128]{3,2,1,0:T(8,128)S(1)} %get-tuple-element.37.ahead_ref, ...), custom_call_target="tpu_custom_call" | custom-call | tf_op jit(solution)/shard_map/pallas_call | solution.py:909
Async XLA Ops:
  3.6 12.0 %collective-permute-start = (f32[17,64,128]{2,1,0:T(8,128)}, f32[17,64,128]{2,1,0:T(8,128)S(1)}, u32[]{:S(2)}, u32[]{:S(2)}) collective-permute-start(f32[17,64,128]{2,1,0:T(8,128)} %get-tuple-element.23), channel_id=1, source_target_pairs={{1,2},{2,1},{3,4},{4,3},{5,6},{6,5},{7,8},{8,7},{9,10},{10,9},{11,... | collective-permute-start | bytes 1671176 | tf_op jit(solution)/shard_map/ppermute | solution.py:879
  8.2 7.4 %collective-permute-start.1 = (f32[17,64,128]{2,1,0:T(8,128)}, f32[17,64,128]{2,1,0:T(8,128)S(1)}, u32[]{:S(2)}, u32[]{:S(2)}) collective-permute-start(f32[17,64,128]{2,1,0:T(8,128)} %get-tuple-element.24), channel_id=1, source_target_pairs={{0,1},{1,0},{2,3},{3,2},{4,5},{5,4},{6,7},{7,6},{8,9},{9,8},{10,11... | collective-permute-start | bytes 1671176 | tf_op jit(solution)/shard_map/ppermute | solution.py:880
  8.3 1.1 %copy-start = (f32[3,8,64,128]{3,2,1,0:T(8,128)S(1)}, f32[3,8,64,128]{3,2,1,0:T(8,128)}, u32[]{:S(2)}) copy-start(f32[3,8,64,128]{3,2,1,0:T(8,128)} %load_ref.1) | copy-start | bytes 2359300
  9.4 0.9 %copy-start.1 = (f32[8,64,128]{2,1,0:T(8,128)S(1)}, f32[8,64,128]{2,1,0:T(8,128)}, u32[]{:S(2)}) copy-start(f32[8,64,128]{2,1,0:T(8,128)} %get-tuple-element.25.own_ref) | copy-start | bytes 786436
  10.4 0.8 copy-start.2

commit v8 on v7

--- a/solution.py
+++ b/solution.py
@@ -452,11 +452,17 @@
 
 
 def pack_kernel(load_hbm, phases_hbm, table_ref,
-                chip_hbm, link_hbm, moduli_hbm,
+                chip_hbm, near_hbm, far_hbm, moduli_hbm,
                 load_ref, phases_ref, moduli_ref, arrived, sent):
     tile = tile_index()
 
-    def fill(top_hbm, low_hbm):
+    def chip(first, last):
+        return chip_hbm.at[first:last]
+
+    def link(first, last):
+        return near_hbm.at[first:last] if last <= 5 else far_hbm.at[first - 5 : last - 5]
+
+    def fill(top, low):
         moves = []
 
         def move(source, target):
@@ -483,27 +489,26 @@
             inside = interior if n < 7 else interior & (tile < 127)
             moduli_ref[n] = jnp.where(inside, value, 0.0)
         for k in range(3):
-            behind = slice(5 + 3 * k, 8 + 3 * k)
             parts[k].wait()
-            move(load_ref.at[k, 4:7], top_hbm.at[behind])
-            move(load_ref.at[k, 1:4], low_hbm.at[behind])
-            move(load_ref.at[k, 7], top_hbm.at[k])
-            move(load_ref.at[k, 0], low_hbm.at[k])
-        move(moduli_ref.at[6:8], top_hbm.at[3:5])
-        move(moduli_ref.at[3:6], top_hbm.at[14:17])
-        move(moduli_ref.at[0:2], low_hbm.at[3:5])
-        move(moduli_ref.at[1:4], low_hbm.at[14:17])
+            move(load_ref.at[k, 7:8], top(k, k + 1))
+            move(load_ref.at[k, 0:1], low(k, k + 1))
+            move(load_ref.at[k, 4:7], top(5 + 3 * k, 8 + 3 * k))
+            move(load_ref.at[k, 1:4], low(5 + 3 * k, 8 + 3 * k))
+        move(moduli_ref.at[6:8], top(3, 5))
+        move(moduli_ref.at[0:2], low(3, 5))
+        move(moduli_ref.at[3:6], top(14, 17))
+        move(moduli_ref.at[1:4], low(14, 17))
         move(moduli_ref, moduli_hbm)
         for copy in moves:
             copy.wait()
 
     @pl.when((tile & 1) == 0)
     def even():
-        fill(chip_hbm, link_hbm)
+        fill(chip, link)
 
     @pl.when((tile & 1) == 1)
     def odd():
-        fill(link_hbm, chip_hbm)
+        fill(link, chip)
 
 
 def inverse_of(before, value, n, keep_ref, tile):
@@ -562,15 +567,18 @@
     inner_layers(add)
 
 
-def set_up(link_ref, chip_ref, own_rhs_ref, own_moduli_ref, own_inverse_ref, keep_ref,
+def set_up(low, high, near_ref, far_ref, chip_ref, own_rhs_ref, own_moduli_ref, own_inverse_ref, keep_ref,
            rhs_ref, moduli_ref, inverse_ref, tile):
     even = (tile & 1) == 0
 
+    def link(i):
+        return near_ref[i] if i < 5 else far_ref[i - 5]
+
     def below(i):
-        return jnp.where(even, link_ref[i], chip_ref[i])
+        return jnp.where(even, link(i), chip_ref[i])
 
     def above(i):
-        return jnp.where(even, chip_ref[i], link_ref[i])
+        return jnp.where(even, chip_ref[i], link(i))
 
     def moduli(n):
         if n < -2:
@@ -593,15 +601,15 @@
         return above(5 + 3 * k + n - 9)
 
     before = None
-    for n in range(-5, 12):
+    for n in range(low - 1, high):
         value = moduli(n)
         moduli_ref[n + H] = value
         if 0 < n < 8:
             inverse_ref[n + H] = own_inverse_ref[n + H]
-        elif n > -5:
+        elif n >= low:
             inverse_ref[n + H] = inverse_of(before, value, n, keep_ref, tile)
         before = value
-        if n < -4:
+        if n < low:
             continue
         for k in range(3):
             if 0 <= n < 8:
@@ -612,13 +620,13 @@
                 rhs_ref[k, n + H] = jnp.maximum(keep_ref[...], inside) * load(k, n)
 
 
-def first_kernel(link_ref, chip_ref, own_rhs_ref, own_moduli_ref, own_inverse_ref, keep_ref,
+def first_kernel(near_ref, chip_ref, own_rhs_ref, own_moduli_ref, own_inverse_ref, keep_ref,
                  inner_ref, own_sum_ref,
-                 send_ref, rhs_ref, moduli_ref, inverse_ref,
-                 along_ref, x_ref, total_ref, sum_ref):
+                 send_ref,
+                 rhs_ref, moduli_ref, inverse_ref, along_ref, x_ref, total_ref, sum_ref):
     tile = tile_index()
-    set_up(link_ref, chip_ref, own_rhs_ref, own_moduli_ref, own_inverse_ref, keep_ref,
-           rhs_ref, moduli_ref, inverse_ref, tile)
+    set_up(-1, 9, near_ref, None, chip_ref, own_rhs_ref, own_moduli_ref, own_inverse_ref,
+           keep_ref, rhs_ref, moduli_ref, inverse_ref, tile)
     free = free_of(keep_ref, tile)
     total_ref[...] = inner_ref[...]
     first = first_of(rhs_ref, inverse_ref)
@@ -650,11 +658,14 @@
     send_rows(send_ref, four)
 
 
-def middle_kernel(gathered_ref, rhs_ref, moduli_ref, inverse_ref, keep_ref,
-                  ahead_ref, image_ref, coarse_ref, send_ref,
+def middle_kernel(gathered_ref, near_ref, far_ref, chip_ref, own_rhs_ref, own_moduli_ref,
+                  own_inverse_ref, keep_ref,
+                  ahead_ref, image_ref, coarse_ref, send_ref, rhs_ref, moduli_ref, inverse_ref,
                   along_ref, up_ref, x_ref, late_ref, total_ref,
                   sum_ref, dots_ref, window_ref, solved_ref, spread_ref):
     tile = tile_index()
+    set_up(-4, 12, near_ref, far_ref, chip_ref, own_rhs_ref, own_moduli_ref, own_inverse_ref,
+           keep_ref, rhs_ref, moduli_ref, inverse_ref, tile)
     free = free_of(keep_ref, tile)
     coarse_ref[...] = coarse_solve(gathered_ref, None, tile, window_ref, solved_ref, spread_ref)
     correction = correction_of(spread_ref)
@@ -862,11 +873,11 @@
     work = [(12,) + plane, (12,) + plane, (6,) + plane, (6,) + plane]
     halo = (17,) + plane
     hbm = pl.BlockSpec(memory_space=pltpu.HBM)
-    to_chip, to_link, moduli_own = pl.pallas_call(
+    to_chip, to_near, to_far, moduli_own = pl.pallas_call(
         pack_kernel,
-        out_shape=[jax.ShapeDtypeStruct(s, jnp.float32) for s in (halo, halo, (8,) + plane)],
+        out_shape=[jax.ShapeDtypeStruct(s, jnp.float32) for s in (halo, (5,) + plane, (12,) + plane, (8,) + plane)],
         in_specs=[hbm, hbm, pl.BlockSpec(memory_space=pltpu.SMEM)],
-        out_specs=[hbm, hbm, hbm],
+        out_specs=[hbm] * 4,
         scratch_shapes=[
             pltpu.VMEM(load.shape, jnp.float32),
             pltpu.VMEM(phases.shape, jnp.int32),
@@ -876,7 +887,8 @@
         ],
         compiler_params=pltpu.CompilerParams(vmem_limit_bytes=60 * 2**20),
     )(load, phases, phase_moduli)
-    from_link = lax.ppermute(to_link, BOTH, links)
+    from_near = lax.ppermute(to_near, BOTH, links)
+    from_far = lax.ppermute(to_far, BOTH, links)
     from_chip = lax.ppermute(to_chip, BOTH, pairs)
     own = (3, 8) + plane
     own_rhs, own_moduli, own_inverse, keep, inner, own_sum = call(
@@ -884,18 +896,18 @@
         [(12,) + plane, (6,) + plane], load, moduli_own, clamp,
         cost=pl.CostEstimate(flops=20_000_000, bytes_accessed=20_000_000, transcendentals=0),
     )
-    send, rhs, moduli, inverse = call(
-        first_kernel, [(512, 128)] + ready,
-        [(12,) + plane, (6,) + plane, (24,) + plane, (4,) + plane],
-        from_link, from_chip, own_rhs, own_moduli, own_inverse, keep, inner, own_sum,
+    (send,) = call(
+        first_kernel, [(512, 128)],
+        ready + [(12,) + plane, (6,) + plane, (24,) + plane, (4,) + plane],
+        from_near, from_chip, own_rhs, own_moduli, own_inverse, keep, inner, own_sum,
     )
     gathered = to_all(send)
-    ahead, image, coarse, send = call(
+    ahead, image, coarse, send, rhs, moduli, inverse = call(
         middle_kernel,
-        [field, field, (WINDOW, 128), (512, 128)],
+        [field, field, (WINDOW, 128), (512, 128)] + ready,
         work + [(24,) + plane, (3,) + plane, (2, 3, 8, 128), (4 * WINDOW, 128),
                 (3 * WINDOW, 128), (72, 128)],
-        gathered, rhs, moduli, inverse, keep,
+        gathered, from_near, from_far, from_chip, own_rhs, own_moduli, own_inverse, keep,
     )
     gathered = to_all(send)
     following, following_image, scalars, send = call(

time: 90.4 us -> 91.5 us (1.012)
  blocking collectives: 53.4 us -> 28.9 us
  starting transfers between devices: 4.67 us -> 21.3 us
  waiting for transfers between devices: 3.4 us -> 10.7 us
    all_to_all x3 -> x2, blocking collectives: 53.4 us -> 28.9 us  [to_all(): parts = lax.all_to_all(block.reshape(128, count, 128), BOTH, 0, 0)]
    all_to_all x0 -> x1, starting transfers between devices: none -> 14.3 us  [to_all(): parts = lax.all_to_all(block.reshape(128, count, 128), BOTH, 0, 0)]
    all_to_all x0 -> x1, waiting for transfers between devices: none -> 10.7 us  [to_all(): parts = lax.all_to_all(block.reshape(128, count, 128), BOTH, 0, 0)]
    ppermute x1 -> x2, waiting for transfers between devices: 3.4 us -> 0.01 us  [the longest x1 0.01 us: body(): from_near = lax.ppermute(to_near, BOTH, links)]
    ppermute x1, starting transfers between devices: 0.08 us -> 1.5 us  [body(): from_chip = lax.ppermute(to_chip, BOTH, pairs)]
    ppermute x1 -> x2, starting transfers between devices: 4.59 us -> 5.55 us  [the longest x1 3.19 us: body(): from_near = lax.ppermute(to_near, BOTH, links)]
    unnamed x6 -> x8, local copies, waits for them, and re-layouts: 2.84 us -> 3.53 us
  transfers between devices with their start and end apart: 2 -> 4, of which waited for: 1 -> 1; matrix products, arithmetic and copies ran while one was open for 0% -> 0% of each run, Pallas kernels for 1% -> 2%
where the time goes in v8:
time: 91.5 us; the launch traced here: 91.1 us
  blocking collectives  28.9 us (32%)
  Pallas kernels  25.9 us (28%)
  starting transfers between devices  21.3 us (23%)
  waiting for transfers between devices  10.7 us (12%)
  local copies, waits for them, and re-layouts  3.53 us (4%)
    all_to_all x2, blocking collectives, to_all(): parts = lax.all_to_all(block.reshape(128, count, 128), BOTH, 0, 0)  28.9 us
    pallas_call x4, Pallas kernels, call(): pl.pallas_call(kernel, out_shape=[jax.ShapeDtypeStruct(s, jnp.float32) fo...  21.5 us
    all_to_all x1, starting transfers between devices, to_all(): parts = lax.all_to_all(block.reshape(128, count, 128), BOTH, 0, 0)  14.3 us
    all_to_all x1, waiting for transfers between devices, to_all(): parts = lax.all_to_all(block.reshape(128, count, 128), BOTH, 0, 0)  10.7 us
    unnamed x8, local copies, waits for them, and re-layouts  3.53 us
    ppermute x1, starting transfers between devices, body(): from_near = lax.ppermute(to_near, BOTH, links)  3.19 us
    pallas_call x1, Pallas kernels, body(): pl.pallas_call(pack_kernel, out_shape=[jax.ShapeDtypeStruct(s, jnp.float3...  2.95 us
    ppermute x1, starting transfers between devices, body(): from_far = lax.ppermute(to_far, BOTH, links)  2.37 us
  transfers between devices with their start and end apart: 4, of which 1 were waited for; matrix products, arithmetic and copies ran while one was open for 0% of the time, Pallas kernels for 2%

profile of v8, /device:TPU:1, one launch (start us, length us, event | category | flops | bytes accessed | tf_op | source)
XLA Modules:
  0.0 91.1 jit_solution(9203431172972194518)
XLA Ops:
  0.6 3.0 %shard_map.59 = (f32[17,64,128]{2,1,0:T(8,128)}, f32[5,64,128]{2,1,0:T(8,128)}, f32[12,64,128]{2,1,0:T(8,128)}, f32[8,64,128]{2,1,0:T(8,128)}) custom-call(f32[3,8,64,128]{3,2,1,0:T(8,128)} %load_ref.1, s32[8,64,128]{2,1,0:T(8,128)} %phases_hbm.1, f32[4]{0:T(128)} %table_ref.1), custom_call_target="tpu_custom_call" | custom-call | tf_op jit(solution)/shard_map/pallas_call | solution.py:876
  3.6 1.5 %collective-permute-start.1 = (f32[17,64,128]{2,1,0:T(8,128)}, f32[17,64,128]{2,1,0:T(8,128)S(1)}, u32[]{:S(2)}, u32[]{:S(2)}) collective-permute-start(f32[17,64,128]{2,1,0:T(8,128)} %get-tuple-element.24), channel_id=1, source_target_pairs={{0,1},{1,0},{2,3},{3,2},{4,5},{5,4},{6,7},{7,6},{8,9},{9,8},{10,11... | collective-permute-start | bytes 1671176 | tf_op jit(solution)/shard_map/ppermute | solution.py:892
  5.1 3.2 %collective-permute-start = (f32[5,64,128]{2,1,0:T(8,128)}, f32[5,64,128]{2,1,0:T(8,128)S(1)}, u32[]{:S(2)}, u32[]{:S(2)}) collective-permute-start(f32[5,64,128]{2,1,0:T(8,128)} %get-tuple-element.23), channel_id=1, source_target_pairs={{1,2},{2,1},{3,4},{4,3},{5,6},{6,5},{7,8},{8,7},{9,10},{10,9},{11,... | collective-permute-start | bytes 491528 | tf_op jit(solution)/shard_map/ppermute | solution.py:890
  8.3 2.4 %collective-permute-start.2 = (f32[12,64,128]{2,1,0:T(8,128)}, f32[12,64,128]{2,1,0:T(8,128)}, u32[]{:S(2)}, u32[]{:S(2)}) collective-permute-start(f32[12,64,128]{2,1,0:T(8,128)} %get-tuple-element.32), channel_id=1, source_target_pairs={{1,2},{2,1},{3,4},{4,3},{5,6},{6,5},{7,8},{8,7},{9,10},{10,9},{11,... | collective-permute-start | bytes 1179656 | tf_op jit(solution)/shard_map/ppermute | solution.py:891
  10.7 0.0 copy-start
  10.7 1.1 %copy-done = f32[3,8,64,128]{3,2,1,0:T(8,128)S(1)} copy-done((f32[3,8,64,128]{3,2,1,0:T(8,128)S(1)}, f32[3,8,64,128]{3,2,1,0:T(8,128)}, u32[]{:S(2)}) %copy-start) | copy-done | bytes 786456
  11.8 0.0 copy-start.2
  11.8 0.9 %copy-done.2 = f32[8,64,128]{2,1,0:T(8,128)S(1)} copy-done((f32[8,64,128]{2,1,0:T(8,128)S(1)}, f32[8,64,128]{2,1,0:T(8,128)}, u32[]{:S(2)}) %copy-start.2) | copy-done | bytes 262168
  12.7 0.0 copy-start.3
  12.7 0.8 copy-done.3
  13.5 1.1 %shard_map.60 = (f32[3,17,64,128]{3,2,1,0:T(8,128)S(1)}, f32[17,64,128]{2,1,0:T(8,128)S(1)}, f32[17,64,128]{2,1,0:T(8,128)S(1)}, f32[64,128]{1,0:T(8,128)S(1)}, ...) custom-call(f32[3,8,64,128]{3,2,1,0:T(8,128)S(1)} %copy-done, f32[8,64,128]{2,1,0:T(8,128)S(1)} %copy-done.2, ...), custom_call_target="tpu_custom_call" | custom-call | flops 20000000 | bytes 20000000 | tf_op jit(solution)/shard_map/pallas_call | solution.py:849
  14.6 0.0 collective-permute-done.near_ref
  14.6 0.0 collective-permute-done.1.chip_ref
  14.6 1.1 %shard_map.61 = f32[512,128]{1,0:T(8,128)S(1)} custom-call(f32[5,64,128]{2,1,0:T(8,128)S(1)} %collective-permute-done.near_ref, f32[17,64,128]{2,1,0:T(8,128)S(1)} %collective-permute-done.1.chip_ref, f32[3,17,64,128]{3,2,1,0:T(8,128)S(1)} %get-tuple-element.26.own_rhs_ref, f32[17,64,128]{2,1,0:T(8,128)S(1)} %get-tuple-element.27.own_moduli_ref, ...), custom_call_target="tpu_custom_call" | custom-call | tf_op jit(solution)/shard_map/pallas_call | solution.py:849
  15.7 0.0 copy-start.1
  15.7 0.7 copy-done.1
  16.4 14.3 %all-to-all-start = ((f32[128,4,128]{2,1,0:T(4,128)}), f32[128,4,128]{2,1,0:T(4,128)}, u32[]{:S(2)}, u32[]{:S(2)}) async-start(f32[128,4,128]{2,1,0:T(4,128)} %bitcast.8), calls=%async_computation | async-start | bytes 524288 | tf_op jit(solution)/shard_map/all_to_all | solution.py:862
  30.7 0.0 collective-permute-done.2.far_ref
  30.7 10.7 %all-to-all-done = f32[128,4,128]{2,1,0:T(4,128)} async-done(((f32[128,4,128]{2,1,0:T(4,128)}), f32[128,4,128]{2,1,0:T(4,128)}, u32[]{:S(2)}, u32[]{:S(2)}) %all-to-all-start) | async-done | bytes 262176 | tf_op jit(solution)/shard_map/all_to_all | solution.py:862
  41.4 12.2 %shard_map.62 = (f32[3,17,64,128]{3,2,1,0:T(8,128)S(1)}, f32[3,17,64,128]{3,2,1,0:T(8,128)S(1)}, f32[16,128]{1,0:T(8,128)S(1)}, f32[512,128]{1,0:T(8,128)S(1)}, ...) custom-call(f32[512,128]{1,0:T(8,128)} %bitcast.1.gathered_ref, ...), custom_call_target="tpu_custom_call" | custom-call | tf_op jit(solution)/shard_map/pallas_call | solution.py:849
  53.6 15.2 %all_to_all.15 = f32[128,4,128]{2,1,0:T(4,128)S(1)} all-to-all(f32[128,4,128]{2,1,0:T(4,128)S(1)} %bitcast.11), channel_id=1, replica_groups=mesh['grp'=4,'gz'=32] {'grp','gz'}, dimensions={0} | all-to-all | bytes 524288 | tf_op jit(solution)/shard_map/all_to_all | solution.py:862
  68.8 7.1 %shard_map.63 = (f32[3,8,64,128]{3,2,1,0:T(8,128)S(1)}, f32[3,8,64,128]{3,2,1,0:T(8,128)S(1)}, f32[8,128]{1,0:T(8,128)S(1)}, f32[128,128]{1,0:T(8,128)S(1)}) custom-call(f32[512,128]{1,0:T(8,128)S(1)} %bitcast.9, f32[3,17,64,128]{3,2,1,0:T(8,128)S(1)} %get-tuple-element.34.rhs_ref, f32[17,64,128]{2,1,0:T(8,128)S(1)} %get-tuple-element.35.moduli_ref, ...), custom_call_target="tpu_custom_call" | custom-call | tf_op jit(solution)/shard_map/pallas_call | solution.py:849
  75.9 13.7 %all_to_all.16 = f32[128,1,128]{2,1,0:T(1,128)S(1)} all-to-all(f32[128,1,128]{2,1,0:T(1,128)S(1)} %bitcast.12), channel_id=1, replica_groups=mesh['grp'=4,'gz'=32] {'grp','gz'}, dimensions={0} | all-to-all | bytes 131072 | tf_op jit(solution)/shard_map/all_to_all | solution.py:862
  89.7 1.5 %shard_map.64 = (f32[3,8,64,128]{3,2,1,0:T(8,128)}, f32[3,8,64,128]{3,2,1,0:T(8,128)}) custom-call(f32[128,128]{1,0:T(8,128)S(1)} %bitcast.10, f32[8,128]{1,0:T(8,128)S(1)} %get-tuple-element.41.scalars_ref, f32[3,17,64,128]{3,2,1,0:T(8,128)S(1)} %get-tuple-element.34.rhs_ref, f32[3,17,64,128]{3,2,1,0:T(8,128)S(1)} %get-tuple-element.37.ahead_ref, ...), custom_call_target="tpu_custom_call" | custom-call | tf_op jit(solution)/shard_map/pallas_call | solution.py:921
Async XLA Ops:
  3.6 11.0 %collective-permute-start.1 = (f32[17,64,128]{2,1,0:T(8,128)}, f32[17,64,128]{2,1,0:T(8,128)S(1)}, u32[]{:S(2)}, u32[]{:S(2)}) collective-permute-start(f32[17,64,128]{2,1,0:T(8,128)} %get-tuple-element.24), channel_id=1, source_target_pairs={{0,1},{1,0},{2,3},{3,2},{4,5},{5,4},{6,7},{7,6},{8,9},{9,8},{10,11... | collective-permute-start | bytes 1671176 | tf_op jit(solution)/shard_map/ppermute | solution.py:892
  5.1 9.5 %collective-permute-start = (f32[5,64,128]{2,1,0:T(8,128)}, f32[5,64,128]{2,1,0:T(8,128)S(1)}, u32[]{:S(2)}, u32[]{:S(2)}) collective-permute-start(f32[5,64,128]{2,1,0:T(8,128)} %get-tuple-element.23), channel_id=1, source_target_pairs={{1,2},{2,1},{3,4},{4,3},{5,6},{6,5},{7,8},{8,7},{9,10},{10,9},{11,... | collective-permute-start | bytes 491528 | tf_op jit(solution)/shard_map/ppermute | solution.py:890
  8.3 22.4 %collective-permute-start.2 = (f32[12,64,128]{2,1,0:T(8,128)}, f32[12,64,128]{2,1,0:T(8,128)}, u32[]{:S(2)}, u32[]{:S(2)}) collective-permute-start(f32[12,64,128]{2,1,0:T(8,128)} %get-tuple-element.32), channel_id=1, source_target_pairs={{1,2},{2,1},{3,4},{4,3},{5,6},{6,5},{7,8},{8,7},{9,10},{10,9},{11,... | collective-permute-start | bytes 1179656 | tf_op jit(solution)/shard_map/ppermute | solution.py:891
  10.7 1.1 %copy-start = (f32[3,8,64,128]{3,2,1,0:T(8,128)S(1)}, f32[3,8,64,128]{3,2,1,0:T(8,128)}, u32[]{:S(2)}) copy-start(f32[3,8,64,128]{3,2,1,0:T(8,128)} %load_ref.1) | copy-start | bytes 2359300
  11.8 0.9 %copy-start.2 = (f32[8,64,128]{2,1,0:T(8,128)S(1)}, f32[8,64,128]{2,1,0:T(8,128)}, u32[]{:S(2)}) copy-start(f32[8,64,128]{2,1,0:T(8,128)} %get-tuple-element.25.own_ref) | copy-start | bytes 786436
  12.7 0.8 copy-start.3
  15.7 0.7 copy-start.1
  16.4 25.0 %all-to-all-start = ((f32[128,4,128]{2,1,0:T(4,128)}), f32[128,4,128]{2,1,0:T(4,128)}, u32[]{:S(2)}, u32[]{:S(2)}) async-start(f32[128,4,128]{2,1,0:T(4,128)} %bitcast.8), calls=%async_computation | async-start | bytes 524288 | tf_op jit(solution)/shard_map/all_to_all | solution.py:862
